TPU v7x, 512 devices: a whole 4x4x16 slice. The times are simulated.
512 devices in a mesh: section: 4 (over z_hi, core), dp: 16 (over x, y), tensor: 8 (over z_lo).
Axes of the slice: x: 4, y: 4, z: 16 (z_hi: 2, z_lo: 8; z = z_hi * 8 + z_lo), core: 2. Of those that a mesh axis runs over, the one named last changes fastest.
Arguments:
- hidden_state_matrix: bfloat16 [4, 2048, 4096], P('section', 'dp', 'tensor'), may hold values from -6 to 6
- specialist_choice_ids: int32 [4, 2048, 8], P('section', 'dp'), may hold values from 0 to 15, as said below
- seat_quota_per_specialist: int32 [4, 16], P('section'), may hold values from 8 to 16, as said below
- candidate_active_extent: int32 [4, 16], P('section', 'dp'), may hold values from 16 to 128, as said below
- normalizer_gain_vector: bfloat16 [4, 4096], P('section'), may hold values from 0.5 to 1.5
- dispatcher_matrix: bfloat16 [4, 16, 4096], P('section'), may hold values from -0.09375 to 0.09375
- gating_matrices: bfloat16 [4, 16, 1536, 4096], P('section', 'dp', 'tensor'), may hold values from -0.09375 to 0.09375
- expanding_matrices: bfloat16 [4, 16, 1536, 4096], P('section', 'dp', 'tensor'), may hold values from -0.09375 to 0.09375
- contracting_matrices: bfloat16 [4, 16, 1536, 4096], P('section', 'dp', None, 'tensor'), may hold values from -0.15625 to 0.15625
Outputs:
- handed: bfloat16 [4, 2048, 4096], P('section', 'dp', 'tensor')
Inputs may be any that keep to these rules, and one draw needn't show every extreme that they name: `specialist_choice_ids`: each row names 8 different experts. In each section one expert is named by every row. `seat_quota_per_specialist`: the expert that every row of a section names has capacity 16 there. `candidate_active_extent`: each section has a sequence of 128 live positions.
All inputs are finite; a program needn't handle non-finite values.
Results may differ from a plain program's by a relative error of at most 0.002.
Values may be sent and summed in bfloat16 or wider, within the bound.
No kernel may reach another device: no remote copies, remote signals or barrier semaphores. Data moves between devices by JAX's collectives and lax.ppermute only.
A program may use at most 64 MiB of HBM per device.

v0:
```python
import jax
import jax.numpy as jnp
from jax import lax
from jax.sharding import PartitionSpec as P

norm_eps = 1e-06


def passed_along(value, axis, by):
    count = lax.axis_size(axis)
    return lax.ppermute(value, axis, [(i, (i + by) % count) for i in range(count)])


def against_rows(left, right):
    return lax.dot_general(
        left, right, (((1,), (1,)), ((), ())), preferred_element_type=jnp.float32
    )


def on_device(
    hidden_state_matrix,
    specialist_choice_ids,
    seat_quota_per_specialist,
    candidate_active_extent,
    normalizer_gain_vector,
    dispatcher_matrix,
    gating_matrices,
    expanding_matrices,
    contracting_matrices,
):
    tokens = hidden_state_matrix[0]
    routes = specialist_choice_ids[0]
    extent_bounds = seat_quota_per_specialist[0]
    length = candidate_active_extent[0, 0]
    gain = normalizer_gain_vector[0].astype(jnp.float32)
    router_rows = dispatcher_matrix[0]
    w_gate = gating_matrices[0, 0]
    w_up = expanding_matrices[0, 0]
    w_down = contracting_matrices[0, 0]
    n_rows = tokens.shape[0]
    n_experts = extent_bounds.shape[0]
    slots = n_rows // 8
    expert_iota = lax.broadcasted_iota(jnp.int32, (1, 1, n_experts), 2)
    chosen = jnp.sum((routes[:, :, None] == expert_iota).astype(jnp.int32), axis=1)
    row_iota = lax.broadcasted_iota(jnp.int32, (n_rows, 1), 0)
    picked = chosen * (row_iota < length).astype(jnp.int32)
    order = jnp.cumsum(picked, axis=0) - picked
    kept = picked * (order < extent_bounds[None, :]).astype(jnp.int32)
    slot_iota = lax.broadcasted_iota(jnp.int32, (1, 1, slots), 2)
    match = kept[:, :, None] * (order[:, :, None] == slot_iota).astype(jnp.int32)
    slot_row = jnp.sum(match * row_iota[:, :, None], axis=0)
    filled = jnp.sum(match, axis=0)[:, :, None] > 0
    slot_choice = jnp.where(filled, jnp.take(chosen, slot_row, axis=0), 0).astype(jnp.bfloat16)
    source = lax.all_gather(tokens, "tensor", axis=1, tiled=True)
    outgoing = jnp.where(filled, jnp.take(source, slot_row, axis=0), jnp.zeros((), jnp.bfloat16))
    arrived = lax.all_to_all(outgoing, "dp", split_axis=0, concat_axis=0, tiled=True)
    arrived_choice = lax.all_to_all(slot_choice, "dp", split_axis=0, concat_axis=0, tiled=True)
    n_source, n_items, width = arrived.shape
    widened = arrived.reshape(n_source * n_items, width).astype(jnp.float32)
    inverse = lax.rsqrt(jnp.mean(widened * widened, axis=1, keepdims=True) + norm_eps)
    normed = (widened * inverse * gain[None, :]).astype(jnp.bfloat16)
    logits = against_rows(normed, router_rows)
    marked = arrived_choice.reshape(n_source * n_items, n_experts).astype(jnp.float32)
    powered = jnp.exp(logits) * marked
    own_expert = (
        lax.broadcasted_iota(jnp.int32, (1, n_experts), 1) == lax.axis_index("dp")
    ).astype(jnp.float32)
    denominator = jnp.sum(powered, axis=1) + (1.0 - jnp.max(marked, axis=1))
    weight = jnp.sum(powered * own_expert, axis=1) / denominator
    gate = against_rows(normed, w_gate)
    upper = against_rows(normed, w_up)
    hidden = (jax.nn.silu(gate) * upper).astype(jnp.bfloat16)
    projected = jnp.dot(
        lax.all_gather(hidden, "tensor", axis=1, tiled=True),
        w_down,
        preferred_element_type=jnp.float32,
    )
    reply = (
        (projected * weight[:, None])
        .astype(jnp.bfloat16)
        .reshape(n_source, n_items, w_down.shape[1])
    )
    returned = lax.all_to_all(reply, "dp", split_axis=0, concat_axis=0, tiled=True)
    width = returned.shape[2]
    spot = jnp.take_along_axis(order, routes, axis=1)
    taken = jnp.take_along_axis(kept, routes, axis=1)
    flat_index = routes * slots + jnp.minimum(spot, slots - 1)
    pulled = jnp.take(returned.reshape(n_experts * slots, width), flat_index, axis=0)
    mixed = jnp.sum(
        jnp.where(taken[:, :, None] > 0, pulled.astype(jnp.float32), jnp.zeros((), jnp.float32)),
        axis=1,
    )
    layer_out = (tokens.astype(jnp.float32) + mixed).astype(jnp.bfloat16)
    handed = passed_along(layer_out, "section", 1)
    return handed[None]


def solution(mesh):
    return jax.shard_map(
        on_device,
        mesh=mesh,
        in_specs=(
            P("section", "dp", "tensor"),
            P("section", "dp", None),
            P("section", None),
            P("section", "dp"),
            P("section", None),
            P("section", None, None),
            P("section", "dp", "tensor", None),
            P("section", "dp", "tensor", None),
            P("section", "dp", None, "tensor"),
        ),
        out_specs=P("section", "dp", "tensor"),
        check_vma=False,
    )
```

profile of v0, /device:TPU:8, one launch (start us, length us, event | category | flops | bytes accessed | tf_op | source)
XLA Modules:
  0.0 220.0 jit_solution(5084894138479048002)
XLA Ops:
  6.5 0.7 all-gather.3.cloned.1.call-update
  7.9 0.7 convert_reduce_fusion
  8.6 0.1 copy.21
  8.8 0.2 reduce_window_sum.11
  9.0 0.7 compare_select_fusion.2
  9.8 0.6 select_reduce_fusion.1
  10.6 0.7 gather_fusion.1
  11.5 0.7 reshape.244
  12.2 9.1 %all-to-all-start.1 = ((bf16[16,2,128]{2,1,0:T(2,128)(2,1)}), bf16[16,2,128]{2,1,0:T(2,128)(2,1)S(1)}, u32[]{:S(2)}, u32[]{:S(2)}) async-start(bf16[16,2,128]{2,1,0:T(2,128)(2,1)} %reshape.244), calls=%async_computation.1 | async-start | bytes 16384 | tf_op jit(solution)/shard_map/all_to_all | solution.py:57
  21.3 59.9 %all-gather.3.cloned.1.call-done = bf16[1,128,4096]{2,1,0:T(8,128)(2,1)} async-done(((bf16[1,128,512]{2,1,0:T(8,128)(2,1)}), bf16[1,128,4096]{2,1,0:T(8,128)(2,1)}) %all-gather.3.cloned.1.call-update) | async-done | bytes 1048592 | tf_op jit(solution)/shard_map/all_gather | solution.py:54
  81.2 6.6 %gather_fusion = bf16[256,4096]{1,0:T(8,128)(2,1)} fusion(bf16[128,4096]{1,0:T(8,128)(2,1)} %bitcast.77, s32[1024]{0:T(1024)S(1)} %pad_clamp_fusion), kind=kCustom, calls=%fused_computation.2 | custom fusion | bytes 4195328 | tf_op jit(solution)/shard_map/jit(_take)/gather | solution.py:55
  87.8 3.2 %select_select_fusion = bf16[16,16,4096]{2,1,0:T(8,128)(2,1)} fusion(bf16[16,16,4096]{2,1,0:T(8,128)(2,1)} %bitcast.81, pred[16,16]{1,0:T(8,128)(4,1)S(1)} %get-tuple-element.15, pred[16,16]{1,0:T(8,128)(4,1)S(1)} %get-tuple-element.16), kind=kLoop, calls=%fused_computation.11 | loop fusion | flops 2097152 | bytes 4194816 | tf_op jit(solution)/shard_map/jit(_where)/select_n | solution.py:55
  91.0 7.6 %all-to-all-start = ((bf16[16,16,4096]{2,1,0:T(8,128)(2,1)}), bf16[16,16,4096]{2,1,0:T(8,128)(2,1)}, u32[]{:S(2)}, u32[]{:S(2)}) async-start(bf16[16,16,4096]{2,1,0:T(8,128)(2,1)} %select_select_fusion), calls=%async_computation | async-start | bytes 4194304 | tf_op jit(solution)/shard_map/all_to_all | solution.py:56
  98.9 7.1 %gather_fusion.3 = s32[1024]{0:T(1024)S(1)} fusion(s32[128,16]{1,0:T(8,128)S(1)} %get-tuple-element.12, s32[1024]{0:T(1024)S(1)} %reshape.235), kind=kCustom, calls=%fused_computation.clone | custom fusion | bytes 16384 | tf_op jit(solution)/shard_map/jit(take_along_axis)/gather | solution.py:86
  106.0 7.1 %gather_fusion.4 = s32[1024]{0:T(1024)S(1)} fusion(s32[128,16]{1,0:T(8,128)S(1)} %get-tuple-element.13, s32[1024]{0:T(1024)S(1)} %reshape.235), kind=kCustom, calls=%fused_computation.1.clone | custom fusion | bytes 16384 | tf_op jit(solution)/shard_map/jit(take_along_axis)/gather | solution.py:85
  113.5 0.1 reshape.181
  113.6 5.7 %all-to-all-done = bf16[16,16,4096]{2,1,0:T(8,128)(2,1)} async-done(((bf16[16,16,4096]{2,1,0:T(8,128)(2,1)}), bf16[16,16,4096]{2,1,0:T(8,128)(2,1)}, u32[]{:S(2)}, u32[]{:S(2)}) %all-to-all-start) | async-done | bytes 2097184 | tf_op jit(solution)/shard_map/all_to_all | solution.py:56
  119.4 2.1 fusion
  121.4 2.3 %fusion.2 = bf16[16,16,4096]{2,1,0:T(8,128)(2,1)S(1)} fusion(bf16[16,16,4096]{2,1,0:T(8,128)(2,1)} %all-to-all-done, f32[4096]{0:T(1024)S(1)} %bitcast.85, f32[16,16]{1,0:T(8,128)S(1)} %add_rsqrt_fusion), kind=kLoop, calls=%fused_computation.9 | loop fusion | flops 4194304 | bytes 4211712 | tf_op jit(solution)/shard_map/convert_element_type | solution.py:61
  123.8 0.8 fusion.7
  124.7 0.5 copy-done.6
  125.2 0.8 fusion.18
  126.1 49.3 %all_gather.7 = bf16[256,1536]{0,1:T(8,128)(2,1)S(1)} all-gather(bf16[256,192]{0,1:T(8,128)(2,1)S(1)} %fusion.18), channel_id=1, replica_groups=mesh['section'=4,'dp'=16,'tensor'=8] {'tensor'}, dimensions={1}, use_global_device_ids=true | all-gather | bytes 884736 | tf_op jit(solution)/shard_map/all_gather | solution.py:74
  175.3 0.7 fusion.26
  176.0 1.3 fusion.12
  177.3 7.0 %all-to-all-start.2 = ((bf16[16,16,512]{2,1,0:T(8,128)(2,1)}), bf16[16,16,512]{2,1,0:T(8,128)(2,1)S(1)}, u32[]{:S(2)}, u32[]{:S(2)}) async-start(bf16[16,16,512]{2,1,0:T(8,128)(2,1)} %bitcast.17), calls=%async_computation.2 | async-start | bytes 524288 | tf_op jit(solution)/shard_map/all_to_all | solution.py:83
  184.5 6.8 %all-to-all-done.2 = bf16[16,16,512]{2,1,0:T(8,128)(2,1)S(1)} async-done(((bf16[16,16,512]{2,1,0:T(8,128)(2,1)}), bf16[16,16,512]{2,1,0:T(8,128)(2,1)S(1)}, u32[]{:S(2)}, u32[]{:S(2)}) %all-to-all-start.2) | async-done | bytes 262176 | tf_op jit(solution)/shard_map/all_to_all | solution.py:83
  191.3 4.0 %gather_fusion.2 = bf16[1024,512]{1,0:T(8,128)(2,1)S(1)} fusion(bf16[256,512]{1,0:T(8,128)(2,1)S(1)} %bitcast.76, s32[1024]{0:T(1024)S(1)} %broadcast_clamp_fusion), kind=kCustom, calls=%fused_computation.4 | custom fusion | bytes 2101248 | tf_op jit(solution)/shard_map/jit(_take)/gather | solution.py:88
  195.3 0.9 select_reduce_fusion
  196.2 1.9 collective-permute-start
  198.2 14.3 %collective-permute-done = bf16[128,512]{1,0:T(8,128)(2,1)S(1)} collective-permute-done((bf16[128,512]{1,0:T(8,128)(2,1)S(1)}, bf16[128,512]{1,0:T(8,128)(2,1)S(1)}, u32[]{:S(2)}, u32[]{:S(2)}) %collective-permute-start) | collective-permute-done | bytes 131104 | tf_op jit(solution)/shard_map/ppermute | solution.py:11
  212.5 0.7 copy.30
  (43 shorter events, 1.3 us)
Async XLA Ops:
  6.5 169.5 %copy-start = (bf16[1,1,1536,512]{3,2,1,0:T(8,128)(2,1)S(1)}, bf16[1,1,1536,512]{3,2,1,0:T(8,128)(2,1)}, u32[]{:S(2)}) copy-start(bf16[1,1,1536,512]{3,2,1,0:T(8,128)(2,1)} %param.19) | copy-start | bytes 4718596
  6.5 74.7 %all-gather.3.cloned.1.call-start = ((), (), s32[]{:S(2)}) async-start(), calls=%async_computation.3 | async-start | bytes 1179648 | tf_op jit(solution)/shard_map/all_gather | solution.py:54
  12.2 78.8 %all-to-all-start.1 = ((bf16[16,2,128]{2,1,0:T(2,128)(2,1)}), bf16[16,2,128]{2,1,0:T(2,128)(2,1)S(1)}, u32[]{:S(2)}, u32[]{:S(2)}) async-start(bf16[16,2,128]{2,1,0:T(2,128)(2,1)} %reshape.244), calls=%async_computation.1 | async-start | bytes 16384 | tf_op jit(solution)/shard_map/all_to_all | solution.py:57
  91.0 7.6 %copy-start.4 = (s32[1,128,8]{1,2,0:T(8,128)S(1)}, s32[1,128,8]{1,2,0:T(8,128)}, u32[]{:S(2)}) copy-start(s32[1,128,8]{1,2,0:T(8,128)} %param.12) | copy-start | bytes 12292
  91.0 28.3 %all-to-all-start = ((bf16[16,16,4096]{2,1,0:T(8,128)(2,1)}), bf16[16,16,4096]{2,1,0:T(8,128)(2,1)}, u32[]{:S(2)}, u32[]{:S(2)}) async-start(bf16[16,16,4096]{2,1,0:T(8,128)(2,1)} %select_select_fusion), calls=%async_computation | async-start | bytes 4194304 | tf_op jit(solution)/shard_map/all_to_all | solution.py:56
  106.0 7.1 %copy-start.5 = (bf16[1,4096]{1,0:T(2,128)(2,1)S(1)}, bf16[1,4096]{1,0:T(2,128)(2,1)}, u32[]{:S(2)}) copy-start(bf16[1,4096]{1,0:T(2,128)(2,1)} %param.15) | copy-start | bytes 24580
  121.4 2.4 %copy-start.1 = (bf16[1,1,192,4096]{3,2,1,0:T(8,128)(2,1)S(1)}, bf16[1,1,192,4096]{3,2,1,0:T(8,128)(2,1)}, u32[]{:S(2)}) copy-start(bf16[1,1,192,4096]{3,2,1,0:T(8,128)(2,1)} %param.17) | copy-start | bytes 4718596
  123.8 1.4 copy-start.6
  125.2 50.1 %copy-start.3 = (bf16[1,16,4096]{2,1,0:T(8,128)(2,1)S(1)}, bf16[1,16,4096]{2,1,0:T(8,128)(2,1)}, u32[]{:S(2)}) copy-start(bf16[1,16,4096]{2,1,0:T(8,128)(2,1)} %param.16) | copy-start | bytes 393220
  177.3 14.0 %all-to-all-start.2 = ((bf16[16,16,512]{2,1,0:T(8,128)(2,1)}), bf16[16,16,512]{2,1,0:T(8,128)(2,1)S(1)}, u32[]{:S(2)}, u32[]{:S(2)}) async-start(bf16[16,16,512]{2,1,0:T(8,128)(2,1)} %bitcast.17), calls=%async_computation.2 | async-start | bytes 524288 | tf_op jit(solution)/shard_map/all_to_all | solution.py:83
  191.3 4.9 %copy-start.2 = (bf16[1,128,512]{2,1,0:T(8,128)(2,1)S(1)}, bf16[1,128,512]{2,1,0:T(8,128)(2,1)}, u32[]{:S(2)}) copy-start(bf16[1,128,512]{2,1,0:T(8,128)(2,1)} %param.11) | copy-start | bytes 393220
  196.2 16.2 %collective-permute-start = (bf16[128,512]{1,0:T(8,128)(2,1)S(1)}, bf16[128,512]{1,0:T(8,128)(2,1)S(1)}, u32[]{:S(2)}, u32[]{:S(2)}) collective-permute-start(bf16[128,512]{1,0:T(8,128)(2,1)S(1)} %fusion.22), channel_id=1, source_target_pairs={{0,128},{128,256},{256,384},{384,0},{1,129},{129,257},{257,385},{3... | collective-permute-start | bytes 393224 | tf_op jit(solution)/shard_map/ppermute | solution.py:11
Sparse Core Ops, SparseCore 0:
  9.4 71.7 all-gather.2
where the time goes:
time: 221 us; the launch traced here: 220 us
  waiting for transfers between devices  87.5 us (40%)
  blocking collectives  49.3 us (22%)
  local copies, waits for them, and re-layouts  28.5 us (13%)
  starting transfers between devices  25.6 us (12%)
  between operations  14.3 us (6%)
  other arithmetic  11.1 us (5%)
  matrix products  3.66 us (2%)
    all_gather x1, waiting for transfers between devices, on_device(): source = lax.all_gather(tokens, 'tensor', axis=1, tiled=True)  59.9 us
    all_gather x1, blocking collectives, on_device(): lax.all_gather(hidden, 'tensor', axis=1, tiled=True)  49.3 us
    ppermute x1, waiting for transfers between devices, passed_along(): lax.ppermute(value, axis, [(i, (i + by) % count) for i in range(count)])  14.3 us
    all_to_all x1, starting transfers between devices, on_device(): lax.all_to_all(slot_choice, 'dp', split_axis=0, concat_axis=0, tiled=True)  9.08 us
    all_to_all x1, starting transfers between devices, on_device(): lax.all_to_all(outgoing, 'dp', split_axis=0, concat_axis=0, tiled=True)  7.63 us
    gather x3, local copies, waits for them, and re-layouts, on_device(): taken = jnp.take_along_axis(kept, routes, axis=1)  7.24 us
    gather x2, local copies, waits for them, and re-layouts, on_device(): spot = jnp.take_along_axis(order, routes, axis=1)  7.15 us
    all_to_all x1, starting transfers between devices, on_device(): lax.all_to_all(reply, 'dp', split_axis=0, concat_axis=0, tiled=True)  7 us
  transfers between devices with their start and end apart: 5, of which 4 were waited for; matrix products, arithmetic and copies ran while one was open for 13% of the time, Pallas kernels for 0%

commit v1 on v0

v1 whole, which is shorter than its diff:
```python
import jax
import jax.numpy as jnp
from jax import lax
from jax.experimental import pallas as pl
from jax.experimental.pallas import tpu as pltpu
from jax.sharding import PartitionSpec as P

norm_eps = 1e-06
BF = jnp.bfloat16
F32 = jnp.float32
EXPERTS = 16
SLOTS = 16
VM = pl.BlockSpec(memory_space=pltpu.VMEM)
SM = pl.BlockSpec(memory_space=pltpu.SMEM)
FOURS = [[0, 1, 2, 3], [4, 5, 6, 7]]


def dot(a, b, da, db):
    return lax.dot_general(a, b, (((da,), (db,)), ((), ())), preferred_element_type=F32)


def call(body, shape, specs, args, flops=0, moved=0, limit=24):
    return pl.pallas_call(
        body,
        out_shape=shape,
        in_specs=specs,
        out_specs=jax.tree.map(lambda _: VM, shape),
        compiler_params=pltpu.CompilerParams(vmem_limit_bytes=limit * 2**20),
        cost_estimate=pl.CostEstimate(flops=flops, bytes_accessed=moved, transcendentals=0),
    )(*args)


def choices(ids):
    expert = lax.broadcasted_iota(jnp.int32, (EXPERTS, ids.shape[1]), 0)
    total = jnp.zeros(expert.shape, F32)
    for j in range(ids.shape[0]):
        total = total + (ids[j : j + 1, :] == expert).astype(F32)
    return total


def route_body(length_ref, ids_ref, quota_ref, match_ref):
    n = ids_ref.shape[1]
    at = lax.broadcasted_iota(jnp.int32, (1, n), 1)
    picked = choices(ids_ref[...]) * (at < length_ref[0]).astype(F32)
    before = (
        lax.broadcasted_iota(jnp.int32, (n, n), 0) < lax.broadcasted_iota(jnp.int32, (n, n), 1)
    ).astype(BF)
    order = dot(picked.astype(BF), before, 1, 0)
    kept = picked * (order < quota_ref[...].astype(F32)).astype(F32)
    slot = lax.broadcasted_iota(jnp.int32, (SLOTS, n), 0).astype(F32)
    for e in range(EXPERTS):
        hit = (order[e : e + 1, :] == slot).astype(F32) * kept[e : e + 1, :]
        match_ref[e * SLOTS : (e + 1) * SLOTS, :] = hit.astype(BF)


def pick_body(match_ref, rows_ref, out_ref):
    parts, _, width = rows_ref.shape
    for k in range(parts):
        out_ref[:, k * width : (k + 1) * width] = dot(match_ref[...], rows_ref[k], 1, 0).astype(BF)


def weigh_body(half_ref, first_ref, second_ref, gain_ref, router_ref, ids_ref, match_ref, high_ref, low_ref):
    parts, n, width = first_ref.shape
    full = 2 * parts * width
    squares = jnp.zeros((n, 1), F32)
    for ref in (first_ref, second_ref):
        for k in range(parts):
            v = ref[k].astype(F32)
            squares = squares + jnp.sum(v * v, axis=1, keepdims=True)
    inverse = lax.rsqrt(squares / full + norm_eps)
    logits = jnp.zeros((EXPERTS, n), F32)
    for ref, half in ((first_ref, half_ref[0]), (second_ref, 1 - half_ref[0])):
        for k in range(parts):
            cols = pl.ds(pl.multiple_of((half * parts + k) * width, width), width)
            normed = (ref[k].astype(F32) * inverse * gain_ref[:, cols].astype(F32)).astype(BF)
            logits = logits + dot(router_ref[:, cols], normed, 1, 1)
    powered = jnp.exp(logits) * choices(ids_ref[...])
    weight = powered / jnp.sum(powered, axis=0, keepdims=True)
    for e in range(EXPERTS):
        rows = slice(e * SLOTS, (e + 1) * SLOTS)
        value = match_ref[rows, :].astype(F32) * weight[e : e + 1, :]
        high = value.astype(BF)
        high_ref[rows, :] = high
        low_ref[rows, :] = (value - high.astype(F32)).astype(BF)


def expand_body(half_ref, first_ref, second_ref, gain_ref, gate_ref, up_ref, out_ref):
    rows, span = first_ref.shape
    step = 512
    squares = jnp.zeros((rows, 1), F32)
    for ref in (first_ref, second_ref):
        for k in range(span // step):
            v = ref[:, k * step : (k + 1) * step].astype(F32)
            squares = squares + jnp.sum(v * v, axis=1, keepdims=True)
    inverse = lax.rsqrt(squares / (2 * span) + norm_eps)
    hid = gate_ref.shape[0]
    gate = jnp.zeros((hid, rows), F32)
    up = jnp.zeros((hid, rows), F32)
    for ref, half in ((first_ref, half_ref[0]), (second_ref, 1 - half_ref[0])):
        for k in range(span // step):
            cols = pl.ds(pl.multiple_of(half * span + k * step, step), step)
            v = ref[:, k * step : (k + 1) * step].astype(F32)
            normed = (v * inverse * gain_ref[:, cols].astype(F32)).astype(BF)
            gate = gate + dot(gate_ref[:, cols], normed, 1, 1)
            up = up + dot(up_ref[:, cols], normed, 1, 1)
    out_ref[...] = (gate / (1.0 + jnp.exp(-gate)) * up).astype(BF)


def contract_body(half_ref, first_ref, second_ref, down_ref, out_ref):
    parts, hid, _ = first_ref.shape
    total = jnp.zeros(out_ref.shape, F32)
    for ref, half in ((first_ref, half_ref[0]), (second_ref, 1 - half_ref[0])):
        for k in range(parts):
            rows = pl.ds(pl.multiple_of((half * parts + k) * hid, hid), hid)
            total = total + dot(ref[k], down_ref[rows, :], 0, 0)
    out_ref[...] = total.astype(BF)


def mix_body(high_ref, low_ref, reply_ref, tokens_ref, out_ref):
    mixed = dot(high_ref[...], reply_ref[...], 0, 0) + dot(low_ref[...], reply_ref[...], 0, 0)
    out_ref[...] = (tokens_ref[...].astype(F32) + mixed).astype(BF)


def to_fours(shard):
    copies = jnp.broadcast_to(shard[None], (4,) + shard.shape)
    return lax.all_to_all(copies, "tensor", 0, 0, axis_index_groups=FOURS)


def across(shard):
    return lax.ppermute(shard, "tensor", [(i, i ^ 4) for i in range(8)])


def over_dp(rows):
    n, width = rows.shape
    return lax.all_to_all(rows.reshape(EXPERTS, n // EXPERTS, width), "dp", 0, 0).reshape(n, width)


def on_device(
    hidden_state_matrix,
    specialist_choice_ids,
    seat_quota_per_specialist,
    candidate_active_extent,
    normalizer_gain_vector,
    dispatcher_matrix,
    gating_matrices,
    expanding_matrices,
    contracting_matrices,
):
    tokens = hidden_state_matrix[0]
    ids = specialist_choice_ids[0].T
    quota = seat_quota_per_specialist[0][:, None]
    length = candidate_active_extent[0]
    gain = normalizer_gain_vector
    router = dispatcher_matrix[0]
    w_gate = gating_matrices[0, 0]
    w_up = expanding_matrices[0, 0]
    w_down = contracting_matrices[0, 0]
    n, width = tokens.shape
    slots = EXPERTS * SLOTS
    hid = w_gate.shape[0]
    half = (lax.axis_index("tensor") // 4).astype(jnp.int32)[None]

    other = across(tokens)
    first = to_fours(tokens)
    match = call(route_body, jax.ShapeDtypeStruct((slots, n), BF), [SM, VM, VM], (length, ids, quota))
    out_rows = jax.ShapeDtypeStruct((slots, 4 * width), BF)
    first_rows = over_dp(call(pick_body, out_rows, [VM] * 2, (match, first)))
    second = to_fours(other)
    second_rows = over_dp(call(pick_body, out_rows, [VM] * 2, (match, second)))
    pair = jax.ShapeDtypeStruct((slots, n), BF)
    high, low = call(
        weigh_body, (pair, pair), [SM] + [VM] * 6, (half, first, second, gain, router, ids, match)
    )
    hidden = call(
        expand_body,
        jax.ShapeDtypeStruct((hid, slots), BF),
        [SM] + [VM] * 5,
        (half, first_rows, second_rows, gain, w_gate, w_up),
    )
    hidden_other = across(hidden)
    hidden_first = to_fours(hidden)
    hidden_second = to_fours(hidden_other)
    reply = call(
        contract_body,
        jax.ShapeDtypeStruct((slots, width), BF),
        [SM] + [VM] * 3,
        (half, hidden_first, hidden_second, w_down),
    )
    returned = over_dp(reply)
    layer_out = call(
        mix_body, jax.ShapeDtypeStruct((n, width), BF), [VM] * 4, (high, low, returned, tokens)
    )
    count = lax.axis_size("section")
    handed = lax.ppermute(layer_out, "section", [(i, (i + 1) % count) for i in range(count)])
    return handed[None]


def solution(mesh):
    return jax.shard_map(
        on_device,
        mesh=mesh,
        in_specs=(
            P("section", "dp", "tensor"),
            P("section", "dp", None),
            P("section", None),
            P("section", "dp"),
            P("section", None),
            P("section", None, None),
            P("section", "dp", "tensor", None),
            P("section", "dp", "tensor", None),
            P("section", "dp", None, "tensor"),
        ),
        out_specs=P("section", "dp", "tensor"),
        check_vma=False,
    )
```

time: 221 us -> 165 us (0.75)
  the two profiles are of different devices: /device:TPU:8 before, /device:TPU:32 now
where the time goes in v1:
time: 165 us; the launch traced here: 164 us
  waiting for transfers between devices  79.3 us (48%)
  starting transfers between devices  57 us (35%)
  blocking collectives  12.9 us (8%)
  Pallas kernels  7.38 us (4%)
  local copies, waits for them, and re-layouts  7.03 us (4%)
    all_to_all x3, waiting for transfers between devices, over_dp(): lax.all_to_all(rows.reshape(EXPERTS, n // EXPERTS, width), 'dp', 0, 0)  38.1 us
    all_to_all x3, starting transfers between devices, to_fours(): return lax.all_to_all(copies, 'tensor', 0, 0, axis_index_groups=FOURS)  26.6 us
    ppermute x1, waiting for transfers between devices, on_device(): lax.ppermute(layer_out, 'section', [(i, (i + 1) % count) for i in range(c...  17.3 us
    all_to_all x3, starting transfers between devices, over_dp(): lax.all_to_all(rows.reshape(EXPERTS, n // EXPERTS, width), 'dp', 0, 0)  17.1 us
    ppermute x2, waiting for transfers between devices, across(): return lax.ppermute(shard, 'tensor', [(i, i ^ 4) for i in range(8)])  15.7 us
    all_to_all x1, blocking collectives, to_fours(): return lax.all_to_all(copies, 'tensor', 0, 0, axis_index_groups=FOURS)  12.9 us
    ppermute x2, starting transfers between devices, across(): return lax.ppermute(shard, 'tensor', [(i, i ^ 4) for i in range(8)])  11.4 us
    all_to_all x3, waiting for transfers between devices, to_fours(): return lax.all_to_all(copies, 'tensor', 0, 0, axis_index_groups=FOURS)  8.21 us
  transfers between devices with their start and end apart: 9, of which 7 were waited for; matrix products, arithmetic and copies ran while one was open for 0% of the time, Pallas kernels for 2%

profile of v1, /device:TPU:32, one launch (start us, length us, event | category | flops | bytes accessed | tf_op | source)
XLA Modules:
  0.0 164.4 jit_solution(878415118887147840)
XLA Ops:
  0.0 1.8 %broadcast_in_dim.16 = bf16[4,128,512]{2,1,0:T(8,128)(2,1)} broadcast(bf16[128,512]{1,0:T(8,128)(2,1)} %bitcast.25), dimensions={1,2} | broadcast | bytes 655360 | tf_op jit(solution)/shard_map/broadcast_in_dim | solution.py:125
  1.8 8.9 %all-to-all-start = ((bf16[4,128,512]{2,1,0:T(8,128)(2,1)}), bf16[4,128,512]{2,1,0:T(8,128)(2,1)S(1)}, u32[]{:S(2)}, u32[]{:S(2)}) async-start(bf16[4,128,512]{2,1,0:T(8,128)(2,1)} %broadcast_in_dim.16), calls=%async_computation | async-start | bytes 1048576 | tf_op jit(solution)/shard_map/all_to_all | solution.py:126
  10.7 6.2 %collective-permute-start = (bf16[128,512]{1,0:T(8,128)(2,1)S(1)}, bf16[128,512]{1,0:T(8,128)(2,1)S(1)}, u32[]{:S(2)}, u32[]{:S(2)}) collective-permute-start(bf16[128,512]{1,0:T(8,128)(2,1)S(1)} %bitcast.26), channel_id=1, source_target_pairs={{0,4},{1,5},{2,6},{3,7},{4,0},{5,1},{6,2},{7,3},{8,12},{9,13},{10,... | collective-permute-start | bytes 393224 | tf_op jit(solution)/shard_map/ppermute | solution.py:130
  16.9 8.4 %collective-permute-done = bf16[128,512]{1,0:T(8,128)(2,1)S(1)} collective-permute-done((bf16[128,512]{1,0:T(8,128)(2,1)S(1)}, bf16[128,512]{1,0:T(8,128)(2,1)S(1)}, u32[]{:S(2)}, u32[]{:S(2)}) %collective-permute-start) | collective-permute-done | bytes 131104 | tf_op jit(solution)/shard_map/ppermute | solution.py:130
  25.4 0.8 broadcast_in_dim.34
  26.2 11.0 %all-to-all-start.1 = ((bf16[4,128,512]{2,1,0:T(8,128)(2,1)}), bf16[4,128,512]{2,1,0:T(8,128)(2,1)S(1)}, u32[]{:S(2)}, u32[]{:S(2)}) async-start(bf16[4,128,512]{2,1,0:T(8,128)(2,1)} %broadcast_in_dim.34), calls=%async_computation.1 | async-start | bytes 1048576 | tf_op jit(solution)/shard_map/all_to_all | solution.py:126
  37.9 0.1 copy.10.quota_ref
  38.0 0.2 shard_map.91.match_ref
  38.1 1.4 shard_map.93
  39.6 8.2 %all-to-all-done.1.second_ref.rows_ref = bf16[4,128,512]{2,1,0:T(8,128)(2,1)S(1)} async-done(((bf16[4,128,512]{2,1,0:T(8,128)(2,1)}), bf16[4,128,512]{2,1,0:T(8,128)(2,1)S(1)}, u32[]{:S(2)}, u32[]{:S(2)}) %all-to-all-start.1) | async-done | bytes 524320 | tf_op jit(solution)/shard_map/all_to_all | solution.py:126
  47.8 7.0 %all-to-all-start.2 = ((bf16[16,16,2048]{2,1,0:T(8,128)(2,1)}), bf16[16,16,2048]{2,1,0:T(8,128)(2,1)S(1)}, u32[]{:S(2)}, u32[]{:S(2)}) async-start(bf16[16,16,2048]{2,1,0:T(8,128)(2,1)} %bitcast.8), calls=%async_computation.2 | async-start | bytes 2097152 | tf_op jit(solution)/shard_map/all_to_all | solution.py:135
  54.8 0.0 copy-start.5
  54.8 1.4 shard_map.94
  56.2 14.5 %all-to-all-done.2 = bf16[16,16,2048]{2,1,0:T(8,128)(2,1)S(1)} async-done(((bf16[16,16,2048]{2,1,0:T(8,128)(2,1)}), bf16[16,16,2048]{2,1,0:T(8,128)(2,1)S(1)}, u32[]{:S(2)}, u32[]{:S(2)}) %all-to-all-start.2) | async-done | bytes 1048608 | tf_op jit(solution)/shard_map/all_to_all | solution.py:135
  70.7 3.7 %all-to-all-start.3 = ((bf16[16,16,2048]{2,1,0:T(8,128)(2,1)}), bf16[16,16,2048]{2,1,0:T(8,128)(2,1)S(1)}, u32[]{:S(2)}, u32[]{:S(2)}) async-start(bf16[16,16,2048]{2,1,0:T(8,128)(2,1)} %bitcast.10), calls=%async_computation.3 | async-start | bytes 2097152 | tf_op jit(solution)/shard_map/all_to_all | solution.py:135
  74.3 15.9 %all-to-all-done.3 = bf16[16,16,2048]{2,1,0:T(8,128)(2,1)S(1)} async-done(((bf16[16,16,2048]{2,1,0:T(8,128)(2,1)}), bf16[16,16,2048]{2,1,0:T(8,128)(2,1)S(1)}, u32[]{:S(2)}, u32[]{:S(2)}) %all-to-all-start.3) | async-done | bytes 1048608 | tf_op jit(solution)/shard_map/all_to_all | solution.py:135
  90.2 1.4 copy-done.1
  91.6 1.4 copy-done.2
  93.0 2.0 %shard_map.95 = bf16[192,256]{1,0:T(8,128)(2,1)S(1)} custom-call(s32[1]{0:T(128)} %bitcast.half_ref, bf16[256,2048]{1,0:T(8,128)(2,1)S(1)} %bitcast.19, bf16[256,2048]{1,0:T(8,128)(2,1)S(1)} %bitcast.20, bf16[1,4096]{1,0:T(2,128)(2,1)S(1)} %copy-done.5, bf16[192,4096]{1,0:T(8,128)(2,1)S(1)} %bitcast.22, bf16[192,4096]{1,0:T(8,128)(2,1)S(1)} %bitcast.23), custom_call_target="tpu_custom_call" | custom-call | tf_op jit(solution)/shard_map/pallas_call | solution.py:23
  95.1 0.8 broadcast_in_dim.35
  95.9 6.7 %all-to-all-start.4 = ((bf16[4,192,256]{2,1,0:T(8,128)(2,1)}), bf16[4,192,256]{2,1,0:T(8,128)(2,1)S(1)}, u32[]{:S(2)}, u32[]{:S(2)}) async-start(bf16[4,192,256]{2,1,0:T(8,128)(2,1)} %broadcast_in_dim.35), calls=%async_computation.4 | async-start | bytes 786432 | tf_op jit(solution)/shard_map/all_to_all | solution.py:126
  102.5 5.2 %collective-permute-start.1 = (bf16[192,256]{1,0:T(8,128)(2,1)S(1)}, bf16[192,256]{1,0:T(8,128)(2,1)S(1)}, u32[]{:S(2)}, u32[]{:S(2)}) collective-permute-start(bf16[192,256]{1,0:T(8,128)(2,1)S(1)} %shard_map.95), channel_id=1, source_target_pairs={{0,4},{1,5},{2,6},{3,7},{4,0},{5,1},{6,2},{7,3},{8,12},{9,13},{10,... | collective-permute-start | bytes 294920 | tf_op jit(solution)/shard_map/ppermute | solution.py:130
  107.7 7.2 %collective-permute-done.1 = bf16[192,256]{1,0:T(8,128)(2,1)S(1)} collective-permute-done((bf16[192,256]{1,0:T(8,128)(2,1)S(1)}, bf16[192,256]{1,0:T(8,128)(2,1)S(1)}, u32[]{:S(2)}, u32[]{:S(2)}) %collective-permute-start.1) | collective-permute-done | bytes 98336 | tf_op jit(solution)/shard_map/ppermute | solution.py:130
  115.0 12.9 %all_to_all.35.second_ref = bf16[4,192,256]{2,1,0:T(8,128)(2,1)S(1)} all-to-all(bf16[4,192,256]{2,1,0:T(8,128)(2,1)S(1)} %broadcast_in_dim.36), channel_id=1, replica_groups={{0,1,2,3},{4,5,6,7},{8,9,10,11},{12,13,14,15},{16,17,18,19},{20,21,22,2..., dimensions={0} | all-to-all | bytes 786432 | tf_op jit(solution)/shard_map/all_to_all | solution.py:126
  127.9 1.4 shard_map.96
  129.4 6.4 %all-to-all-start.6 = ((bf16[16,16,512]{2,1,0:T(8,128)(2,1)}), bf16[16,16,512]{2,1,0:T(8,128)(2,1)S(1)}, u32[]{:S(2)}, u32[]{:S(2)}) async-start(bf16[16,16,512]{2,1,0:T(8,128)(2,1)} %bitcast.15), calls=%async_computation.6 | async-start | bytes 524288 | tf_op jit(solution)/shard_map/all_to_all | solution.py:135
  135.8 0.7 shard_map.92
  136.5 7.8 %all-to-all-done.6 = bf16[16,16,512]{2,1,0:T(8,128)(2,1)S(1)} async-done(((bf16[16,16,512]{2,1,0:T(8,128)(2,1)}), bf16[16,16,512]{2,1,0:T(8,128)(2,1)S(1)}, u32[]{:S(2)}, u32[]{:S(2)}) %all-to-all-start.6) | async-done | bytes 262176 | tf_op jit(solution)/shard_map/all_to_all | solution.py:135
  144.3 0.3 shard_map.97
  144.5 1.9 %collective-permute-start.2 = (bf16[128,512]{1,0:T(8,128)(2,1)S(1)}, bf16[128,512]{1,0:T(8,128)(2,1)S(1)}, u32[]{:S(2)}, u32[]{:S(2)}) collective-permute-start(bf16[128,512]{1,0:T(8,128)(2,1)S(1)} %shard_map.97), channel_id=1, source_target_pairs={{0,128},{128,256},{256,384},{384,0},{1,129},{129,257},{257,385},{3... | collective-permute-start | bytes 393224 | tf_op jit(solution)/shard_map/ppermute | solution.py:194
  146.4 17.3 %collective-permute-done.2 = bf16[128,512]{1,0:T(8,128)(2,1)S(1)} collective-permute-done((bf16[128,512]{1,0:T(8,128)(2,1)S(1)}, bf16[128,512]{1,0:T(8,128)(2,1)S(1)}, u32[]{:S(2)}, u32[]{:S(2)}) %collective-permute-start.2) | collective-permute-done | bytes 131104 | tf_op jit(solution)/shard_map/ppermute | solution.py:194
  163.8 0.7 copy.13
  (16 shorter events, 0.1 us)
Async XLA Ops:
  0.0 10.7 %copy-start.3 = (bf16[1,128,512]{2,1,0:T(8,128)(2,1)S(1)}, bf16[1,128,512]{2,1,0:T(8,128)(2,1)}, u32[]{:S(2)}) copy-start(bf16[1,128,512]{2,1,0:T(8,128)(2,1)} %param.9) | copy-start | bytes 393220
  0.0 37.9 %copy-start.7 = (s32[1,16]{1,0:T(1,128)S(1)}, s32[1,16]{1,0:T(1,128)}, u32[]{:S(2)}) copy-start(s32[1,16]{1,0:T(1,128)} %param.11) | copy-start | bytes 196
  0.0 38.0 %copy-start.6 = (s32[1,128,8]{1,2,0:T(8,128)S(1)}, s32[1,128,8]{1,2,0:T(8,128)}, u32[]{:S(2)}) copy-start(s32[1,128,8]{1,2,0:T(8,128)} %param.10) | copy-start | bytes 12292
  1.8 23.5 %all-to-all-start = ((bf16[4,128,512]{2,1,0:T(8,128)(2,1)}), bf16[4,128,512]{2,1,0:T(8,128)(2,1)S(1)}, u32[]{:S(2)}, u32[]{:S(2)}) async-start(bf16[4,128,512]{2,1,0:T(8,128)(2,1)} %broadcast_in_dim.16), calls=%async_computation | async-start | bytes 1048576 | tf_op jit(solution)/shard_map/all_to_all | solution.py:126
  10.7 14.6 %collective-permute-start = (bf16[128,512]{1,0:T(8,128)(2,1)S(1)}, bf16[128,512]{1,0:T(8,128)(2,1)S(1)}, u32[]{:S(2)}, u32[]{:S(2)}) collective-permute-start(bf16[128,512]{1,0:T(8,128)(2,1)S(1)} %bitcast.26), channel_id=1, source_target_pairs={{0,4},{1,5},{2,6},{3,7},{4,0},{5,1},{6,2},{7,3},{8,12},{9,13},{10,... | collective-permute-start | bytes 393224 | tf_op jit(solution)/shard_map/ppermute | solution.py:130
  26.2 21.6 %all-to-all-start.1 = ((bf16[4,128,512]{2,1,0:T(8,128)(2,1)}), bf16[4,128,512]{2,1,0:T(8,128)(2,1)S(1)}, u32[]{:S(2)}, u32[]{:S(2)}) async-start(bf16[4,128,512]{2,1,0:T(8,128)(2,1)} %broadcast_in_dim.34), calls=%async_computation.1 | async-start | bytes 1048576 | tf_op jit(solution)/shard_map/all_to_all | solution.py:126
  47.8 22.9 %all-to-all-start.2 = ((bf16[16,16,2048]{2,1,0:T(8,128)(2,1)}), bf16[16,16,2048]{2,1,0:T(8,128)(2,1)S(1)}, u32[]{:S(2)}, u32[]{:S(2)}) async-start(bf16[16,16,2048]{2,1,0:T(8,128)(2,1)} %bitcast.8), calls=%async_computation.2 | async-start | bytes 2097152 | tf_op jit(solution)/shard_map/all_to_all | solution.py:135
  54.8 35.4 %copy-start.5 = (bf16[1,4096]{1,0:T(2,128)(2,1)S(1)}, bf16[1,4096]{1,0:T(2,128)(2,1)}, u32[]{:S(2)}) copy-start(bf16[1,4096]{1,0:T(2,128)(2,1)} %gain_ref.3) | copy-start | bytes 24580
  70.7 19.6 %all-to-all-start.3 = ((bf16[16,16,2048]{2,1,0:T(8,128)(2,1)}), bf16[16,16,2048]{2,1,0:T(8,128)(2,1)S(1)}, u32[]{:S(2)}, u32[]{:S(2)}) async-start(bf16[16,16,2048]{2,1,0:T(8,128)(2,1)} %bitcast.10), calls=%async_computation.3 | async-start | bytes 2097152 | tf_op jit(solution)/shard_map/all_to_all | solution.py:135
  90.2 1.4 copy-start.1
  91.6 1.4 copy-start.2
  95.1 32.8 %copy-start = (bf16[1,1,1536,512]{3,2,1,0:T(8,128)(2,1)S(1)}, bf16[1,1,1536,512]{3,2,1,0:T(8,128)(2,1)}, u32[]{:S(2)}) copy-start(bf16[1,1,1536,512]{3,2,1,0:T(8,128)(2,1)} %param.17) | copy-start | bytes 4718596
  95.9 19.1 %all-to-all-start.4 = ((bf16[4,192,256]{2,1,0:T(8,128)(2,1)}), bf16[4,192,256]{2,1,0:T(8,128)(2,1)S(1)}, u32[]{:S(2)}, u32[]{:S(2)}) async-start(bf16[4,192,256]{2,1,0:T(8,128)(2,1)} %broadcast_in_dim.35), calls=%async_computation.4 | async-start | bytes 786432 | tf_op jit(solution)/shard_map/all_to_all | solution.py:126
  102.5 12.4 %collective-permute-start.1 = (bf16[192,256]{1,0:T(8,128)(2,1)S(1)}, bf16[192,256]{1,0:T(8,128)(2,1)S(1)}, u32[]{:S(2)}, u32[]{:S(2)}) collective-permute-start(bf16[192,256]{1,0:T(8,128)(2,1)S(1)} %shard_map.95), channel_id=1, source_target_pairs={{0,4},{1,5},{2,6},{3,7},{4,0},{5,1},{6,2},{7,3},{8,12},{9,13},{10,... | collective-permute-start | bytes 294920 | tf_op jit(solution)/shard_map/ppermute | solution.py:130
  127.9 7.9 %copy-start.4 = (bf16[1,16,4096]{2,1,0:T(8,128)(2,1)S(1)}, bf16[1,16,4096]{2,1,0:T(8,128)(2,1)}, u32[]{:S(2)}) copy-start(bf16[1,16,4096]{2,1,0:T(8,128)(2,1)} %param.14) | copy-start | bytes 393220
  129.4 14.9 %all-to-all-start.6 = ((bf16[16,16,512]{2,1,0:T(8,128)(2,1)}), bf16[16,16,512]{2,1,0:T(8,128)(2,1)S(1)}, u32[]{:S(2)}, u32[]{:S(2)}) async-start(bf16[16,16,512]{2,1,0:T(8,128)(2,1)} %bitcast.15), calls=%async_computation.6 | async-start | bytes 524288 | tf_op jit(solution)/shard_map/all_to_all | solution.py:135
  144.5 19.3 %collective-permute-start.2 = (bf16[128,512]{1,0:T(8,128)(2,1)S(1)}, bf16[128,512]{1,0:T(8,128)(2,1)S(1)}, u32[]{:S(2)}, u32[]{:S(2)}) collective-permute-start(bf16[128,512]{1,0:T(8,128)(2,1)S(1)} %shard_map.97), channel_id=1, source_target_pairs={{0,128},{128,256},{256,384},{384,0},{1,129},{129,257},{257,385},{3... | collective-permute-start | bytes 393224 | tf_op jit(solution)/shard_map/ppermute | solution.py:194

commit v2 on v1

--- a/solution.py
+++ b/solution.py
@@ -12,6 +12,7 @@
 SLOTS = 16
 VM = pl.BlockSpec(memory_space=pltpu.VMEM)
 SM = pl.BlockSpec(memory_space=pltpu.SMEM)
+HB = pl.BlockSpec(memory_space=pltpu.HBM)
 FOURS = [[0, 1, 2, 3], [4, 5, 6, 7]]
 
 
@@ -19,9 +20,10 @@
     return lax.dot_general(a, b, (((da,), (db,)), ((), ())), preferred_element_type=F32)
 
 
-def call(body, shape, specs, args, flops=0, moved=0, limit=24):
+def call(body, shape, specs, args, scratch=(), flops=0, moved=0, limit=24):
     return pl.pallas_call(
         body,
+        scratch_shapes=list(scratch),
         out_shape=shape,
         in_specs=specs,
         out_specs=jax.tree.map(lambda _: VM, shape),
@@ -53,27 +55,39 @@
         match_ref[e * SLOTS : (e + 1) * SLOTS, :] = hit.astype(BF)
 
 
-def pick_body(match_ref, rows_ref, out_ref):
-    parts, _, width = rows_ref.shape
+def blocks_of(rank, half, width):
+    order = [half * 4 + k for k in range(4)] + [rank ^ 4 ^ k for k in range(4)]
+    return [pl.ds(pl.multiple_of(r * width, width), width) for r in order]
+
+
+def pick_first_body(match_ref, group_ref, other_ref, out_ref):
+    parts, _, width = group_ref.shape
     for k in range(parts):
-        out_ref[:, k * width : (k + 1) * width] = dot(match_ref[...], rows_ref[k], 1, 0).astype(BF)
-
-
-def weigh_body(half_ref, first_ref, second_ref, gain_ref, router_ref, ids_ref, match_ref, high_ref, low_ref):
-    parts, n, width = first_ref.shape
-    full = 2 * parts * width
+        out_ref[:, k * width : (k + 1) * width] = dot(match_ref[...], group_ref[k], 1, 0).astype(BF)
+    out_ref[:, parts * width :] = dot(match_ref[...], other_ref[...], 1, 0).astype(BF)
+
+
+def pick_second_body(match_ref, *refs):
+    *rows_refs, out_ref = refs
+    width = rows_refs[0].shape[1]
+    for k, ref in enumerate(rows_refs):
+        out_ref[:, k * width : (k + 1) * width] = dot(match_ref[...], ref[...], 1, 0).astype(BF)
+
+
+def weigh_body(group_ref, a_ref, b_ref, c_ref, d_ref, gain_ref, router_ref, ids_ref, match_ref, high_ref, low_ref):
+    n, width = a_ref.shape
+    rank = lax.axis_index("tensor")
+    blocks = blocks_of(rank, rank // 4, width)
+    views = [group_ref.at[k] for k in range(4)] + [a_ref, b_ref, c_ref, d_ref]
     squares = jnp.zeros((n, 1), F32)
-    for ref in (first_ref, second_ref):
-        for k in range(parts):
-            v = ref[k].astype(F32)
-            squares = squares + jnp.sum(v * v, axis=1, keepdims=True)
-    inverse = lax.rsqrt(squares / full + norm_eps)
+    for view in views:
+        v = view[...].astype(F32)
+        squares = squares + jnp.sum(v * v, axis=1, keepdims=True)
+    inverse = lax.rsqrt(squares / (8 * width) + norm_eps)
     logits = jnp.zeros((EXPERTS, n), F32)
-    for ref, half in ((first_ref, half_ref[0]), (second_ref, 1 - half_ref[0])):
-        for k in range(parts):
-            cols = pl.ds(pl.multiple_of((half * parts + k) * width, width), width)
-            normed = (ref[k].astype(F32) * inverse * gain_ref[:, cols].astype(F32)).astype(BF)
-            logits = logits + dot(router_ref[:, cols], normed, 1, 1)
+    for view, cols in zip(views, blocks):
+        normed = (view[...].astype(F32) * inverse * gain_ref[:, cols].astype(F32)).astype(BF)
+        logits = logits + dot(router_ref[:, cols], normed, 1, 1)
     powered = jnp.exp(logits) * choices(ids_ref[...])
     weight = powered / jnp.sum(powered, axis=0, keepdims=True)
     for e in range(EXPERTS):
@@ -84,25 +98,34 @@
         low_ref[rows, :] = (value - high.astype(F32)).astype(BF)
 
 
-def expand_body(half_ref, first_ref, second_ref, gain_ref, gate_ref, up_ref, out_ref):
-    rows, span = first_ref.shape
-    step = 512
+def expand_body(first_ref, second_ref, gain_ref, gate_ref, up_ref, out_ref, gate_buf, up_buf, sems):
+    rows = first_ref.shape[0]
+    parts, hid, width = gate_buf.shape
+    rank = lax.axis_index("tensor")
+    blocks = blocks_of(rank, rank // 4, width)
+    copies = []
+    for k, cols in enumerate(blocks):
+        one = pltpu.make_async_copy(gate_ref.at[:, cols], gate_buf.at[k], sems.at[0, k])
+        two = pltpu.make_async_copy(up_ref.at[:, cols], up_buf.at[k], sems.at[1, k])
+        one.start()
+        two.start()
+        copies.append((one, two))
+    cut = first_ref.shape[1] // width
+    views = [first_ref.at[:, k * width : (k + 1) * width] for k in range(cut)]
+    views += [second_ref.at[:, k * width : (k + 1) * width] for k in range(parts - cut)]
     squares = jnp.zeros((rows, 1), F32)
-    for ref in (first_ref, second_ref):
-        for k in range(span // step):
-            v = ref[:, k * step : (k + 1) * step].astype(F32)
-            squares = squares + jnp.sum(v * v, axis=1, keepdims=True)
-    inverse = lax.rsqrt(squares / (2 * span) + norm_eps)
-    hid = gate_ref.shape[0]
+    for view in views:
+        v = view[...].astype(F32)
+        squares = squares + jnp.sum(v * v, axis=1, keepdims=True)
+    inverse = lax.rsqrt(squares / (parts * width) + norm_eps)
     gate = jnp.zeros((hid, rows), F32)
     up = jnp.zeros((hid, rows), F32)
-    for ref, half in ((first_ref, half_ref[0]), (second_ref, 1 - half_ref[0])):
-        for k in range(span // step):
-            cols = pl.ds(pl.multiple_of(half * span + k * step, step), step)
-            v = ref[:, k * step : (k + 1) * step].astype(F32)
-            normed = (v * inverse * gain_ref[:, cols].astype(F32)).astype(BF)
-            gate = gate + dot(gate_ref[:, cols], normed, 1, 1)
-            up = up + dot(up_ref[:, cols], normed, 1, 1)
+    for k, (view, cols) in enumerate(zip(views, blocks)):
+        normed = (view[...].astype(F32) * inverse * gain_ref[:, cols].astype(F32)).astype(BF)
+        for copy in copies[k]:
+            copy.wait()
+        gate = gate + dot(gate_buf[k], normed, 1, 1)
+        up = up + dot(up_buf[k], normed, 1, 1)
     out_ref[...] = (gate / (1.0 + jnp.exp(-gate)) * up).astype(BF)
 
 
@@ -126,8 +149,8 @@
     return lax.all_to_all(copies, "tensor", 0, 0, axis_index_groups=FOURS)
 
 
-def across(shard):
-    return lax.ppermute(shard, "tensor", [(i, i ^ 4) for i in range(8)])
+def along(shard, by):
+    return lax.ppermute(shard, "tensor", [(i, i ^ by) for i in range(8)])
 
 
 def over_dp(rows):
@@ -160,24 +183,32 @@
     hid = w_gate.shape[0]
     half = (lax.axis_index("tensor") // 4).astype(jnp.int32)[None]
 
-    other = across(tokens)
-    first = to_fours(tokens)
+    other = along(tokens, 4)
+    group = to_fours(tokens)
     match = call(route_body, jax.ShapeDtypeStruct((slots, n), BF), [SM, VM, VM], (length, ids, quota))
-    out_rows = jax.ShapeDtypeStruct((slots, 4 * width), BF)
-    first_rows = over_dp(call(pick_body, out_rows, [VM] * 2, (match, first)))
-    second = to_fours(other)
-    second_rows = over_dp(call(pick_body, out_rows, [VM] * 2, (match, second)))
+    first = call(
+        pick_first_body, jax.ShapeDtypeStruct((slots, 5 * width), BF), [VM] * 3, (match, group, other)
+    )
+    first_rows = over_dp(first)
+    rest = [along(other, by) for by in (1, 2, 3)]
+    second = call(
+        pick_second_body, jax.ShapeDtypeStruct((slots, 3 * width), BF), [VM] * 4, (match, *rest)
+    )
+    first_rows, second = lax.optimization_barrier((first_rows, second))
+    second_rows = over_dp(second)
     pair = jax.ShapeDtypeStruct((slots, n), BF)
     high, low = call(
-        weigh_body, (pair, pair), [SM] + [VM] * 6, (half, first, second, gain, router, ids, match)
+        weigh_body, (pair, pair), [VM] * 9, (group, other, *rest, gain, router, ids, match)
     )
     hidden = call(
         expand_body,
         jax.ShapeDtypeStruct((hid, slots), BF),
-        [SM] + [VM] * 5,
-        (half, first_rows, second_rows, gain, w_gate, w_up),
-    )
-    hidden_other = across(hidden)
+        [VM] * 3 + [HB] * 2,
+        (first_rows, second_rows, gain, w_gate, w_up),
+        [pltpu.VMEM((8, hid, width), BF)] * 2 + [pltpu.SemaphoreType.DMA((2, 8))],
+        limit=48,
+    )
+    hidden_other = along(hidden, 4)
     hidden_first = to_fours(hidden)
     hidden_second = to_fours(hidden_other)
     reply = call(

time: 165 us -> 148 us (0.90)
  the two profiles are of different devices: /device:TPU:32 before, /device:TPU:1 now
where the time goes in v2:
time: 148 us; the launch traced here: 147 us
  starting transfers between devices  83.2 us (56%)
  waiting for transfers between devices  30.2 us (20%)
  blocking collectives  16.7 us (11%)
  local copies, waits for them, and re-layouts  8.62 us (6%)
  Pallas kernels  7.65 us (5%)
    ppermute x5, starting transfers between devices, along(): return lax.ppermute(shard, 'tensor', [(i, i ^ by) for i in range(8)])  26.6 us
    all_to_all x3, starting transfers between devices, to_fours(): return lax.all_to_all(copies, 'tensor', 0, 0, axis_index_groups=FOURS)  22.6 us
    all_to_all x2, starting transfers between devices, over_dp(): lax.all_to_all(rows.reshape(EXPERTS, n // EXPERTS, width), 'dp', 0, 0)  19.1 us
    all_to_all x1, blocking collectives, over_dp(): lax.all_to_all(rows.reshape(EXPERTS, n // EXPERTS, width), 'dp', 0, 0)  16.7 us
    ppermute x1, starting transfers between devices, on_device(): lax.ppermute(layer_out, 'section', [(i, (i + 1) % count) for i in range(c...  14.9 us
    ppermute x5, waiting for transfers between devices, along(): return lax.ppermute(shard, 'tensor', [(i, i ^ by) for i in range(8)])  12 us
    all_to_all x3, waiting for transfers between devices, to_fours(): return lax.all_to_all(copies, 'tensor', 0, 0, axis_index_groups=FOURS)  8.7 us
    pallas_call x7, Pallas kernels, call(): pl.pallas_call(body, scratch_shapes=list(scratch), out_shape=shape, in_sp...  7.65 us
  transfers between devices with their start and end apart: 11, of which 7 were waited for; matrix products, arithmetic and copies ran while one was open for 0% of the time, Pallas kernels for 1%

profile of v2, /device:TPU:1, one launch (start us, length us, event | category | flops | bytes accessed | tf_op | source)
XLA Modules:
  0.0 147.3 jit_solution(5957293779786802073)
XLA Ops:
  0.0 1.8 %broadcast_in_dim.26 = bf16[4,128,512]{2,1,0:T(8,128)(2,1)} broadcast(bf16[128,512]{1,0:T(8,128)(2,1)} %bitcast.26), dimensions={1,2} | broadcast | bytes 655360 | tf_op jit(solution)/shard_map/broadcast_in_dim | solution.py:148
  1.8 6.4 %all-to-all-start = ((bf16[4,128,512]{2,1,0:T(8,128)(2,1)}), bf16[4,128,512]{2,1,0:T(8,128)(2,1)S(1)}, u32[]{:S(2)}, u32[]{:S(2)}) async-start(bf16[4,128,512]{2,1,0:T(8,128)(2,1)} %broadcast_in_dim.26), calls=%async_computation | async-start | bytes 1048576 | tf_op jit(solution)/shard_map/all_to_all | solution.py:149
  8.3 8.8 %collective-permute-start = (bf16[128,512]{1,0:T(8,128)(2,1)S(1)}, bf16[128,512]{1,0:T(8,128)(2,1)S(1)}, u32[]{:S(2)}, u32[]{:S(2)}) collective-permute-start(bf16[128,512]{1,0:T(8,128)(2,1)S(1)} %bitcast.27), channel_id=1, source_target_pairs={{0,4},{1,5},{2,6},{3,7},{4,0},{5,1},{6,2},{7,3},{8,12},{9,13},{10,... | collective-permute-start | bytes 393224 | tf_op jit(solution)/shard_map/ppermute | solution.py:153
  18.0 1.7 %collective-permute-done.a_ref.other_ref = bf16[128,512]{1,0:T(8,128)(2,1)S(1)} collective-permute-done((bf16[128,512]{1,0:T(8,128)(2,1)S(1)}, bf16[128,512]{1,0:T(8,128)(2,1)S(1)}, u32[]{:S(2)}, u32[]{:S(2)}) %collective-permute-start) | collective-permute-done | bytes 131104 | tf_op jit(solution)/shard_map/ppermute | solution.py:153
  19.6 1.0 all-to-all-done.group_ref
  20.6 1.6 %shard_map.93 = bf16[256,2560]{1,0:T(8,128)(2,1)} custom-call(bf16[256,128]{1,0:T(8,128)(2,1)S(1)} %shard_map.91.match_ref, bf16[4,128,512]{2,1,0:T(8,128)(2,1)S(1)} %all-to-all-done.group_ref, bf16[128,512]{1,0:T(8,128)(2,1)S(1)} %collective-permute-done.a_ref.other_ref), custom_call_target="tpu_custom_call" | custom-call | tf_op jit(solution)/shard_map/pallas_call | solution.py:24
  22.2 14.0 %all-to-all-start.1 = ((bf16[16,16,2560]{2,1,0:T(8,128)(2,1)}), bf16[16,16,2560]{2,1,0:T(8,128)(2,1)S(1)}, u32[]{:S(2)}, u32[]{:S(2)}) async-start(bf16[16,16,2560]{2,1,0:T(8,128)(2,1)} %bitcast.8), calls=%async_computation.1 | async-start | bytes 2621440 | tf_op jit(solution)/shard_map/all_to_all | solution.py:158
  36.2 1.9 %collective-permute-start.1 = (bf16[128,512]{1,0:T(8,128)(2,1)S(1)}, bf16[128,512]{1,0:T(8,128)(2,1)S(1)}, u32[]{:S(2)}, u32[]{:S(2)}) collective-permute-start(bf16[128,512]{1,0:T(8,128)(2,1)S(1)} %collective-permute-done.a_ref.other_ref), channel_id=1, source_target_pairs={{0,1},{1,0},{2,3},{3,2},{4,5},{5,4},{6,7},{7,6},{8,9},{9,8},{10,11... | collective-permute-start | bytes 393224 | tf_op jit(solution)/shard_map/ppermute | solution.py:153
  38.1 8.8 %collective-permute-start.2 = (bf16[128,512]{1,0:T(8,128)(2,1)S(1)}, bf16[128,512]{1,0:T(8,128)(2,1)S(1)}, u32[]{:S(2)}, u32[]{:S(2)}) collective-permute-start(bf16[128,512]{1,0:T(8,128)(2,1)S(1)} %collective-permute-done.a_ref.other_ref), channel_id=1, source_target_pairs={{0,2},{1,3},{2,0},{3,1},{4,6},{5,7},{6,4},{7,5},{8,10},{9,11},{10,... | collective-permute-start | bytes 393224 | tf_op jit(solution)/shard_map/ppermute | solution.py:153
  47.0 3.1 %collective-permute-start.3 = (bf16[128,512]{1,0:T(8,128)(2,1)S(1)}, bf16[128,512]{1,0:T(8,128)(2,1)S(1)}, u32[]{:S(2)}, u32[]{:S(2)}) collective-permute-start(bf16[128,512]{1,0:T(8,128)(2,1)S(1)} %collective-permute-done.a_ref.other_ref), channel_id=1, source_target_pairs={{0,3},{1,2},{2,1},{3,0},{4,7},{5,6},{6,5},{7,4},{8,11},{9,10},{10,... | collective-permute-start | bytes 393224 | tf_op jit(solution)/shard_map/ppermute | solution.py:153
  50.1 4.9 %collective-permute-done.3.d_ref.refs_2_ = bf16[128,512]{1,0:T(8,128)(2,1)S(1)} collective-permute-done((bf16[128,512]{1,0:T(8,128)(2,1)S(1)}, bf16[128,512]{1,0:T(8,128)(2,1)S(1)}, u32[]{:S(2)}, u32[]{:S(2)}) %collective-permute-start.3) | collective-permute-done | bytes 131104 | tf_op jit(solution)/shard_map/ppermute | solution.py:153
  55.3 0.6 copy-done.9
  56.0 0.7 copy-done.11
  56.6 16.7 %all_to_all.30 = bf16[16,16,1536]{2,1,0:T(8,128)(2,1)S(1)} all-to-all(bf16[16,16,1536]{2,1,0:T(8,128)(2,1)S(1)} %bitcast.20), channel_id=1, replica_groups=mesh['section'=4,'dp'=16,'tensor'=8] {'dp'}, dimensions={0} | all-to-all | bytes 1572864 | tf_op jit(solution)/shard_map/all_to_all | solution.py:158
  73.4 1.4 copy-done.2
  74.8 3.2 %shard_map.95 = bf16[192,256]{1,0:T(8,128)(2,1)S(1)} custom-call(bf16[256,2560]{1,0:T(8,128)(2,1)S(1)} %bitcast.19, bf16[256,1536]{1,0:T(8,128)(2,1)S(1)} %bitcast.21, bf16[1,4096]{1,0:T(2,128)(2,1)S(1)} %copy-done.14, bf16[192,4096]{1,0:T(8,128)(2,1)S(1)} %bitcast.23, bf16[192,4096]{1,0:T(8,128)(2,1)S(1)} %bitcast.24), custom_call_target="tpu_custom_call" | custom-call | tf_op jit(solution)/shard_map/pallas_call | solution.py:24
  78.0 0.8 broadcast_in_dim.28
  78.8 8.4 %all-to-all-start.3 = ((bf16[4,192,256]{2,1,0:T(8,128)(2,1)}), bf16[4,192,256]{2,1,0:T(8,128)(2,1)S(1)}, u32[]{:S(2)}, u32[]{:S(2)}) async-start(bf16[4,192,256]{2,1,0:T(8,128)(2,1)} %broadcast_in_dim.28), calls=%async_computation.3 | async-start | bytes 786432 | tf_op jit(solution)/shard_map/all_to_all | solution.py:149
  87.2 4.0 %collective-permute-start.4 = (bf16[192,256]{1,0:T(8,128)(2,1)S(1)}, bf16[192,256]{1,0:T(8,128)(2,1)S(1)}, u32[]{:S(2)}, u32[]{:S(2)}) collective-permute-start(bf16[192,256]{1,0:T(8,128)(2,1)S(1)} %shard_map.95), channel_id=1, source_target_pairs={{0,4},{1,5},{2,6},{3,7},{4,0},{5,1},{6,2},{7,3},{8,12},{9,13},{10,... | collective-permute-start | bytes 294920 | tf_op jit(solution)/shard_map/ppermute | solution.py:153
  91.2 5.5 %collective-permute-done.4 = bf16[192,256]{1,0:T(8,128)(2,1)S(1)} collective-permute-done((bf16[192,256]{1,0:T(8,128)(2,1)S(1)}, bf16[192,256]{1,0:T(8,128)(2,1)S(1)}, u32[]{:S(2)}, u32[]{:S(2)}) %collective-permute-start.4) | collective-permute-done | bytes 98336 | tf_op jit(solution)/shard_map/ppermute | solution.py:153
  96.7 0.8 broadcast_in_dim.29
  97.4 7.8 %all-to-all-start.4 = ((bf16[4,192,256]{2,1,0:T(8,128)(2,1)}), bf16[4,192,256]{2,1,0:T(8,128)(2,1)S(1)}, u32[]{:S(2)}, u32[]{:S(2)}) async-start(bf16[4,192,256]{2,1,0:T(8,128)(2,1)} %broadcast_in_dim.29), calls=%async_computation.4 | async-start | bytes 786432 | tf_op jit(solution)/shard_map/all_to_all | solution.py:149
  105.2 7.7 %all-to-all-done.4.second_ref = bf16[4,192,256]{2,1,0:T(8,128)(2,1)S(1)} async-done(((bf16[4,192,256]{2,1,0:T(8,128)(2,1)}), bf16[4,192,256]{2,1,0:T(8,128)(2,1)S(1)}, u32[]{:S(2)}, u32[]{:S(2)}) %all-to-all-start.4) | async-done | bytes 393248 | tf_op jit(solution)/shard_map/all_to_all | solution.py:149
  113.0 1.4 shard_map.96
  114.4 5.1 %all-to-all-start.5 = ((bf16[16,16,512]{2,1,0:T(8,128)(2,1)}), bf16[16,16,512]{2,1,0:T(8,128)(2,1)S(1)}, u32[]{:S(2)}, u32[]{:S(2)}) async-start(bf16[16,16,512]{2,1,0:T(8,128)(2,1)} %bitcast.15), calls=%async_computation.5 | async-start | bytes 524288 | tf_op jit(solution)/shard_map/all_to_all | solution.py:158
  119.5 0.9 copy-done.12
  120.4 0.9 copy-done.13
  121.3 0.7 shard_map.92
  122.0 4.8 %all-to-all-done.5 = bf16[16,16,512]{2,1,0:T(8,128)(2,1)S(1)} async-done(((bf16[16,16,512]{2,1,0:T(8,128)(2,1)}), bf16[16,16,512]{2,1,0:T(8,128)(2,1)S(1)}, u32[]{:S(2)}, u32[]{:S(2)}) %all-to-all-start.5) | async-done | bytes 262176 | tf_op jit(solution)/shard_map/all_to_all | solution.py:158
  127.0 14.9 %collective-permute-start.5 = (bf16[128,512]{1,0:T(8,128)(2,1)S(1)}, bf16[128,512]{1,0:T(8,128)(2,1)S(1)}, u32[]{:S(2)}, u32[]{:S(2)}) collective-permute-start(bf16[128,512]{1,0:T(8,128)(2,1)S(1)} %shard_map.97), channel_id=1, source_target_pairs={{0,128},{128,256},{256,384},{384,0},{1,129},{129,257},{257,385},{3... | collective-permute-start | bytes 393224 | tf_op jit(solution)/shard_map/ppermute | solution.py:225
  141.9 4.7 %collective-permute-done.5 = bf16[128,512]{1,0:T(8,128)(2,1)S(1)} collective-permute-done((bf16[128,512]{1,0:T(8,128)(2,1)S(1)}, bf16[128,512]{1,0:T(8,128)(2,1)S(1)}, u32[]{:S(2)}, u32[]{:S(2)}) %collective-permute-start.5) | collective-permute-done | bytes 131104 | tf_op jit(solution)/shard_map/ppermute | solution.py:225
  146.6 0.7 copy.13
  (37 shorter events, 0.9 us)
Async XLA Ops:
  0.0 8.3 %copy-start.3 = (bf16[1,128,512]{2,1,0:T(8,128)(2,1)S(1)}, bf16[1,128,512]{2,1,0:T(8,128)(2,1)}, u32[]{:S(2)}) copy-start(bf16[1,128,512]{2,1,0:T(8,128)(2,1)} %param.9) | copy-start | bytes 393220
  0.0 17.7 %copy-start.16 = (s32[1,16]{1,0:T(1,128)S(1)}, s32[1,16]{1,0:T(1,128)}, u32[]{:S(2)}) copy-start(s32[1,16]{1,0:T(1,128)} %param.11) | copy-start | bytes 196
  0.0 17.8 %copy-start.15 = (s32[1,128,8]{1,2,0:T(8,128)S(1)}, s32[1,128,8]{1,2,0:T(8,128)}, u32[]{:S(2)}) copy-start(s32[1,128,8]{1,2,0:T(8,128)} %param.10) | copy-start | bytes 12292
  1.8 18.8 %all-to-all-start = ((bf16[4,128,512]{2,1,0:T(8,128)(2,1)}), bf16[4,128,512]{2,1,0:T(8,128)(2,1)S(1)}, u32[]{:S(2)}, u32[]{:S(2)}) async-start(bf16[4,128,512]{2,1,0:T(8,128)(2,1)} %broadcast_in_dim.26), calls=%async_computation | async-start | bytes 1048576 | tf_op jit(solution)/shard_map/all_to_all | solution.py:149
  8.3 11.4 %collective-permute-start = (bf16[128,512]{1,0:T(8,128)(2,1)S(1)}, bf16[128,512]{1,0:T(8,128)(2,1)S(1)}, u32[]{:S(2)}, u32[]{:S(2)}) collective-permute-start(bf16[128,512]{1,0:T(8,128)(2,1)S(1)} %bitcast.27), channel_id=1, source_target_pairs={{0,4},{1,5},{2,6},{3,7},{4,0},{5,1},{6,2},{7,3},{8,12},{9,13},{10,... | collective-permute-start | bytes 393224 | tf_op jit(solution)/shard_map/ppermute | solution.py:153
  19.6 27.3 %copy-start.5 = (bf16[128,512]{1,0:T(8,128)(2,1)}, bf16[128,512]{1,0:T(8,128)(2,1)S(1)}, u32[]{:S(2)}) copy-start(bf16[128,512]{1,0:T(8,128)(2,1)S(1)} %collective-permute-done.a_ref.other_ref) | copy-start | bytes 393220
  22.2 34.5 %all-to-all-start.1 = ((bf16[16,16,2560]{2,1,0:T(8,128)(2,1)}), bf16[16,16,2560]{2,1,0:T(8,128)(2,1)S(1)}, u32[]{:S(2)}, u32[]{:S(2)}) async-start(bf16[16,16,2560]{2,1,0:T(8,128)(2,1)} %bitcast.8), calls=%async_computation.1 | async-start | bytes 2621440 | tf_op jit(solution)/shard_map/all_to_all | solution.py:158
  36.2 37.2 %copy-start.14 = (bf16[1,4096]{1,0:T(2,128)(2,1)S(1)}, bf16[1,4096]{1,0:T(2,128)(2,1)}, u32[]{:S(2)}) copy-start(bf16[1,4096]{1,0:T(2,128)(2,1)} %gain_ref.3) | copy-start | bytes 24580
  36.2 13.9 %collective-permute-start.1 = (bf16[128,512]{1,0:T(8,128)(2,1)S(1)}, bf16[128,512]{1,0:T(8,128)(2,1)S(1)}, u32[]{:S(2)}, u32[]{:S(2)}) collective-permute-start(bf16[128,512]{1,0:T(8,128)(2,1)S(1)} %collective-permute-done.a_ref.other_ref), channel_id=1, source_target_pairs={{0,1},{1,0},{2,3},{3,2},{4,5},{5,4},{6,7},{7,6},{8,9},{9,8},{10,11... | collective-permute-start | bytes 393224 | tf_op jit(solution)/shard_map/ppermute | solution.py:153
  38.1 12.0 %collective-permute-start.2 = (bf16[128,512]{1,0:T(8,128)(2,1)S(1)}, bf16[128,512]{1,0:T(8,128)(2,1)S(1)}, u32[]{:S(2)}, u32[]{:S(2)}) collective-permute-start(bf16[128,512]{1,0:T(8,128)(2,1)S(1)} %collective-permute-done.a_ref.other_ref), channel_id=1, source_target_pairs={{0,2},{1,3},{2,0},{3,1},{4,6},{5,7},{6,4},{7,5},{8,10},{9,11},{10,... | collective-permute-start | bytes 393224 | tf_op jit(solution)/shard_map/ppermute | solution.py:153
  47.0 8.0 %collective-permute-start.3 = (bf16[128,512]{1,0:T(8,128)(2,1)S(1)}, bf16[128,512]{1,0:T(8,128)(2,1)S(1)}, u32[]{:S(2)}, u32[]{:S(2)}) collective-permute-start(bf16[128,512]{1,0:T(8,128)(2,1)S(1)} %collective-permute-done.a_ref.other_ref), channel_id=1, source_target_pairs={{0,3},{1,2},{2,1},{3,0},{4,7},{5,6},{6,5},{7,4},{8,11},{9,10},{10,... | collective-permute-start | bytes 393224 | tf_op jit(solution)/shard_map/ppermute | solution.py:153
  50.1 23.3 %copy-start.7 = (bf16[128,512]{1,0:T(8,128)(2,1)}, bf16[128,512]{1,0:T(8,128)(2,1)S(1)}, u32[]{:S(2)}) copy-start(bf16[128,512]{1,0:T(8,128)(2,1)S(1)} %collective-permute-done.1.b_ref.refs_0_) | copy-start | bytes 393220
  55.3 0.6 copy-start.9
  56.0 0.7 copy-start.11
  56.6 16.7 %copy-start.1 = (bf16[1,1,192,4096]{3,2,1,0:T(8,128)(2,1)S(1)}, bf16[1,1,192,4096]{3,2,1,0:T(8,128)(2,1)}, u32[]{:S(2)}) copy-start(bf16[1,1,192,4096]{3,2,1,0:T(8,128)(2,1)} %param.15) | copy-start | bytes 4718596
  73.4 1.4 copy-start.2
  78.0 34.9 %copy-start = (bf16[1,1,1536,512]{3,2,1,0:T(8,128)(2,1)S(1)}, bf16[1,1,1536,512]{3,2,1,0:T(8,128)(2,1)}, u32[]{:S(2)}) copy-start(bf16[1,1,1536,512]{3,2,1,0:T(8,128)(2,1)} %param.17) | copy-start | bytes 4718596
  78.8 17.9 %all-to-all-start.3 = ((bf16[4,192,256]{2,1,0:T(8,128)(2,1)}), bf16[4,192,256]{2,1,0:T(8,128)(2,1)S(1)}, u32[]{:S(2)}, u32[]{:S(2)}) async-start(bf16[4,192,256]{2,1,0:T(8,128)(2,1)} %broadcast_in_dim.28), calls=%async_computation.3 | async-start | bytes 786432 | tf_op jit(solution)/shard_map/all_to_all | solution.py:149
  87.2 9.4 %collective-permute-start.4 = (bf16[192,256]{1,0:T(8,128)(2,1)S(1)}, bf16[192,256]{1,0:T(8,128)(2,1)S(1)}, u32[]{:S(2)}, u32[]{:S(2)}) collective-permute-start(bf16[192,256]{1,0:T(8,128)(2,1)S(1)} %shard_map.95), channel_id=1, source_target_pairs={{0,4},{1,5},{2,6},{3,7},{4,0},{5,1},{6,2},{7,3},{8,12},{9,13},{10,... | collective-permute-start | bytes 294920 | tf_op jit(solution)/shard_map/ppermute | solution.py:153
  97.4 15.5 %all-to-all-start.4 = ((bf16[4,192,256]{2,1,0:T(8,128)(2,1)}), bf16[4,192,256]{2,1,0:T(8,128)(2,1)S(1)}, u32[]{:S(2)}, u32[]{:S(2)}) async-start(bf16[4,192,256]{2,1,0:T(8,128)(2,1)} %broadcast_in_dim.29), calls=%async_computation.4 | async-start | bytes 786432 | tf_op jit(solution)/shard_map/all_to_all | solution.py:149
  112.9 6.5 %copy-start.6 = (bf16[128,512]{1,0:T(8,128)(2,1)S(1)}, bf16[128,512]{1,0:T(8,128)(2,1)}, u32[]{:S(2)}) copy-start(bf16[128,512]{1,0:T(8,128)(2,1)} %copy-done.5) | copy-start | bytes 393220
  112.9 6.5 %copy-start.8 = (bf16[128,512]{1,0:T(8,128)(2,1)S(1)}, bf16[128,512]{1,0:T(8,128)(2,1)}, u32[]{:S(2)}) copy-start(bf16[128,512]{1,0:T(8,128)(2,1)} %copy-done.7) | copy-start | bytes 393220
  112.9 6.6 %copy-start.10 = (bf16[128,512]{1,0:T(8,128)(2,1)S(1)}, bf16[128,512]{1,0:T(8,128)(2,1)}, u32[]{:S(2)}) copy-start(bf16[128,512]{1,0:T(8,128)(2,1)} %copy-done.9) | copy-start | bytes 393220
  112.9 13.8 %copy-start.4 = (bf16[1,128,512]{2,1,0:T(8,128)(2,1)S(1)}, bf16[1,128,512]{2,1,0:T(8,128)(2,1)}, u32[]{:S(2)}) copy-start(bf16[1,128,512]{2,1,0:T(8,128)(2,1)} %param.9) | copy-start | bytes 393220
  114.4 12.4 %all-to-all-start.5 = ((bf16[16,16,512]{2,1,0:T(8,128)(2,1)}), bf16[16,16,512]{2,1,0:T(8,128)(2,1)S(1)}, u32[]{:S(2)}, u32[]{:S(2)}) async-start(bf16[16,16,512]{2,1,0:T(8,128)(2,1)} %bitcast.15), calls=%async_computation.5 | async-start | bytes 524288 | tf_op jit(solution)/shard_map/all_to_all | solution.py:158
  119.5 0.9 copy-start.12
  120.4 0.9 copy-start.13
  127.0 19.6 %collective-permute-start.5 = (bf16[128,512]{1,0:T(8,128)(2,1)S(1)}, bf16[128,512]{1,0:T(8,128)(2,1)S(1)}, u32[]{:S(2)}, u32[]{:S(2)}) collective-permute-start(bf16[128,512]{1,0:T(8,128)(2,1)S(1)} %shard_map.97), channel_id=1, source_target_pairs={{0,128},{128,256},{256,384},{384,0},{1,129},{129,257},{257,385},{3... | collective-permute-start | bytes 393224 | tf_op jit(solution)/shard_map/ppermute | solution.py:225

commit v3 on v2

v3 whole, which is shorter than its diff:
```python
import jax
import jax.numpy as jnp
from jax import lax
from jax.experimental import pallas as pl
from jax.experimental.pallas import tpu as pltpu
from jax.sharding import PartitionSpec as P

norm_eps = 1e-06
BF = jnp.bfloat16
F32 = jnp.float32
EXPERTS = 16
SLOTS = 16
VM = pl.BlockSpec(memory_space=pltpu.VMEM)
SM = pl.BlockSpec(memory_space=pltpu.SMEM)
HB = pl.BlockSpec(memory_space=pltpu.HBM)
SIZES = (48, 64, 80, 96, 128)
FOURS = [[0, 1, 2, 3], [4, 5, 6, 7]]


def dot(a, b, da, db):
    return lax.dot_general(a, b, (((da,), (db,)), ((), ())), preferred_element_type=F32)


def call(body, shape, specs, args, scratch=(), out_specs=None, flops=0, moved=0, limit=24):
    return pl.pallas_call(
        body,
        scratch_shapes=list(scratch),
        out_shape=shape,
        in_specs=specs,
        out_specs=out_specs or jax.tree.map(lambda _: VM, shape),
        compiler_params=pltpu.CompilerParams(vmem_limit_bytes=limit * 2**20),
        cost_estimate=pl.CostEstimate(flops=flops, bytes_accessed=moved, transcendentals=0),
    )(*args)


def eye(n):
    return (lax.broadcasted_iota(jnp.int32, (n, n), 0) == lax.broadcasted_iota(jnp.int32, (n, n), 1)).astype(BF)


def route_body(ids_ref, length_ref, quota_ref, tokens_ref, rows_ref, match_ref, held_ref, chosen_ref, which_ref):
    n = ids_ref.shape[1]
    expert = lax.broadcasted_iota(jnp.int32, (EXPERTS, n), 0)
    chosen = jnp.zeros((EXPERTS, n), F32)
    for j in range(ids_ref.shape[0]):
        chosen = chosen + (ids_ref[j : j + 1, :] == expert).astype(F32)
    at = lax.broadcasted_iota(jnp.int32, (1, n), 1)
    picked = chosen * (at < length_ref[...]).astype(F32)
    down = lax.broadcasted_iota(jnp.int32, (n, n), 0)
    before = (down < lax.broadcasted_iota(jnp.int32, (n, n), 1)).astype(BF)
    order = dot(picked.astype(BF), before, 1, 0)
    quota = jnp.sum(eye(EXPERTS).astype(F32) * quota_ref[...].astype(F32), axis=1, keepdims=True)
    kept = picked * (order < quota).astype(F32)
    slot = lax.broadcasted_iota(jnp.int32, (SLOTS, n), 0).astype(F32)
    hits = [(order[e : e + 1, :] == slot).astype(F32) * kept[e : e + 1, :] for e in range(EXPERTS)]
    match = dot(eye(n), jnp.concatenate(hits, axis=0).astype(BF), 1, 1).astype(BF)
    used = jnp.max(kept, axis=0, keepdims=True)
    place = dot(jnp.broadcast_to(used, (8, n)).astype(BF), before, 1, 0)[0:1, :]
    compact = ((place == down.astype(F32)).astype(F32) * used).astype(BF)
    rows_ref[...] = dot(compact, tokens_ref[...], 1, 0).astype(BF)
    match_ref[...] = match
    held_ref[...] = dot(compact, match, 1, 0).astype(BF)
    chosen_ref[...] = dot(compact, chosen.astype(BF), 1, 1)
    count = jnp.sum(used).astype(jnp.int32)
    which_ref[0] = sum((count > size).astype(jnp.int32) for size in SIZES[:-1])


def blocks_of(rank, width):
    order = [rank // 4 * 4 + k for k in range(4)] + [rank ^ 4 ^ k for k in range(4)]
    return [pl.ds(pl.multiple_of(r * width, width), width) for r in order]


def pick(views, blocks, held, gain_ref, router_ref, out_ref):
    n, width = views[0].shape
    squares = jnp.zeros((n, 1), F32)
    logits = jnp.zeros((n, EXPERTS), F32)
    for k, (view, cols) in enumerate(zip(views, blocks)):
        raw = view[...]
        out_ref[:, k * width : (k + 1) * width] = dot(held, raw, 0, 0).astype(BF)
        v = raw.astype(F32)
        squares = squares + jnp.sum(v * v, axis=1, keepdims=True)
        scaled = (v * gain_ref[:, cols].astype(F32)).astype(BF)
        logits = logits + dot(scaled, router_ref[:, cols], 1, 1)
    return squares, logits


def pick_first_body(own_ref, far_ref, held_ref, gain_ref, router_ref, out_ref, kept_far_ref, squares_ref, logits_ref):
    n, width = far_ref.shape
    blocks = blocks_of(lax.axis_index("tensor"), width)[:5]
    views = [own_ref.at[k] for k in range(4)] + [far_ref]
    squares, logits = pick(views, blocks, held_ref[0:n, :], gain_ref, router_ref, out_ref)
    kept_far_ref[0:n, :] = far_ref[...]
    squares_ref[0:n, :] = jnp.broadcast_to(squares, (n, squares_ref.shape[1]))
    logits_ref[0:n, :] = logits


def pick_second_body(
    a_ref, b_ref, c_ref, held_ref, gain_ref, router_ref, squares_ref, logits_ref, match_ref, chosen_ref,
    out_ref, high_ref, low_ref,
):
    n, width = a_ref.shape
    blocks = blocks_of(lax.axis_index("tensor"), width)[5:]
    held = held_ref[0:n, :]
    squares, logits = pick([a_ref, b_ref, c_ref], blocks, held, gain_ref, router_ref, out_ref)
    inverse = lax.rsqrt((squares + squares_ref[0:n, 0:1]) / (8 * width) + norm_eps)
    chosen = chosen_ref[0:n, :]
    powered = jnp.exp((logits + logits_ref[0:n, :]) * inverse) * chosen
    weight = powered / (jnp.sum(powered, axis=1, keepdims=True) + (1.0 - jnp.max(chosen, axis=1, keepdims=True)))
    slots = held.shape[1]
    owner = (
        lax.broadcasted_iota(jnp.int32, (EXPERTS, slots), 1) // SLOTS
        == lax.broadcasted_iota(jnp.int32, (EXPERTS, slots), 0)
    ).astype(BF)
    spread = jnp.zeros((n, slots), F32)
    for _ in range(3):
        piece = weight.astype(BF)
        spread = spread + dot(piece, owner, 1, 0)
        weight = weight - piece.astype(F32)
    row = jnp.sum(spread * held.astype(F32), axis=0, keepdims=True)
    value = match_ref[...].astype(F32) * row
    high = value.astype(BF)
    high_ref[...] = high
    low_ref[...] = (value - high.astype(F32)).astype(BF)


def partial_products(rows_ref, gain_ref, blocks, weights):
    rows = rows_ref.shape[0]
    squares = jnp.zeros((rows, 1), F32)
    gate = up = 0.0
    for k, cols in enumerate(blocks):
        width = rows_ref.shape[1] // len(blocks)
        v = rows_ref[:, k * width : (k + 1) * width].astype(F32)
        squares = squares + jnp.sum(v * v, axis=1, keepdims=True)
        scaled = (v * gain_ref[:, cols].astype(F32)).astype(BF)
        gate_part, up_part = weights(k)
        gate = gate + dot(gate_part, scaled, 1, 1)
        up = up + dot(up_part, scaled, 1, 1)
    return gate, up, jnp.broadcast_to(squares, (rows, 128)).T[0:1, :]


def expand_first_body(
    rows_ref, gain_ref, gate_ref, up_ref,
    parts_ref, gate_rest, up_rest, gate_buf, up_buf, sems,
):
    rank = lax.axis_index("tensor")
    now, _, width = gate_buf.shape
    blocks = blocks_of(rank, width)
    copies = []
    for k, cols in enumerate(blocks):
        targets = (gate_buf, up_buf) if k < now else (gate_rest, up_rest)
        at = k if k < now else k - now
        pair = [
            pltpu.make_async_copy(source.at[:, cols], target.at[at], sems.at[i, k])
            for i, (source, target) in enumerate(zip((gate_ref, up_ref), targets))
        ]
        for copy in pair:
            copy.start()
        copies.append(pair)

    def weights(k):
        for copy in copies[k]:
            copy.wait()
        return gate_buf[k], up_buf[k]

    gate, up, squares = partial_products(rows_ref, gain_ref, blocks[:now], weights)
    hid, rows = gate.shape
    parts_ref[0:hid, :] = gate
    parts_ref[hid : 2 * hid, :] = up
    parts_ref[2 * hid :, :] = jnp.broadcast_to(squares, (8, rows))
    for pair in copies[now:]:
        for copy in pair:
            copy.wait()


def expand_second_body(rows_ref, parts_ref, gain_ref, gate_rest, up_rest, out_ref):
    rank = lax.axis_index("tensor")
    parts, hid, width = gate_rest.shape
    blocks = blocks_of(rank, width)[8 - parts :]
    gate, up, squares = partial_products(
        rows_ref, gain_ref, blocks, lambda k: (gate_rest[k], up_rest[k])
    )
    inverse = lax.rsqrt((squares + parts_ref[2 * hid : 2 * hid + 1, :]) / (8 * width) + norm_eps)
    gate = (gate + parts_ref[0:hid, :]) * inverse
    up = (up + parts_ref[hid : 2 * hid, :]) * inverse
    out_ref[...] = (gate / (1.0 + jnp.exp(-gate)) * up).astype(BF)


def contract_body(half_ref, first_ref, second_ref, down_ref, out_ref):
    parts, hid, _ = first_ref.shape
    total = jnp.zeros(out_ref.shape, F32)
    for ref, half in ((first_ref, half_ref[0]), (second_ref, 1 - half_ref[0])):
        for k in range(parts):
            rows = pl.ds(pl.multiple_of((half * parts + k) * hid, hid), hid)
            total = total + dot(ref[k], down_ref[rows, :], 0, 0)
    out_ref[...] = total.astype(BF)


def mix_body(high_ref, low_ref, reply_ref, tokens_ref, out_ref):
    mixed = dot(high_ref[...], reply_ref[...], 1, 0) + dot(low_ref[...], reply_ref[...], 1, 0)
    out_ref[...] = (tokens_ref[...].astype(F32) + mixed).astype(BF)


def to_fours(shard):
    copies = jnp.broadcast_to(shard[None], (4,) + shard.shape)
    return lax.all_to_all(copies, "tensor", 0, 0, axis_index_groups=FOURS)


def along(shard, by):
    return lax.ppermute(shard, "tensor", [(i, i ^ by) for i in range(8)])


def over_dp(rows):
    n, width = rows.shape
    return lax.all_to_all(rows.reshape(EXPERTS, n // EXPERTS, width), "dp", 0, 0).reshape(n, width)


def on_device(
    hidden_state_matrix,
    specialist_choice_ids,
    seat_quota_per_specialist,
    candidate_active_extent,
    normalizer_gain_vector,
    dispatcher_matrix,
    gating_matrices,
    expanding_matrices,
    contracting_matrices,
):
    tokens = hidden_state_matrix[0]
    ids = specialist_choice_ids[0].T
    gain = normalizer_gain_vector
    router = dispatcher_matrix[0]
    w_gate = gating_matrices[0, 0]
    w_up = expanding_matrices[0, 0]
    w_down = contracting_matrices[0, 0]
    n, width = tokens.shape
    slots = EXPERTS * SLOTS
    hid = w_gate.shape[0]
    half = (lax.axis_index("tensor") // 4).astype(jnp.int32)[None]

    table = jax.ShapeDtypeStruct((n, slots), BF)
    rows, match, held, chosen, which = call(
        route_body,
        (
            jax.ShapeDtypeStruct((n, width), BF),
            table,
            table,
            jax.ShapeDtypeStruct((n, EXPERTS), F32),
            jax.ShapeDtypeStruct((1,), jnp.int32),
        ),
        [VM] * 4,
        (ids, candidate_active_extent, seat_quota_per_specialist, tokens),
        out_specs=(VM, VM, VM, VM, SM),
        limit=16,
    )

    def first_part(size):
        def run(rows, held, gain, router):
            mine = rows[:size]
            far = along(mine, 4)
            return call(
                pick_first_body,
                (
                    jax.ShapeDtypeStruct((slots, 5 * width), BF),
                    jax.ShapeDtypeStruct((n, width), BF),
                    jax.ShapeDtypeStruct((n, 128), F32),
                    jax.ShapeDtypeStruct((n, EXPERTS), F32),
                ),
                [VM] * 5,
                (to_fours(mine), far, held, gain, router),
                limit=16,
            )

        return run

    def second_part(size):
        def run(far, held, gain, router, squares, logits, match, chosen):
            rest = [along(far[:size], by) for by in (1, 2, 3)]
            return call(
                pick_second_body,
                (jax.ShapeDtypeStruct((slots, 3 * width), BF), table, table),
                [VM] * 10,
                (*rest, held, gain, router, squares, logits, match, chosen),
                limit=16,
            )

        return run

    first, far, squares, logits = lax.switch(
        which[0], [first_part(size) for size in SIZES], rows, held, gain, router
    )
    first_rows = over_dp(first)
    second, high, low = lax.switch(
        which[0], [second_part(size) for size in SIZES], far, held, gain, router, squares, logits, match, chosen
    )
    first_rows, second = lax.optimization_barrier((first_rows, second))
    second_rows = over_dp(second)
    parts = jax.ShapeDtypeStruct((2 * hid + 8, slots), F32)
    weights = jax.ShapeDtypeStruct((3, hid, width), BF)
    parts, gate_rest, up_rest = call(
        expand_first_body,
        (parts, weights, weights),
        [VM] * 2 + [HB] * 2,
        (first_rows, gain, w_gate, w_up),
        [pltpu.VMEM((5, hid, width), BF)] * 2 + [pltpu.SemaphoreType.DMA((2, 8))],
        limit=16,
    )
    hidden = call(
        expand_second_body,
        jax.ShapeDtypeStruct((hid, slots), BF),
        [VM] * 5,
        (second_rows, parts, gain, gate_rest, up_rest),
        limit=16,
    )
    hidden_other = along(hidden, 4)
    hidden_first = to_fours(hidden)
    hidden_second = to_fours(hidden_other)
    reply = call(
        contract_body,
        jax.ShapeDtypeStruct((slots, width), BF),
        [SM] + [VM] * 3,
        (half, hidden_first, hidden_second, w_down),
    )
    returned = over_dp(reply)
    layer_out = call(
        mix_body, jax.ShapeDtypeStruct((n, width), BF), [VM] * 4, (high, low, returned, tokens)
    )
    count = lax.axis_size("section")
    handed = lax.ppermute(layer_out, "section", [(i, (i + 1) % count) for i in range(count)])
    return handed[None]


def solution(mesh):
    return jax.shard_map(
        on_device,
        mesh=mesh,
        in_specs=(
            P("section", "dp", "tensor"),
            P("section", "dp", None),
            P("section", None),
            P("section", "dp"),
            P("section", None),
            P("section", None, None),
            P("section", "dp", "tensor", None),
            P("section", "dp", "tensor", None),
            P("section", "dp", None, "tensor"),
        ),
        out_specs=P("section", "dp", "tensor"),
        check_vma=False,
    )
```

time: 148 us -> 142 us (0.959)
  starting transfers between devices: 83.2 us -> 77.7 us
  waiting for transfers between devices: 30.2 us -> 25.7 us
    all_to_all x2, starting transfers between devices: 19.1 us -> 13.4 us  [over_dp(): lax.all_to_all(rows.reshape(EXPERTS, n // EXPERTS, width), 'dp', 0, 0)]
    ppermute x5, starting transfers between devices: 26.6 us -> 30.8 us  [along(): return lax.ppermute(shard, 'tensor', [(i, i ^ by) for i in range(8)])]
    ppermute x5, waiting for transfers between devices: 12 us -> 8.16 us  [along(): return lax.ppermute(shard, 'tensor', [(i, i ^ by) for i in range(8)])]
    unnamed x35 -> x23, local copies, waits for them, and re-layouts: 5.2 us -> 7.49 us
    all_to_all x3, starting transfers between devices: 22.6 us -> 20.6 us  [to_fours(): return lax.all_to_all(copies, 'tensor', 0, 0, axis_index_groups=FOURS)]
    ppermute x1, starting transfers between devices: 14.9 us -> 13 us  [on_device(): lax.ppermute(layer_out, 'section', [(i, (i + 1) % count) for i in range(c...]
  transfers between devices with their start and end apart: 11 -> 11, of which waited for: 7 -> 7; matrix products, arithmetic and copies ran while one was open for 0% -> 0% of each run, Pallas kernels for 1% -> 2%
where the time goes in v3:
time: 142 us; the launch traced here: 141 us
  starting transfers between devices  77.7 us (55%)
  waiting for transfers between devices  25.7 us (18%)
  blocking collectives  17.8 us (13%)
  local copies, waits for them, and re-layouts  9.82 us (7%)
  Pallas kernels  8.61 us (6%)
  between operations  1.43 us (1%)
    ppermute x5, starting transfers between devices, along(): return lax.ppermute(shard, 'tensor', [(i, i ^ by) for i in range(8)])  30.8 us
    all_to_all x3, starting transfers between devices, to_fours(): return lax.all_to_all(copies, 'tensor', 0, 0, axis_index_groups=FOURS)  20.6 us
    all_to_all x1, blocking collectives, over_dp(): lax.all_to_all(rows.reshape(EXPERTS, n // EXPERTS, width), 'dp', 0, 0)  17.8 us
    all_to_all x2, starting transfers between devices, over_dp(): lax.all_to_all(rows.reshape(EXPERTS, n // EXPERTS, width), 'dp', 0, 0)  13.4 us
    ppermute x1, starting transfers between devices, on_device(): lax.ppermute(layer_out, 'section', [(i, (i + 1) % count) for i in range(c...  13 us
    pallas_call x7, Pallas kernels, call(): pl.pallas_call(body, scratch_shapes=list(scratch), out_shape=shape, in_sp...  8.61 us
    ppermute x5, waiting for transfers between devices, along(): return lax.ppermute(shard, 'tensor', [(i, i ^ by) for i in range(8)])  8.16 us
    all_to_all x3, waiting for transfers between devices, to_fours(): return lax.all_to_all(copies, 'tensor', 0, 0, axis_index_groups=FOURS)  7.74 us
  transfers between devices with their start and end apart: 11, of which 7 were waited for; matrix products, arithmetic and copies ran while one was open for 0% of the time, Pallas kernels for 2%

profile of v3, /device:TPU:1, one launch (start us, length us, event | category | flops | bytes accessed | tf_op | source)
XLA Modules:
  0.0 141.2 jit_solution(6155502916810536707)
XLA Ops:
  0.7 0.9 copy-done.3
  2.9 0.8 shard_map.91
  4.4 20.4 %conditional.2 = ((bf16[256,2560]{1,0:T(8,128)(2,1)}, bf16[128,512]{1,0:T(8,128)(2,1)S(1)}, f32[128,128]{1,0:T(8,128)S(1)}, f32[128,16]{1,0:T(8,128)S(1)})) conditional(s32[]{:T(128)} %bitcast.3, (bf16[128,512]{1,0:T(8,128)(2,1)S(1)}, bf16[128,256]{1,0:T(8,128)(2,1)S(1)}, bf16[1,4096]{1,0:T(2,128)(2,1)}, ...), branch_computations={%region_0.1_spmd, %region_1.2_spmd, %region_2.3_spmd, %region_3.4_... | conditional | bytes 3309704 | solution.py:287
  5.2 6.4 %all-to-all-start.1 = ((bf16[4,64,512]{2,1,0:T(8,128)(2,1)}), bf16[4,64,512]{2,1,0:T(8,128)(2,1)S(1)}, u32[]{:S(2)}, u32[]{:S(2)}) async-start(bf16[4,64,512]{2,1,0:T(8,128)(2,1)} %broadcast_in_dim.18), calls=%async_computation.1 | async-start | bytes 524288 | tf_op jit(solution)/shard_map/cond/branch_1_fun/all_to_all | solution.py:204
  11.6 8.8 %collective-permute-start.1 = (bf16[64,512]{1,0:T(8,128)(2,1)S(1)}, bf16[64,512]{1,0:T(8,128)(2,1)S(1)}, u32[]{:S(2)}, u32[]{:S(2)}) collective-permute-start(bf16[64,512]{1,0:T(8,128)(2,1)S(1)} %slice.16), channel_id=1, source_target_pairs={{0,4},{1,5},{2,6},{3,7},{4,0},{5,1},{6,2},{7,3},{8,12},{9,13},{10,... | collective-permute-start | bytes 196616 | tf_op jit(solution)/shard_map/cond/branch_1_fun/ppermute | solution.py:208
  20.4 1.7 %collective-permute-done.1.far_ref = bf16[64,512]{1,0:T(8,128)(2,1)S(1)} collective-permute-done((bf16[64,512]{1,0:T(8,128)(2,1)S(1)}, bf16[64,512]{1,0:T(8,128)(2,1)S(1)}, u32[]{:S(2)}, u32[]{:S(2)}) %collective-permute-start.1) | collective-permute-done | bytes 65568 | tf_op jit(solution)/shard_map/cond/branch_1_fun/ppermute | solution.py:208
  22.2 2.6 %branch_1_fun.2 = (bf16[256,2560]{1,0:T(8,128)(2,1)}, bf16[128,512]{1,0:T(8,128)(2,1)S(1)}, f32[128,128]{1,0:T(8,128)S(1)}, f32[128,16]{1,0:T(8,128)S(1)}) custom-call(bf16[4,64,512]{2,1,0:T(8,128)(2,1)S(1)} %all-to-all-done.1.own_ref, bf16[64,512]{1,0:T(8,128)(2,1)S(1)} %collective-permute-done.1.far_ref, bf16[128,256]{1,0:T(8,128)(2,1)S(1)} %get-tuple-element.130.held_ref, ...), custom_call_target="tpu_custom_call" | custom-call | tf_op jit(solution)/shard_map/cond/branch_1_fun/pallas_call | solution.py:25
  24.8 6.8 %all-to-all-start.5 = ((bf16[16,16,2560]{2,1,0:T(8,128)(2,1)}), bf16[16,16,2560]{2,1,0:T(8,128)(2,1)S(1)}, u32[]{:S(2)}, u32[]{:S(2)}) async-start(bf16[16,16,2560]{2,1,0:T(8,128)(2,1)} %bitcast.6), calls=%async_computation.5 | async-start | bytes 2621440 | tf_op jit(solution)/shard_map/all_to_all | solution.py:213
  31.6 19.1 %conditional.3 = ((bf16[256,1536]{1,0:T(8,128)(2,1)}, bf16[128,256]{1,0:T(8,128)(2,1)S(1)}, bf16[128,256]{1,0:T(8,128)(2,1)S(1)})) conditional(s32[]{:T(128)} %bitcast.3, (bf16[128,512]{1,0:T(8,128)(2,1)S(1)}, bf16[128,256]{1,0:T(8,128)(2,1)S(1)}, bf16[1,4096]{1,0:T(2,128)(2,1)S(1)}, bf16[16,4096]{1,0:T(8,128)(2,1)S(1)}, ...), branch_computations={%region_5.6_spmd, %region_6.7_spmd, %region_7.8_spmd, %region_8.9_... | conditional | bytes 1572992 | solution.py:291
  31.7 9.1 %collective-permute-start.10 = (bf16[64,512]{1,0:T(8,128)(2,1)S(1)}, bf16[64,512]{1,0:T(8,128)(2,1)S(1)}, u32[]{:S(2)}, u32[]{:S(2)}) collective-permute-start(bf16[64,512]{1,0:T(8,128)(2,1)S(1)} %slice.26), channel_id=1, source_target_pairs={{0,3},{1,2},{2,1},{3,0},{4,7},{5,6},{6,5},{7,4},{8,11},{9,10},{10,... | collective-permute-start | bytes 196616 | tf_op jit(solution)/shard_map/cond/branch_1_fun/ppermute | solution.py:208
  40.8 2.4 %collective-permute-start.8 = (bf16[64,512]{1,0:T(8,128)(2,1)S(1)}, bf16[64,512]{1,0:T(8,128)(2,1)S(1)}, u32[]{:S(2)}, u32[]{:S(2)}) collective-permute-start(bf16[64,512]{1,0:T(8,128)(2,1)S(1)} %slice.26), channel_id=1, source_target_pairs={{0,1},{1,0},{2,3},{3,2},{4,5},{5,4},{6,7},{7,6},{8,9},{9,8},{10,11... | collective-permute-start | bytes 196616 | tf_op jit(solution)/shard_map/cond/branch_1_fun/ppermute | solution.py:208
  43.2 1.9 %collective-permute-start.9 = (bf16[64,512]{1,0:T(8,128)(2,1)S(1)}, bf16[64,512]{1,0:T(8,128)(2,1)S(1)}, u32[]{:S(2)}, u32[]{:S(2)}) collective-permute-start(bf16[64,512]{1,0:T(8,128)(2,1)S(1)} %slice.26), channel_id=1, source_target_pairs={{0,2},{1,3},{2,0},{3,1},{4,6},{5,7},{6,4},{7,5},{8,10},{9,11},{10,... | collective-permute-start | bytes 196616 | tf_op jit(solution)/shard_map/cond/branch_1_fun/ppermute | solution.py:208
  45.1 1.0 collective-permute-done.8.a_ref
  46.1 3.3 %collective-permute-done.9.b_ref = bf16[64,512]{1,0:T(8,128)(2,1)S(1)} collective-permute-done((bf16[64,512]{1,0:T(8,128)(2,1)S(1)}, bf16[64,512]{1,0:T(8,128)(2,1)S(1)}, u32[]{:S(2)}, u32[]{:S(2)}) %collective-permute-start.9) | collective-permute-done | bytes 65568 | tf_op jit(solution)/shard_map/cond/branch_1_fun/ppermute | solution.py:208
  49.4 1.4 branch_1_fun.3
  50.7 6.6 %all-to-all-start.6 = ((bf16[16,16,1536]{2,1,0:T(8,128)(2,1)}), bf16[16,16,1536]{2,1,0:T(8,128)(2,1)S(1)}, u32[]{:S(2)}, u32[]{:S(2)}) async-start(bf16[16,16,1536]{2,1,0:T(8,128)(2,1)} %bitcast.8), calls=%async_computation.6 | async-start | bytes 1572864 | tf_op jit(solution)/shard_map/all_to_all | solution.py:213
  57.3 1.4 copy-done
  58.7 1.4 copy-done.1
  60.1 2.1 %shard_map.92 = (f32[392,256]{1,0:T(8,128)S(1)}, bf16[3,192,512]{2,1,0:T(8,128)(2,1)S(1)}, bf16[3,192,512]{2,1,0:T(8,128)(2,1)S(1)}) custom-call(bf16[256,2560]{1,0:T(8,128)(2,1)S(1)} %bitcast.17, bf16[1,4096]{1,0:T(2,128)(2,1)S(1)} %copy-done.13, bf16[192,4096]{1,0:T(8,128)(2,1)S(1)} %bitcast.19, bf16[192,4096]{1,0:T(8,128)(2,1)S(1)} %bitcast.20), custom_call_target="tpu_custom_call" | custom-call | tf_op jit(solution)/shard_map/pallas_call | solution.py:25
  62.2 0.8 copy-done.5
  63.0 4.8 %all-to-all-done.6 = bf16[16,16,1536]{2,1,0:T(8,128)(2,1)S(1)} async-done(((bf16[16,16,1536]{2,1,0:T(8,128)(2,1)}), bf16[16,16,1536]{2,1,0:T(8,128)(2,1)S(1)}, u32[]{:S(2)}, u32[]{:S(2)}) %all-to-all-start.6) | async-done | bytes 786464 | tf_op jit(solution)/shard_map/all_to_all | solution.py:213
  67.8 1.0 copy-done.6
  69.5 0.8 broadcast_in_dim.35
  70.3 5.3 %all-to-all-start.7 = ((bf16[4,192,256]{2,1,0:T(8,128)(2,1)}), bf16[4,192,256]{2,1,0:T(8,128)(2,1)S(1)}, u32[]{:S(2)}, u32[]{:S(2)}) async-start(bf16[4,192,256]{2,1,0:T(8,128)(2,1)} %broadcast_in_dim.35), calls=%async_computation.7 | async-start | bytes 786432 | tf_op jit(solution)/shard_map/all_to_all | solution.py:204
  75.6 8.6 %collective-permute-start.20 = (bf16[192,256]{1,0:T(8,128)(2,1)S(1)}, bf16[192,256]{1,0:T(8,128)(2,1)S(1)}, u32[]{:S(2)}, u32[]{:S(2)}) collective-permute-start(bf16[192,256]{1,0:T(8,128)(2,1)S(1)} %shard_map.93), channel_id=1, source_target_pairs={{0,4},{1,5},{2,6},{3,7},{4,0},{5,1},{6,2},{7,3},{8,12},{9,13},{10,... | collective-permute-start | bytes 294920 | tf_op jit(solution)/shard_map/ppermute | solution.py:208
  84.2 2.1 %collective-permute-done.20 = bf16[192,256]{1,0:T(8,128)(2,1)S(1)} collective-permute-done((bf16[192,256]{1,0:T(8,128)(2,1)S(1)}, bf16[192,256]{1,0:T(8,128)(2,1)S(1)}, u32[]{:S(2)}, u32[]{:S(2)}) %collective-permute-start.20) | collective-permute-done | bytes 98336 | tf_op jit(solution)/shard_map/ppermute | solution.py:208
  86.4 0.8 broadcast_in_dim.36
  87.2 8.8 %all-to-all-start.8 = ((bf16[4,192,256]{2,1,0:T(8,128)(2,1)}), bf16[4,192,256]{2,1,0:T(8,128)(2,1)S(1)}, u32[]{:S(2)}, u32[]{:S(2)}) async-start(bf16[4,192,256]{2,1,0:T(8,128)(2,1)} %broadcast_in_dim.36), calls=%async_computation.8 | async-start | bytes 786432 | tf_op jit(solution)/shard_map/all_to_all | solution.py:204
  96.0 7.7 %all-to-all-done.8.second_ref = bf16[4,192,256]{2,1,0:T(8,128)(2,1)S(1)} async-done(((bf16[4,192,256]{2,1,0:T(8,128)(2,1)}), bf16[4,192,256]{2,1,0:T(8,128)(2,1)S(1)}, u32[]{:S(2)}, u32[]{:S(2)}) %all-to-all-start.8) | async-done | bytes 393248 | tf_op jit(solution)/shard_map/all_to_all | solution.py:204
  104.5 17.8 %all_to_all.45 = bf16[16,16,512]{2,1,0:T(8,128)(2,1)S(1)} all-to-all(bf16[16,16,512]{2,1,0:T(8,128)(2,1)S(1)} %bitcast.23), channel_id=1, replica_groups=mesh['section'=4,'dp'=16,'tensor'=8] {'dp'}, dimensions={0} | all-to-all | bytes 524288 | tf_op jit(solution)/shard_map/all_to_all | solution.py:213
  122.5 13.0 %collective-permute-start.21 = (bf16[128,512]{1,0:T(8,128)(2,1)S(1)}, bf16[128,512]{1,0:T(8,128)(2,1)S(1)}, u32[]{:S(2)}, u32[]{:S(2)}) collective-permute-start(bf16[128,512]{1,0:T(8,128)(2,1)S(1)} %shard_map.95), channel_id=1, source_target_pairs={{0,128},{128,256},{256,384},{384,0},{1,129},{129,257},{257,385},{3... | collective-permute-start | bytes 393224 | tf_op jit(solution)/shard_map/ppermute | solution.py:327
  135.5 5.0 %collective-permute-done.21 = bf16[128,512]{1,0:T(8,128)(2,1)S(1)} collective-permute-done((bf16[128,512]{1,0:T(8,128)(2,1)S(1)}, bf16[128,512]{1,0:T(8,128)(2,1)S(1)}, u32[]{:S(2)}, u32[]{:S(2)}) %collective-permute-start.21) | collective-permute-done | bytes 131104 | tf_op jit(solution)/shard_map/ppermute | solution.py:327
  (28 shorter events, 4.5 us)
Async XLA Ops:
  0.7 0.9 copy-start.3
  1.6 0.7 copy-start.7
  2.2 0.7 copy-start.8
  5.2 17.0 %all-to-all-start.1 = ((bf16[4,64,512]{2,1,0:T(8,128)(2,1)}), bf16[4,64,512]{2,1,0:T(8,128)(2,1)S(1)}, u32[]{:S(2)}, u32[]{:S(2)}) async-start(bf16[4,64,512]{2,1,0:T(8,128)(2,1)} %broadcast_in_dim.18), calls=%async_computation.1 | async-start | bytes 524288 | tf_op jit(solution)/shard_map/cond/branch_1_fun/all_to_all | solution.py:204
  11.6 10.6 %collective-permute-start.1 = (bf16[64,512]{1,0:T(8,128)(2,1)S(1)}, bf16[64,512]{1,0:T(8,128)(2,1)S(1)}, u32[]{:S(2)}, u32[]{:S(2)}) collective-permute-start(bf16[64,512]{1,0:T(8,128)(2,1)S(1)} %slice.16), channel_id=1, source_target_pairs={{0,4},{1,5},{2,6},{3,7},{4,0},{5,1},{6,2},{7,3},{8,12},{9,13},{10,... | collective-permute-start | bytes 196616 | tf_op jit(solution)/shard_map/cond/branch_1_fun/ppermute | solution.py:208
  24.8 6.8 %copy-start.9 = (bf16[1,16,4096]{2,1,0:T(8,128)(2,1)S(1)}, bf16[1,16,4096]{2,1,0:T(8,128)(2,1)}, u32[]{:S(2)}) copy-start(bf16[1,16,4096]{2,1,0:T(8,128)(2,1)} %param.24) | copy-start | bytes 393220
  24.8 6.8 %copy-start.13 = (bf16[1,4096]{1,0:T(2,128)(2,1)S(1)}, bf16[1,4096]{1,0:T(2,128)(2,1)}, u32[]{:S(2)}) copy-start(bf16[1,4096]{1,0:T(2,128)(2,1)} %gain_ref.3) | copy-start | bytes 24580
  24.8 25.9 %all-to-all-start.5 = ((bf16[16,16,2560]{2,1,0:T(8,128)(2,1)}), bf16[16,16,2560]{2,1,0:T(8,128)(2,1)S(1)}, u32[]{:S(2)}, u32[]{:S(2)}) async-start(bf16[16,16,2560]{2,1,0:T(8,128)(2,1)} %bitcast.6), calls=%async_computation.5 | async-start | bytes 2621440 | tf_op jit(solution)/shard_map/all_to_all | solution.py:213
  31.7 13.4 %collective-permute-start.10 = (bf16[64,512]{1,0:T(8,128)(2,1)S(1)}, bf16[64,512]{1,0:T(8,128)(2,1)S(1)}, u32[]{:S(2)}, u32[]{:S(2)}) collective-permute-start(bf16[64,512]{1,0:T(8,128)(2,1)S(1)} %slice.26), channel_id=1, source_target_pairs={{0,3},{1,2},{2,1},{3,0},{4,7},{5,6},{6,5},{7,4},{8,11},{9,10},{10,... | collective-permute-start | bytes 196616 | tf_op jit(solution)/shard_map/cond/branch_1_fun/ppermute | solution.py:208
  40.8 5.3 %collective-permute-start.8 = (bf16[64,512]{1,0:T(8,128)(2,1)S(1)}, bf16[64,512]{1,0:T(8,128)(2,1)S(1)}, u32[]{:S(2)}, u32[]{:S(2)}) collective-permute-start(bf16[64,512]{1,0:T(8,128)(2,1)S(1)} %slice.26), channel_id=1, source_target_pairs={{0,1},{1,0},{2,3},{3,2},{4,5},{5,4},{6,7},{7,6},{8,9},{9,8},{10,11... | collective-permute-start | bytes 196616 | tf_op jit(solution)/shard_map/cond/branch_1_fun/ppermute | solution.py:208
  43.2 6.2 %collective-permute-start.9 = (bf16[64,512]{1,0:T(8,128)(2,1)S(1)}, bf16[64,512]{1,0:T(8,128)(2,1)S(1)}, u32[]{:S(2)}, u32[]{:S(2)}) collective-permute-start(bf16[64,512]{1,0:T(8,128)(2,1)S(1)} %slice.26), channel_id=1, source_target_pairs={{0,2},{1,3},{2,0},{3,1},{4,6},{5,7},{6,4},{7,5},{8,10},{9,11},{10,... | collective-permute-start | bytes 196616 | tf_op jit(solution)/shard_map/cond/branch_1_fun/ppermute | solution.py:208
  50.7 17.0 %all-to-all-start.6 = ((bf16[16,16,1536]{2,1,0:T(8,128)(2,1)}), bf16[16,16,1536]{2,1,0:T(8,128)(2,1)S(1)}, u32[]{:S(2)}, u32[]{:S(2)}) async-start(bf16[16,16,1536]{2,1,0:T(8,128)(2,1)} %bitcast.8), calls=%async_computation.6 | async-start | bytes 1572864 | tf_op jit(solution)/shard_map/all_to_all | solution.py:213
  57.3 1.4 copy-start
  58.7 1.4 copy-start.1
  62.2 0.8 copy-start.5
  67.8 1.0 copy-start.6
  69.5 34.2 %copy-start.2 = (bf16[1,1,1536,512]{3,2,1,0:T(8,128)(2,1)S(1)}, bf16[1,1,1536,512]{3,2,1,0:T(8,128)(2,1)}, u32[]{:S(2)}) copy-start(bf16[1,1,1536,512]{3,2,1,0:T(8,128)(2,1)} %param.27) | copy-start | bytes 4718596
  70.3 16.1 %all-to-all-start.7 = ((bf16[4,192,256]{2,1,0:T(8,128)(2,1)}), bf16[4,192,256]{2,1,0:T(8,128)(2,1)S(1)}, u32[]{:S(2)}, u32[]{:S(2)}) async-start(bf16[4,192,256]{2,1,0:T(8,128)(2,1)} %broadcast_in_dim.35), calls=%async_computation.7 | async-start | bytes 786432 | tf_op jit(solution)/shard_map/all_to_all | solution.py:204
  75.6 10.7 %collective-permute-start.20 = (bf16[192,256]{1,0:T(8,128)(2,1)S(1)}, bf16[192,256]{1,0:T(8,128)(2,1)S(1)}, u32[]{:S(2)}, u32[]{:S(2)}) collective-permute-start(bf16[192,256]{1,0:T(8,128)(2,1)S(1)} %shard_map.93), channel_id=1, source_target_pairs={{0,4},{1,5},{2,6},{3,7},{4,0},{5,1},{6,2},{7,3},{8,12},{9,13},{10,... | collective-permute-start | bytes 294920 | tf_op jit(solution)/shard_map/ppermute | solution.py:208
  87.2 16.5 %all-to-all-start.8 = ((bf16[4,192,256]{2,1,0:T(8,128)(2,1)}), bf16[4,192,256]{2,1,0:T(8,128)(2,1)S(1)}, u32[]{:S(2)}, u32[]{:S(2)}) async-start(bf16[4,192,256]{2,1,0:T(8,128)(2,1)} %broadcast_in_dim.36), calls=%async_computation.8 | async-start | bytes 786432 | tf_op jit(solution)/shard_map/all_to_all | solution.py:204
  103.7 18.6 %copy-start.4 = (bf16[1,128,512]{2,1,0:T(8,128)(2,1)S(1)}, bf16[1,128,512]{2,1,0:T(8,128)(2,1)}, u32[]{:S(2)}) copy-start(bf16[1,128,512]{2,1,0:T(8,128)(2,1)} %param.19) | copy-start | bytes 393220
  122.5 18.0 %collective-permute-start.21 = (bf16[128,512]{1,0:T(8,128)(2,1)S(1)}, bf16[128,512]{1,0:T(8,128)(2,1)S(1)}, u32[]{:S(2)}, u32[]{:S(2)}) collective-permute-start(bf16[128,512]{1,0:T(8,128)(2,1)S(1)} %shard_map.95), channel_id=1, source_target_pairs={{0,128},{128,256},{256,384},{384,0},{1,129},{129,257},{257,385},{3... | collective-permute-start | bytes 393224 | tf_op jit(solution)/shard_map/ppermute | solution.py:327

commit v4 on v3

--- a/solution.py
+++ b/solution.py
@@ -184,10 +184,11 @@
     out_ref[...] = (gate / (1.0 + jnp.exp(-gate)) * up).astype(BF)
 
 
-def contract_body(half_ref, first_ref, second_ref, down_ref, out_ref):
+def contract_body(first_ref, second_ref, down_ref, out_ref):
     parts, hid, _ = first_ref.shape
+    side = lax.axis_index("tensor") // parts
     total = jnp.zeros(out_ref.shape, F32)
-    for ref, half in ((first_ref, half_ref[0]), (second_ref, 1 - half_ref[0])):
+    for ref, half in ((first_ref, side), (second_ref, 1 - side)):
         for k in range(parts):
             rows = pl.ds(pl.multiple_of((half * parts + k) * hid, hid), hid)
             total = total + dot(ref[k], down_ref[rows, :], 0, 0)
@@ -202,6 +203,11 @@
 def to_fours(shard):
     copies = jnp.broadcast_to(shard[None], (4,) + shard.shape)
     return lax.all_to_all(copies, "tensor", 0, 0, axis_index_groups=FOURS)
+
+
+def to_fours_apart(shard, always):
+    same = jax.ShapeDtypeStruct((4,) + shard.shape, shard.dtype)
+    return lax.cond(always, to_fours, lambda x: jnp.zeros(same.shape, same.dtype), shard)
 
 
 def along(shard, by):
@@ -234,7 +240,6 @@
     n, width = tokens.shape
     slots = EXPERTS * SLOTS
     hid = w_gate.shape[0]
-    half = (lax.axis_index("tensor") // 4).astype(jnp.int32)[None]
 
     table = jax.ShapeDtypeStruct((n, slots), BF)
     rows, match, held, chosen, which = call(
@@ -253,7 +258,7 @@
     )
 
     def first_part(size):
-        def run(rows, held, gain, router):
+        def run(always, rows, held, gain, router):
             mine = rows[:size]
             far = along(mine, 4)
             return call(
@@ -265,7 +270,7 @@
                     jax.ShapeDtypeStruct((n, EXPERTS), F32),
                 ),
                 [VM] * 5,
-                (to_fours(mine), far, held, gain, router),
+                (to_fours_apart(mine, always), far, held, gain, router),
                 limit=16,
             )
 
@@ -284,8 +289,9 @@
 
         return run
 
+    always = which[0] < len(SIZES)
     first, far, squares, logits = lax.switch(
-        which[0], [first_part(size) for size in SIZES], rows, held, gain, router
+        which[0], [first_part(size) for size in SIZES], always, rows, held, gain, router
     )
     first_rows = over_dp(first)
     second, high, low = lax.switch(
@@ -311,13 +317,13 @@
         limit=16,
     )
     hidden_other = along(hidden, 4)
-    hidden_first = to_fours(hidden)
+    hidden_first = to_fours_apart(hidden, always)
     hidden_second = to_fours(hidden_other)
     reply = call(
         contract_body,
         jax.ShapeDtypeStruct((slots, width), BF),
-        [SM] + [VM] * 3,
-        (half, hidden_first, hidden_second, w_down),
+        [VM] * 3,
+        (hidden_first, hidden_second, w_down),
     )
     returned = over_dp(reply)
     layer_out = call(

time: 142 us -> 142 us (level)
  blocking collectives: 17.8 us -> 52.3 us
  starting transfers between devices: 77.7 us -> 51 us
  waiting for transfers between devices: 25.7 us -> 15.6 us
    all_to_all x0 -> x3, blocking collectives: none -> 39.8 us  [to_fours(): return lax.all_to_all(copies, 'tensor', 0, 0, axis_index_groups=FOURS)]
    all_to_all x3 -> x0, starting transfers between devices: 20.6 us -> none  [to_fours(): return lax.all_to_all(copies, 'tensor', 0, 0, axis_index_groups=FOURS)]
    ppermute x5, starting transfers between devices: 30.8 us -> 20.8 us  [along(): return lax.ppermute(shard, 'tensor', [(i, i ^ by) for i in range(8)])]
    all_to_all x3 -> x0, waiting for transfers between devices: 7.74 us -> none  [to_fours(): return lax.all_to_all(copies, 'tensor', 0, 0, axis_index_groups=FOURS)]
    ppermute x1, starting transfers between devices: 13 us -> 19.5 us  [on_device(): lax.ppermute(layer_out, 'section', [(i, (i + 1) % count) for i in range(c...]
    all_to_all x1, blocking collectives: 17.8 us -> 12.5 us  [over_dp(): lax.all_to_all(rows.reshape(EXPERTS, n // EXPERTS, width), 'dp', 0, 0)]
    ppermute x5, waiting for transfers between devices: 8.16 us -> 3.05 us  [along(): return lax.ppermute(shard, 'tensor', [(i, i ^ by) for i in range(8)])]
    all_to_all x2, waiting for transfers between devices: 4.76 us -> 9.45 us  [over_dp(): lax.all_to_all(rows.reshape(EXPERTS, n // EXPERTS, width), 'dp', 0, 0)]
  transfers between devices with their start and end apart: 11 -> 8, of which waited for: 7 -> 5; matrix products, arithmetic and copies ran while one was open for 0% -> 1% of each run, Pallas kernels for 2% -> 2%
where the time goes in v4:
time: 142 us; the launch traced here: 141 us
  blocking collectives  52.3 us (37%)
  starting transfers between devices  51 us (36%)
  waiting for transfers between devices  15.6 us (11%)
  local copies, waits for them, and re-layouts  11 us (8%)
  Pallas kernels  8.68 us (6%)
  between operations  2.05 us (1%)
    all_to_all x3, blocking collectives, to_fours(): return lax.all_to_all(copies, 'tensor', 0, 0, axis_index_groups=FOURS)  39.8 us
    ppermute x5, starting transfers between devices, along(): return lax.ppermute(shard, 'tensor', [(i, i ^ by) for i in range(8)])  20.8 us
    ppermute x1, starting transfers between devices, on_device(): lax.ppermute(layer_out, 'section', [(i, (i + 1) % count) for i in range(c...  19.5 us
    all_to_all x1, blocking collectives, over_dp(): lax.all_to_all(rows.reshape(EXPERTS, n // EXPERTS, width), 'dp', 0, 0)  12.5 us
    all_to_all x2, starting transfers between devices, over_dp(): lax.all_to_all(rows.reshape(EXPERTS, n // EXPERTS, width), 'dp', 0, 0)  10.7 us
    all_to_all x2, waiting for transfers between devices, over_dp(): lax.all_to_all(rows.reshape(EXPERTS, n // EXPERTS, width), 'dp', 0, 0)  9.45 us
    pallas_call x7, Pallas kernels, call(): pl.pallas_call(body, scratch_shapes=list(scratch), out_shape=shape, in_sp...  8.68 us
    unnamed x23, local copies, waits for them, and re-layouts  7.48 us
  transfers between devices with their start and end apart: 8, of which 5 were waited for; matrix products, arithmetic and copies ran while one was open for 1% of the time, Pallas kernels for 2%

profile of v4, /device:TPU:1, one launch (start us, length us, event | category | flops | bytes accessed | tf_op | source)
XLA Modules:
  0.0 140.8 jit_solution(1173470028713805426)
XLA Ops:
  2.9 1.1 shard_map.91
  5.3 28.4 %conditional.8 = ((bf16[256,2560]{1,0:T(8,128)(2,1)}, bf16[128,512]{1,0:T(8,128)(2,1)S(1)}, f32[128,128]{1,0:T(8,128)S(1)}, f32[128,16]{1,0:T(8,128)S(1)})) conditional(s32[]{:T(128)} %bitcast.3, (pred[]{:T(512)}, bf16[128,512]{1,0:T(8,128)(2,1)}, bf16[128,256]{1,0:T(8,128)(2,1)S(1)}, bf16[1,4096]{1,0:T(2,128)(2,1)}, ...), branch_computations={%region_0.0_spmd, %region_3.0_spmd, %region_6.0_spmd, %region_9.0_... | conditional | flops 1 | bytes 2785397 | solution.py:293
  5.4 1.6 %slice.35 = bf16[80,512]{1,0:T(8,128)(2,1)} slice(bf16[128,512]{1,0:T(8,128)(2,1)} %get-tuple-element.170), slice={[0:80], [0:512]} | slice | bytes 163840 | tf_op jit(solution)/shard_map/cond/branch_2_fun/slice | solution.py:262
  6.9 9.6 %collective-permute-start.2 = (bf16[80,512]{1,0:T(8,128)(2,1)}, bf16[80,512]{1,0:T(8,128)(2,1)S(1)}, u32[]{:S(2)}, u32[]{:S(2)}) collective-permute-start(bf16[80,512]{1,0:T(8,128)(2,1)} %slice.35), channel_id=1, source_target_pairs={{0,4},{1,5},{2,6},{3,7},{4,0},{5,1},{6,2},{7,3},{8,12},{9,13},{10,... | collective-permute-start | bytes 245768 | tf_op jit(solution)/shard_map/cond/branch_2_fun/ppermute | solution.py:214
  16.6 15.4 %conditional.2 = (bf16[4,80,512]{2,1,0:T(8,128)(2,1)S(1)}) conditional(s32[]{:T(128)} %convert_element_type.14, () %tuple.57, bf16[80,512]{1,0:T(8,128)(2,1)} %slice.35), branch_computations={%region_7.0_spmd, %region_8.0_spmd} | conditional | bytes 1064968 | solution.py:210
  16.6 0.9 broadcast_in_dim.18
  17.5 14.4 %all_to_all.46 = bf16[4,80,512]{2,1,0:T(8,128)(2,1)S(1)} all-to-all(bf16[4,80,512]{2,1,0:T(8,128)(2,1)S(1)} %broadcast_in_dim.18), channel_id=1, replica_groups={{0,1,2,3},{4,5,6,7},{8,9,10,11},{12,13,14,15},{16,17,18,19},{20,21,22,2..., dimensions={0} | all-to-all | bytes 655360 | tf_op jit(solution)/shard_map/cond/branch_2_fun/cond/branch_1_fun/all_to_all | solution.py:205
  31.9 1.7 %branch_2_fun.2 = (bf16[256,2560]{1,0:T(8,128)(2,1)}, bf16[128,512]{1,0:T(8,128)(2,1)S(1)}, f32[128,128]{1,0:T(8,128)S(1)}, f32[128,16]{1,0:T(8,128)S(1)}) custom-call(bf16[4,80,512]{2,1,0:T(8,128)(2,1)S(1)} %get-tuple-element.295.own_ref, bf16[80,512]{1,0:T(8,128)(2,1)S(1)} %collective-permute-done.2.far_ref, ...), custom_call_target="tpu_custom_call" | custom-call | tf_op jit(solution)/shard_map/cond/branch_2_fun/pallas_call | solution.py:25
  33.7 5.0 %all-to-all-start.6 = ((bf16[16,16,2560]{2,1,0:T(8,128)(2,1)}), bf16[16,16,2560]{2,1,0:T(8,128)(2,1)S(1)}, u32[]{:S(2)}, u32[]{:S(2)}) async-start(bf16[16,16,2560]{2,1,0:T(8,128)(2,1)} %bitcast.6), calls=%async_computation.6 | async-start | bytes 2621440 | tf_op jit(solution)/shard_map/all_to_all | solution.py:219
  38.7 13.8 %conditional.9 = ((bf16[256,1536]{1,0:T(8,128)(2,1)}, bf16[128,256]{1,0:T(8,128)(2,1)S(1)}, bf16[128,256]{1,0:T(8,128)(2,1)S(1)})) conditional(s32[]{:T(128)} %bitcast.3, (bf16[128,512]{1,0:T(8,128)(2,1)S(1)}, bf16[128,256]{1,0:T(8,128)(2,1)S(1)}, bf16[1,4096]{1,0:T(2,128)(2,1)S(1)}, bf16[16,4096]{1,0:T(8,128)(2,1)S(1)}, ...), branch_computations={%region_15.0_spmd, %region_16.0_spmd, %region_17.0_spmd, %region_1... | conditional | bytes 1572992 | solution.py:297
  38.7 4.9 %collective-permute-start.13 = (bf16[80,512]{1,0:T(8,128)(2,1)S(1)}, bf16[80,512]{1,0:T(8,128)(2,1)S(1)}, u32[]{:S(2)}, u32[]{:S(2)}) collective-permute-start(bf16[80,512]{1,0:T(8,128)(2,1)S(1)} %slice.42), channel_id=1, source_target_pairs={{0,3},{1,2},{2,1},{3,0},{4,7},{5,6},{6,5},{7,4},{8,11},{9,10},{10,... | collective-permute-start | bytes 245768 | tf_op jit(solution)/shard_map/cond/branch_2_fun/ppermute | solution.py:214
  43.7 1.9 %collective-permute-start.12 = (bf16[80,512]{1,0:T(8,128)(2,1)S(1)}, bf16[80,512]{1,0:T(8,128)(2,1)S(1)}, u32[]{:S(2)}, u32[]{:S(2)}) collective-permute-start(bf16[80,512]{1,0:T(8,128)(2,1)S(1)} %slice.42), channel_id=1, source_target_pairs={{0,2},{1,3},{2,0},{3,1},{4,6},{5,7},{6,4},{7,5},{8,10},{9,11},{10,... | collective-permute-start | bytes 245768 | tf_op jit(solution)/shard_map/cond/branch_2_fun/ppermute | solution.py:214
  45.6 2.4 %collective-permute-start.11 = (bf16[80,512]{1,0:T(8,128)(2,1)S(1)}, bf16[80,512]{1,0:T(8,128)(2,1)S(1)}, u32[]{:S(2)}, u32[]{:S(2)}) collective-permute-start(bf16[80,512]{1,0:T(8,128)(2,1)S(1)} %slice.42), channel_id=1, source_target_pairs={{0,1},{1,0},{2,3},{3,2},{4,5},{5,4},{6,7},{7,6},{8,9},{9,8},{10,11... | collective-permute-start | bytes 245768 | tf_op jit(solution)/shard_map/cond/branch_2_fun/ppermute | solution.py:214
  48.0 2.0 %collective-permute-done.12.b_ref = bf16[80,512]{1,0:T(8,128)(2,1)S(1)} collective-permute-done((bf16[80,512]{1,0:T(8,128)(2,1)S(1)}, bf16[80,512]{1,0:T(8,128)(2,1)S(1)}, u32[]{:S(2)}, u32[]{:S(2)}) %collective-permute-start.12) | collective-permute-done | bytes 81952 | tf_op jit(solution)/shard_map/cond/branch_2_fun/ppermute | solution.py:214
  50.1 1.0 collective-permute-done.11.a_ref
  51.1 1.4 branch_2_fun.3
  52.5 3.1 %all-to-all-done.6 = bf16[16,16,2560]{2,1,0:T(8,128)(2,1)S(1)} async-done(((bf16[16,16,2560]{2,1,0:T(8,128)(2,1)}), bf16[16,16,2560]{2,1,0:T(8,128)(2,1)S(1)}, u32[]{:S(2)}, u32[]{:S(2)}) %all-to-all-start.6) | async-done | bytes 1310752 | tf_op jit(solution)/shard_map/all_to_all | solution.py:219
  55.6 5.7 %all-to-all-start.7 = ((bf16[16,16,1536]{2,1,0:T(8,128)(2,1)}), bf16[16,16,1536]{2,1,0:T(8,128)(2,1)S(1)}, u32[]{:S(2)}, u32[]{:S(2)}) async-start(bf16[16,16,1536]{2,1,0:T(8,128)(2,1)} %bitcast.8), calls=%async_computation.7 | async-start | bytes 1572864 | tf_op jit(solution)/shard_map/all_to_all | solution.py:219
  61.3 1.4 copy-done
  62.7 1.4 copy-done.1
  64.1 2.1 %shard_map.92 = (f32[392,256]{1,0:T(8,128)S(1)}, bf16[3,192,512]{2,1,0:T(8,128)(2,1)S(1)}, bf16[3,192,512]{2,1,0:T(8,128)(2,1)S(1)}) custom-call(bf16[256,2560]{1,0:T(8,128)(2,1)S(1)} %bitcast.17, bf16[1,4096]{1,0:T(2,128)(2,1)S(1)} %copy-done.14, bf16[192,4096]{1,0:T(8,128)(2,1)S(1)} %bitcast.19, bf16[192,4096]{1,0:T(8,128)(2,1)S(1)} %bitcast.20), custom_call_target="tpu_custom_call" | custom-call | tf_op jit(solution)/shard_map/pallas_call | solution.py:25
  67.0 6.3 %all-to-all-done.7 = bf16[16,16,1536]{2,1,0:T(8,128)(2,1)S(1)} async-done(((bf16[16,16,1536]{2,1,0:T(8,128)(2,1)}), bf16[16,16,1536]{2,1,0:T(8,128)(2,1)S(1)}, u32[]{:S(2)}, u32[]{:S(2)}) %all-to-all-start.7) | async-done | bytes 786464 | tf_op jit(solution)/shard_map/all_to_all | solution.py:219
  73.3 1.0 copy-done.6
  74.3 1.4 shard_map.93
  75.7 1.9 %collective-permute-start.20 = (bf16[192,256]{1,0:T(8,128)(2,1)}, bf16[192,256]{1,0:T(8,128)(2,1)S(1)}, u32[]{:S(2)}, u32[]{:S(2)}) collective-permute-start(bf16[192,256]{1,0:T(8,128)(2,1)} %shard_map.93), channel_id=1, source_target_pairs={{0,4},{1,5},{2,6},{3,7},{4,0},{5,1},{6,2},{7,3},{8,12},{9,13},{10,... | collective-permute-start | bytes 294920 | tf_op jit(solution)/shard_map/ppermute | solution.py:214
  77.6 16.2 %conditional.10 = (bf16[4,192,256]{2,1,0:T(8,128)(2,1)S(1)}) conditional(s32[]{:T(128)} %convert_element_type.18, () %tuple.74, bf16[192,256]{1,0:T(8,128)(2,1)} %shard_map.93), branch_computations={%region_20.0_spmd, %region_21.0_spmd} | conditional | bytes 1277960 | solution.py:210
  77.6 1.0 broadcast_in_dim.25
  78.6 15.2 %all_to_all.49 = bf16[4,192,256]{2,1,0:T(8,128)(2,1)S(1)} all-to-all(bf16[4,192,256]{2,1,0:T(8,128)(2,1)S(1)} %broadcast_in_dim.25), channel_id=1, replica_groups={{0,1,2,3},{4,5,6,7},{8,9,10,11},{12,13,14,15},{16,17,18,19},{20,21,22,2..., dimensions={0} | all-to-all | bytes 786432 | tf_op jit(solution)/shard_map/cond/branch_1_fun/all_to_all | solution.py:205
  93.8 10.2 %all_to_all.50.second_ref = bf16[4,192,256]{2,1,0:T(8,128)(2,1)S(1)} all-to-all(bf16[4,192,256]{2,1,0:T(8,128)(2,1)S(1)} %broadcast_in_dim.32), channel_id=1, replica_groups={{0,1,2,3},{4,5,6,7},{8,9,10,11},{12,13,14,15},{16,17,18,19},{20,21,22,2..., dimensions={0} | all-to-all | bytes 786432 | tf_op jit(solution)/shard_map/all_to_all | solution.py:205
  104.8 12.5 %all_to_all.51 = bf16[16,16,512]{2,1,0:T(8,128)(2,1)S(1)} all-to-all(bf16[16,16,512]{2,1,0:T(8,128)(2,1)S(1)} %bitcast.22), channel_id=1, replica_groups=mesh['section'=4,'dp'=16,'tensor'=8] {'dp'}, dimensions={0} | all-to-all | bytes 524288 | tf_op jit(solution)/shard_map/all_to_all | solution.py:219
  117.6 19.5 %collective-permute-start.21 = (bf16[128,512]{1,0:T(8,128)(2,1)S(1)}, bf16[128,512]{1,0:T(8,128)(2,1)S(1)}, u32[]{:S(2)}, u32[]{:S(2)}) collective-permute-start(bf16[128,512]{1,0:T(8,128)(2,1)S(1)} %shard_map.95), channel_id=1, source_target_pairs={{0,128},{128,256},{256,384},{384,0},{1,129},{129,257},{257,385},{3... | collective-permute-start | bytes 393224 | tf_op jit(solution)/shard_map/ppermute | solution.py:333
  137.1 3.1 %collective-permute-done.21 = bf16[128,512]{1,0:T(8,128)(2,1)S(1)} collective-permute-done((bf16[128,512]{1,0:T(8,128)(2,1)S(1)}, bf16[128,512]{1,0:T(8,128)(2,1)S(1)}, u32[]{:S(2)}, u32[]{:S(2)}) %collective-permute-start.21) | collective-permute-done | bytes 131104 | tf_op jit(solution)/shard_map/ppermute | solution.py:333
  (31 shorter events, 4.7 us)
Async XLA Ops:
  0.7 0.9 copy-start.3
  1.6 0.7 copy-start.7
  2.2 0.7 copy-start.8
  5.3 26.6 %copy-start.11 = (bf16[16,4096]{1,0:T(8,128)(2,1)S(1)}, bf16[16,4096]{1,0:T(8,128)(2,1)}, u32[]{:S(2)}) copy-start(bf16[16,4096]{1,0:T(8,128)(2,1)} %get-tuple-element.173.router_ref) | copy-start | bytes 393220 | tf_op jit(solution)/shard_map/cond
  5.4 26.6 %copy-start.15 = (bf16[1,4096]{1,0:T(2,128)(2,1)S(1)}, bf16[1,4096]{1,0:T(2,128)(2,1)}, u32[]{:S(2)}) copy-start(bf16[1,4096]{1,0:T(2,128)(2,1)} %get-tuple-element.172.gain_ref) | copy-start | bytes 24580 | tf_op jit(solution)/shard_map/cond
  6.9 25.0 %collective-permute-start.2 = (bf16[80,512]{1,0:T(8,128)(2,1)}, bf16[80,512]{1,0:T(8,128)(2,1)S(1)}, u32[]{:S(2)}, u32[]{:S(2)}) collective-permute-start(bf16[80,512]{1,0:T(8,128)(2,1)} %slice.35), channel_id=1, source_target_pairs={{0,4},{1,5},{2,6},{3,7},{4,0},{5,1},{6,2},{7,3},{8,12},{9,13},{10,... | collective-permute-start | bytes 245768 | tf_op jit(solution)/shard_map/cond/branch_2_fun/ppermute | solution.py:214
  33.7 5.0 %copy-start.9 = (bf16[1,16,4096]{2,1,0:T(8,128)(2,1)S(1)}, bf16[1,16,4096]{2,1,0:T(8,128)(2,1)}, u32[]{:S(2)}) copy-start(bf16[1,16,4096]{2,1,0:T(8,128)(2,1)} %param.36) | copy-start | bytes 393220
  33.7 5.0 %copy-start.14 = (bf16[1,4096]{1,0:T(2,128)(2,1)S(1)}, bf16[1,4096]{1,0:T(2,128)(2,1)}, u32[]{:S(2)}) copy-start(bf16[1,4096]{1,0:T(2,128)(2,1)} %gain_ref.3) | copy-start | bytes 24580
  33.7 21.9 %all-to-all-start.6 = ((bf16[16,16,2560]{2,1,0:T(8,128)(2,1)}), bf16[16,16,2560]{2,1,0:T(8,128)(2,1)S(1)}, u32[]{:S(2)}, u32[]{:S(2)}) async-start(bf16[16,16,2560]{2,1,0:T(8,128)(2,1)} %bitcast.6), calls=%async_computation.6 | async-start | bytes 2621440 | tf_op jit(solution)/shard_map/all_to_all | solution.py:219
  38.7 9.3 %collective-permute-start.13 = (bf16[80,512]{1,0:T(8,128)(2,1)S(1)}, bf16[80,512]{1,0:T(8,128)(2,1)S(1)}, u32[]{:S(2)}, u32[]{:S(2)}) collective-permute-start(bf16[80,512]{1,0:T(8,128)(2,1)S(1)} %slice.42), channel_id=1, source_target_pairs={{0,3},{1,2},{2,1},{3,0},{4,7},{5,6},{6,5},{7,4},{8,11},{9,10},{10,... | collective-permute-start | bytes 245768 | tf_op jit(solution)/shard_map/cond/branch_2_fun/ppermute | solution.py:214
  43.7 6.4 %collective-permute-start.12 = (bf16[80,512]{1,0:T(8,128)(2,1)S(1)}, bf16[80,512]{1,0:T(8,128)(2,1)S(1)}, u32[]{:S(2)}, u32[]{:S(2)}) collective-permute-start(bf16[80,512]{1,0:T(8,128)(2,1)S(1)} %slice.42), channel_id=1, source_target_pairs={{0,2},{1,3},{2,0},{3,1},{4,6},{5,7},{6,4},{7,5},{8,10},{9,11},{10,... | collective-permute-start | bytes 245768 | tf_op jit(solution)/shard_map/cond/branch_2_fun/ppermute | solution.py:214
  45.6 5.5 %collective-permute-start.11 = (bf16[80,512]{1,0:T(8,128)(2,1)S(1)}, bf16[80,512]{1,0:T(8,128)(2,1)S(1)}, u32[]{:S(2)}, u32[]{:S(2)}) collective-permute-start(bf16[80,512]{1,0:T(8,128)(2,1)S(1)} %slice.42), channel_id=1, source_target_pairs={{0,1},{1,0},{2,3},{3,2},{4,5},{5,4},{6,7},{7,6},{8,9},{9,8},{10,11... | collective-permute-start | bytes 245768 | tf_op jit(solution)/shard_map/cond/branch_2_fun/ppermute | solution.py:214
  55.6 17.7 %all-to-all-start.7 = ((bf16[16,16,1536]{2,1,0:T(8,128)(2,1)}), bf16[16,16,1536]{2,1,0:T(8,128)(2,1)S(1)}, u32[]{:S(2)}, u32[]{:S(2)}) async-start(bf16[16,16,1536]{2,1,0:T(8,128)(2,1)} %bitcast.8), calls=%async_computation.7 | async-start | bytes 1572864 | tf_op jit(solution)/shard_map/all_to_all | solution.py:219
  61.3 1.4 %copy-start = (bf16[1,1,192,4096]{3,2,1,0:T(8,128)(2,1)S(1)}, bf16[1,1,192,4096]{3,2,1,0:T(8,128)(2,1)}, u32[]{:S(2)}) copy-start(bf16[1,1,192,4096]{3,2,1,0:T(8,128)(2,1)} %param.37) | copy-start | bytes 4718596
  62.7 1.4 copy-start.1
  66.2 0.8 copy-start.5
  73.3 1.0 copy-start.6
  75.7 18.1 %collective-permute-start.20 = (bf16[192,256]{1,0:T(8,128)(2,1)}, bf16[192,256]{1,0:T(8,128)(2,1)S(1)}, u32[]{:S(2)}, u32[]{:S(2)}) collective-permute-start(bf16[192,256]{1,0:T(8,128)(2,1)} %shard_map.93), channel_id=1, source_target_pairs={{0,4},{1,5},{2,6},{3,7},{4,0},{5,1},{6,2},{7,3},{8,12},{9,13},{10,... | collective-permute-start | bytes 294920 | tf_op jit(solution)/shard_map/ppermute | solution.py:214
  77.6 26.5 %copy-start.2 = (bf16[1,1,1536,512]{3,2,1,0:T(8,128)(2,1)S(1)}, bf16[1,1,1536,512]{3,2,1,0:T(8,128)(2,1)}, u32[]{:S(2)}) copy-start(bf16[1,1,1536,512]{3,2,1,0:T(8,128)(2,1)} %param.39) | copy-start | bytes 4718596
  104.1 13.3 %copy-start.4 = (bf16[1,128,512]{2,1,0:T(8,128)(2,1)S(1)}, bf16[1,128,512]{2,1,0:T(8,128)(2,1)}, u32[]{:S(2)}) copy-start(bf16[1,128,512]{2,1,0:T(8,128)(2,1)} %param.31) | copy-start | bytes 393220
  117.6 22.6 %collective-permute-start.21 = (bf16[128,512]{1,0:T(8,128)(2,1)S(1)}, bf16[128,512]{1,0:T(8,128)(2,1)S(1)}, u32[]{:S(2)}, u32[]{:S(2)}) collective-permute-start(bf16[128,512]{1,0:T(8,128)(2,1)S(1)} %shard_map.95), channel_id=1, source_target_pairs={{0,128},{128,256},{256,384},{384,0},{1,129},{129,257},{257,385},{3... | collective-permute-start | bytes 393224 | tf_op jit(solution)/shard_map/ppermute | solution.py:333

commit v5 on v4

--- a/solution.py
+++ b/solution.py
@@ -37,7 +37,7 @@
     return (lax.broadcasted_iota(jnp.int32, (n, n), 0) == lax.broadcasted_iota(jnp.int32, (n, n), 1)).astype(BF)
 
 
-def route_body(ids_ref, length_ref, quota_ref, tokens_ref, rows_ref, match_ref, held_ref, chosen_ref, which_ref):
+def route_body(ids_ref, length_ref, quota_ref, tokens_ref, rows_ref, again_ref, match_ref, held_ref, chosen_ref, which_ref):
     n = ids_ref.shape[1]
     expert = lax.broadcasted_iota(jnp.int32, (EXPERTS, n), 0)
     chosen = jnp.zeros((EXPERTS, n), F32)
@@ -56,7 +56,9 @@
     used = jnp.max(kept, axis=0, keepdims=True)
     place = dot(jnp.broadcast_to(used, (8, n)).astype(BF), before, 1, 0)[0:1, :]
     compact = ((place == down.astype(F32)).astype(F32) * used).astype(BF)
-    rows_ref[...] = dot(compact, tokens_ref[...], 1, 0).astype(BF)
+    rows = dot(compact, tokens_ref[...], 1, 0).astype(BF)
+    rows_ref[...] = rows
+    again_ref[...] = rows
     match_ref[...] = match
     held_ref[...] = dot(compact, match, 1, 0).astype(BF)
     chosen_ref[...] = dot(compact, chosen.astype(BF), 1, 1)
@@ -69,13 +71,14 @@
     return [pl.ds(pl.multiple_of(r * width, width), width) for r in order]
 
 
-def pick(views, blocks, held, gain_ref, router_ref, out_ref):
+def pick(views, blocks, held, gain_ref, router_ref, out_ref, leave):
     n, width = views[0].shape
     squares = jnp.zeros((n, 1), F32)
     logits = jnp.zeros((n, EXPERTS), F32)
     for k, (view, cols) in enumerate(zip(views, blocks)):
         raw = view[...]
-        out_ref[:, k * width : (k + 1) * width] = dot(held, raw, 0, 0).astype(BF)
+        out_ref[k] = dot(held, raw, 0, 0).astype(BF)
+        leave(k)
         v = raw.astype(F32)
         squares = squares + jnp.sum(v * v, axis=1, keepdims=True)
         scaled = (v * gain_ref[:, cols].astype(F32)).astype(BF)
@@ -83,24 +86,40 @@
     return squares, logits
 
 
-def pick_first_body(own_ref, far_ref, held_ref, gain_ref, router_ref, out_ref, kept_far_ref, squares_ref, logits_ref):
+def pick_first_body(own_ref, far_ref, held_ref, gain_ref, router_ref, out_ref, kept_far_ref, squares_ref, logits_ref, buffer, sems):
     n, width = far_ref.shape
     blocks = blocks_of(lax.axis_index("tensor"), width)[:5]
     views = [own_ref.at[k] for k in range(4)] + [far_ref]
-    squares, logits = pick(views, blocks, held_ref[0:n, :], gain_ref, router_ref, out_ref)
+    copies = []
+
+    def leave(k):
+        cols = slice(k * width, (k + 1) * width)
+        copies.append(pltpu.make_async_copy(buffer.at[k], out_ref.at[:, cols], sems.at[k]))
+        copies[k].start()
+
+    squares, logits = pick(views, blocks, held_ref[0:n, :], gain_ref, router_ref, buffer, leave)
     kept_far_ref[0:n, :] = far_ref[...]
     squares_ref[0:n, :] = jnp.broadcast_to(squares, (n, squares_ref.shape[1]))
     logits_ref[0:n, :] = logits
+    for copy in copies:
+        copy.wait()
 
 
 def pick_second_body(
     a_ref, b_ref, c_ref, held_ref, gain_ref, router_ref, squares_ref, logits_ref, match_ref, chosen_ref,
-    out_ref, high_ref, low_ref,
+    out_ref, high_ref, low_ref, buffer, sems,
 ):
     n, width = a_ref.shape
     blocks = blocks_of(lax.axis_index("tensor"), width)[5:]
     held = held_ref[0:n, :]
-    squares, logits = pick([a_ref, b_ref, c_ref], blocks, held, gain_ref, router_ref, out_ref)
+    copies = []
+
+    def leave(k):
+        cols = slice(k * width, (k + 1) * width)
+        copies.append(pltpu.make_async_copy(buffer.at[k], out_ref.at[:, cols], sems.at[k]))
+        copies[k].start()
+
+    squares, logits = pick([a_ref, b_ref, c_ref], blocks, held, gain_ref, router_ref, buffer, leave)
     inverse = lax.rsqrt((squares + squares_ref[0:n, 0:1]) / (8 * width) + norm_eps)
     chosen = chosen_ref[0:n, :]
     powered = jnp.exp((logits + logits_ref[0:n, :]) * inverse) * chosen
@@ -120,6 +139,8 @@
     high = value.astype(BF)
     high_ref[...] = high
     low_ref[...] = (value - high.astype(F32)).astype(BF)
+    for copy in copies:
+        copy.wait()
 
 
 def partial_products(rows_ref, gain_ref, blocks, weights):
@@ -171,17 +192,23 @@
             copy.wait()
 
 
-def expand_second_body(rows_ref, parts_ref, gain_ref, gate_rest, up_rest, out_ref):
+def expand_second_body(rows_ref, parts_hbm, gain_ref, gate_rest, up_rest, out_ref, copies_ref, parts_ref, sem):
     rank = lax.axis_index("tensor")
     parts, hid, width = gate_rest.shape
+    copy = pltpu.make_async_copy(parts_hbm, parts_ref, sem)
+    copy.start()
     blocks = blocks_of(rank, width)[8 - parts :]
     gate, up, squares = partial_products(
         rows_ref, gain_ref, blocks, lambda k: (gate_rest[k], up_rest[k])
     )
+    copy.wait()
     inverse = lax.rsqrt((squares + parts_ref[2 * hid : 2 * hid + 1, :]) / (8 * width) + norm_eps)
     gate = (gate + parts_ref[0:hid, :]) * inverse
     up = (up + parts_ref[hid : 2 * hid, :]) * inverse
-    out_ref[...] = (gate / (1.0 + jnp.exp(-gate)) * up).astype(BF)
+    hidden = (gate / (1.0 + jnp.exp(-gate)) * up).astype(BF)
+    out_ref[...] = hidden
+    for k in range(4):
+        copies_ref[k] = hidden
 
 
 def contract_body(first_ref, second_ref, down_ref, out_ref):
@@ -200,14 +227,17 @@
     out_ref[...] = (tokens_ref[...].astype(F32) + mixed).astype(BF)
 
 
+def fours(copies):
+    return lax.all_to_all(copies, "tensor", 0, 0, axis_index_groups=FOURS)
+
+
 def to_fours(shard):
-    copies = jnp.broadcast_to(shard[None], (4,) + shard.shape)
-    return lax.all_to_all(copies, "tensor", 0, 0, axis_index_groups=FOURS)
-
-
-def to_fours_apart(shard, always):
-    same = jax.ShapeDtypeStruct((4,) + shard.shape, shard.dtype)
-    return lax.cond(always, to_fours, lambda x: jnp.zeros(same.shape, same.dtype), shard)
+    return fours(jnp.broadcast_to(shard[None], (4,) + shard.shape))
+
+
+def to_fours_apart(rows, size, always):
+    shape = (4, size) + rows.shape[1:]
+    return lax.cond(always, lambda x: to_fours(x[:size]), lambda x: jnp.zeros(shape, x.dtype), rows)
 
 
 def along(shard, by):
@@ -242,9 +272,10 @@
     hid = w_gate.shape[0]
 
     table = jax.ShapeDtypeStruct((n, slots), BF)
-    rows, match, held, chosen, which = call(
+    rows, again, match, held, chosen, which = call(
         route_body,
         (
+            jax.ShapeDtypeStruct((n, width), BF),
             jax.ShapeDtypeStruct((n, width), BF),
             table,
             table,
@@ -253,14 +284,13 @@
         ),
         [VM] * 4,
         (ids, candidate_active_extent, seat_quota_per_specialist, tokens),
-        out_specs=(VM, VM, VM, VM, SM),
+        out_specs=(VM,) * 5 + (SM,),
         limit=16,
     )
 
     def first_part(size):
-        def run(always, rows, held, gain, router):
-            mine = rows[:size]
-            far = along(mine, 4)
+        def run(which, rows, again, held, gain, router):
+            far = along(rows[:size], 4)
             return call(
                 pick_first_body,
                 (
@@ -270,7 +300,9 @@
                     jax.ShapeDtypeStruct((n, EXPERTS), F32),
                 ),
                 [VM] * 5,
-                (to_fours_apart(mine, always), far, held, gain, router),
+                (to_fours_apart(again, size, which[0] < len(SIZES)), far, held, gain, router),
+                [pltpu.VMEM((5, slots, width), BF), pltpu.SemaphoreType.DMA((5,))],
+                out_specs=(HB, VM, VM, VM),
                 limit=16,
             )
 
@@ -284,6 +316,8 @@
                 (jax.ShapeDtypeStruct((slots, 3 * width), BF), table, table),
                 [VM] * 10,
                 (*rest, held, gain, router, squares, logits, match, chosen),
+                [pltpu.VMEM((3, slots, width), BF), pltpu.SemaphoreType.DMA((3,))],
+                out_specs=(HB, VM, VM),
                 limit=16,
             )
 
@@ -291,7 +325,7 @@
 
     always = which[0] < len(SIZES)
     first, far, squares, logits = lax.switch(
-        which[0], [first_part(size) for size in SIZES], always, rows, held, gain, router
+        which[0], [first_part(size) for size in SIZES], which, rows, again, held, gain, router
     )
     first_rows = over_dp(first)
     second, high, low = lax.switch(
@@ -309,15 +343,16 @@
         [pltpu.VMEM((5, hid, width), BF)] * 2 + [pltpu.SemaphoreType.DMA((2, 8))],
         limit=16,
     )
-    hidden = call(
+    hidden, copies = call(
         expand_second_body,
-        jax.ShapeDtypeStruct((hid, slots), BF),
-        [VM] * 5,
+        (jax.ShapeDtypeStruct((hid, slots), BF), jax.ShapeDtypeStruct((4, hid, slots), BF)),
+        [VM, HB, VM, VM, VM],
         (second_rows, parts, gain, gate_rest, up_rest),
+        [pltpu.VMEM((2 * hid + 8, slots), F32), pltpu.SemaphoreType.DMA],
         limit=16,
     )
     hidden_other = along(hidden, 4)
-    hidden_first = to_fours_apart(hidden, always)
+    hidden_first = lax.cond(always, fours, jnp.zeros_like, copies)
     hidden_second = to_fours(hidden_other)
     reply = call(
         contract_body,

time: 142 us -> 135 us (0.951)
  local copies, waits for them, and re-layouts: 11 us -> 7.57 us
  starting transfers between devices: 51 us -> 48.9 us
    ppermute x1, starting transfers between devices: 19.5 us -> 14.8 us  [on_device(): lax.ppermute(layer_out, 'section', [(i, (i + 1) % count) for i in range(c...]
    all_to_all x2, starting transfers between devices: 10.7 us -> 13 us  [over_dp(): lax.all_to_all(rows.reshape(EXPERTS, n // EXPERTS, width), 'dp', 0, 0)]
    all_to_all x3, blocking collectives: 39.8 us -> 37.7 us  [fours(): return lax.all_to_all(copies, 'tensor', 0, 0, axis_index_groups=FOURS)]
    broadcast_in_dim x3 -> x2, local copies, waits for them, and re-layouts: 2 us -> 0.05 us  [to_fours(): return fours(jnp.broadcast_to(shard[None], (4,) + shard.shape))]
    all_to_all x1, blocking collectives: 12.5 us -> 14.1 us  [over_dp(): lax.all_to_all(rows.reshape(EXPERTS, n // EXPERTS, width), 'dp', 0, 0)]
    slice x1 -> x2, local copies, waits for them, and re-layouts: 1.56 us -> 0.01 us  [the longest x1 0.01 us: to_fours_apart(): x[:size]]
    all_to_all x2, waiting for transfers between devices: 9.45 us -> 8.02 us  [over_dp(): lax.all_to_all(rows.reshape(EXPERTS, n // EXPERTS, width), 'dp', 0, 0)]
  transfers between devices with their start and end apart: 8 -> 8, of which waited for: 5 -> 5; matrix products, arithmetic and copies ran while one was open for 1% -> 0% of each run, Pallas kernels for 2% -> 2%
where the time goes in v5:
time: 135 us; the launch traced here: 134 us
  blocking collectives  51.8 us (38%)
  starting transfers between devices  48.9 us (36%)
  waiting for transfers between devices  14.6 us (11%)
  Pallas kernels  8.29 us (6%)
  local copies, waits for them, and re-layouts  7.57 us (6%)
  between operations  2.11 us (2%)
    all_to_all x3, blocking collectives, fours(): return lax.all_to_all(copies, 'tensor', 0, 0, axis_index_groups=FOURS)  37.7 us
    ppermute x5, starting transfers between devices, along(): return lax.ppermute(shard, 'tensor', [(i, i ^ by) for i in range(8)])  21.1 us
    ppermute x1, starting transfers between devices, on_device(): lax.ppermute(layer_out, 'section', [(i, (i + 1) % count) for i in range(c...  14.8 us
    all_to_all x1, blocking collectives, over_dp(): lax.all_to_all(rows.reshape(EXPERTS, n // EXPERTS, width), 'dp', 0, 0)  14.1 us
    all_to_all x2, starting transfers between devices, over_dp(): lax.all_to_all(rows.reshape(EXPERTS, n // EXPERTS, width), 'dp', 0, 0)  13 us
    pallas_call x7, Pallas kernels, call(): pl.pallas_call(body, scratch_shapes=list(scratch), out_shape=shape, in_sp...  8.29 us
    all_to_all x2, waiting for transfers between devices, over_dp(): lax.all_to_all(rows.reshape(EXPERTS, n // EXPERTS, width), 'dp', 0, 0)  8.02 us
    unnamed x23, local copies, waits for them, and re-layouts  7.49 us
  transfers between devices with their start and end apart: 8, of which 5 were waited for; matrix products, arithmetic and copies ran while one was open for 0% of the time, Pallas kernels for 2%

profile of v5, /device:TPU:1, one launch (start us, length us, event | category | flops | bytes accessed | tf_op | source)
XLA Modules:
  0.0 134.0 jit_solution(8542825859950877606)
XLA Ops:
  0.7 0.9 copy-done.3
  2.9 0.8 shard_map.91
  4.4 23.5 %conditional.8 = ((bf16[256,2560]{1,0:T(8,128)(2,1)}, bf16[128,512]{1,0:T(8,128)(2,1)S(1)}, f32[128,128]{1,0:T(8,128)S(1)}, f32[128,16]{1,0:T(8,128)S(1)})) conditional(s32[]{:T(128)} %bitcast.8, (s32[1]{0:T(128)}, bf16[128,512]{1,0:T(8,128)(2,1)S(1)}, bf16[128,512]{1,0:T(8,128)(2,1)S(1)}, ...), branch_computations={%region_0.0_spmd, %region_3.0_spmd, %region_6.0_spmd, %region_9.0_... | conditional | flops 2 | bytes 2785406 | solution.py:327
  4.5 9.8 %collective-permute-start.1 = (bf16[64,512]{1,0:T(8,128)(2,1)S(1)}, bf16[64,512]{1,0:T(8,128)(2,1)S(1)}, u32[]{:S(2)}, u32[]{:S(2)}) collective-permute-start(bf16[64,512]{1,0:T(8,128)(2,1)S(1)} %slice.29), channel_id=1, source_target_pairs={{0,4},{1,5},{2,6},{3,7},{4,0},{5,1},{6,2},{7,3},{8,12},{9,13},{10,... | collective-permute-start | bytes 196616 | tf_op jit(solution)/shard_map/cond/branch_1_fun/ppermute | solution.py:244
  14.9 11.5 %conditional.1 = (bf16[4,64,512]{2,1,0:T(8,128)(2,1)S(1)}) conditional(s32[]{:T(128)} %bitcast.1, () %tuple.56, bf16[128,512]{1,0:T(8,128)(2,1)S(1)} %get-tuple-element.176), branch_computations={%region_4.0_spmd, %region_5.0_spmd} | conditional | bytes 983048 | solution.py:240
  15.0 11.5 %all_to_all.45 = bf16[4,64,512]{2,1,0:T(8,128)(2,1)S(1)} all-to-all(bf16[4,64,512]{2,1,0:T(8,128)(2,1)S(1)} %broadcast_in_dim.16), channel_id=1, replica_groups={{0,1,2,3},{4,5,6,7},{8,9,10,11},{12,13,14,15},{16,17,18,19},{20,21,22,2..., dimensions={0} | all-to-all | bytes 524288 | tf_op jit(solution)/shard_map/cond/branch_1_fun/cond/branch_1_fun/all_to_all | solution.py:231
  26.5 1.4 %branch_1_fun.2 = (bf16[256,2560]{1,0:T(8,128)(2,1)}, bf16[128,512]{1,0:T(8,128)(2,1)S(1)}, f32[128,128]{1,0:T(8,128)S(1)}, f32[128,16]{1,0:T(8,128)S(1)}) custom-call(bf16[4,64,512]{2,1,0:T(8,128)(2,1)S(1)} %get-tuple-element.315.own_ref, bf16[64,512]{1,0:T(8,128)(2,1)S(1)} %collective-permute-done.1.far_ref, ...), custom_call_target="tpu_custom_call" | custom-call | tf_op jit(solution)/shard_map/cond/branch_1_fun/pallas_call | solution.py:25
  27.9 7.3 %all-to-all-start.6 = ((bf16[16,16,2560]{2,1,0:T(8,128)(2,1)}), bf16[16,16,2560]{2,1,0:T(8,128)(2,1)S(1)}, u32[]{:S(2)}, u32[]{:S(2)}) async-start(bf16[16,16,2560]{2,1,0:T(8,128)(2,1)} %bitcast.11), calls=%async_computation.6 | async-start | bytes 2621440 | tf_op jit(solution)/shard_map/all_to_all | solution.py:249
  35.3 13.6 %conditional.9 = ((bf16[256,1536]{1,0:T(8,128)(2,1)}, bf16[128,256]{1,0:T(8,128)(2,1)S(1)}, bf16[128,256]{1,0:T(8,128)(2,1)S(1)})) conditional(s32[]{:T(128)} %bitcast.8, (bf16[128,512]{1,0:T(8,128)(2,1)S(1)}, bf16[128,256]{1,0:T(8,128)(2,1)S(1)}, bf16[1,4096]{1,0:T(2,128)(2,1)S(1)}, bf16[16,4096]{1,0:T(8,128)(2,1)S(1)}, ...), branch_computations={%region_15.0_spmd, %region_16.0_spmd, %region_17.0_spmd, %region_1... | conditional | bytes 1572992 | solution.py:331
  35.3 5.0 %collective-permute-start.10 = (bf16[64,512]{1,0:T(8,128)(2,1)S(1)}, bf16[64,512]{1,0:T(8,128)(2,1)S(1)}, u32[]{:S(2)}, u32[]{:S(2)}) collective-permute-start(bf16[64,512]{1,0:T(8,128)(2,1)S(1)} %slice.41), channel_id=1, source_target_pairs={{0,3},{1,2},{2,1},{3,0},{4,7},{5,6},{6,5},{7,4},{8,11},{9,10},{10,... | collective-permute-start | bytes 196616 | tf_op jit(solution)/shard_map/cond/branch_1_fun/ppermute | solution.py:244
  40.4 1.9 %collective-permute-start.9 = (bf16[64,512]{1,0:T(8,128)(2,1)S(1)}, bf16[64,512]{1,0:T(8,128)(2,1)S(1)}, u32[]{:S(2)}, u32[]{:S(2)}) collective-permute-start(bf16[64,512]{1,0:T(8,128)(2,1)S(1)} %slice.41), channel_id=1, source_target_pairs={{0,2},{1,3},{2,0},{3,1},{4,6},{5,7},{6,4},{7,5},{8,10},{9,11},{10,... | collective-permute-start | bytes 196616 | tf_op jit(solution)/shard_map/cond/branch_1_fun/ppermute | solution.py:244
  42.3 2.3 %collective-permute-start.8 = (bf16[64,512]{1,0:T(8,128)(2,1)S(1)}, bf16[64,512]{1,0:T(8,128)(2,1)S(1)}, u32[]{:S(2)}, u32[]{:S(2)}) collective-permute-start(bf16[64,512]{1,0:T(8,128)(2,1)S(1)} %slice.41), channel_id=1, source_target_pairs={{0,1},{1,0},{2,3},{3,2},{4,5},{5,4},{6,7},{7,6},{8,9},{9,8},{10,11... | collective-permute-start | bytes 196616 | tf_op jit(solution)/shard_map/cond/branch_1_fun/ppermute | solution.py:244
  44.6 2.1 %collective-permute-done.9.b_ref = bf16[64,512]{1,0:T(8,128)(2,1)S(1)} collective-permute-done((bf16[64,512]{1,0:T(8,128)(2,1)S(1)}, bf16[64,512]{1,0:T(8,128)(2,1)S(1)}, u32[]{:S(2)}, u32[]{:S(2)}) %collective-permute-start.9) | collective-permute-done | bytes 65568 | tf_op jit(solution)/shard_map/cond/branch_1_fun/ppermute | solution.py:244
  46.7 0.9 collective-permute-done.8.a_ref
  47.6 1.2 branch_1_fun.3
  48.8 3.2 %all-to-all-done.6 = bf16[16,16,2560]{2,1,0:T(8,128)(2,1)S(1)} async-done(((bf16[16,16,2560]{2,1,0:T(8,128)(2,1)}), bf16[16,16,2560]{2,1,0:T(8,128)(2,1)S(1)}, u32[]{:S(2)}, u32[]{:S(2)}) %all-to-all-start.6) | async-done | bytes 1310752 | tf_op jit(solution)/shard_map/all_to_all | solution.py:249
  52.0 5.6 %all-to-all-start.7 = ((bf16[16,16,1536]{2,1,0:T(8,128)(2,1)}), bf16[16,16,1536]{2,1,0:T(8,128)(2,1)S(1)}, u32[]{:S(2)}, u32[]{:S(2)}) async-start(bf16[16,16,1536]{2,1,0:T(8,128)(2,1)} %bitcast.13), calls=%async_computation.7 | async-start | bytes 1572864 | tf_op jit(solution)/shard_map/all_to_all | solution.py:249
  57.7 1.4 %copy-done = bf16[1,1,192,4096]{3,2,1,0:T(8,128)(2,1)S(1)} copy-done((bf16[1,1,192,4096]{3,2,1,0:T(8,128)(2,1)S(1)}, bf16[1,1,192,4096]{3,2,1,0:T(8,128)(2,1)}, u32[]{:S(2)}) %copy-start) | copy-done | bytes 1572888
  59.1 1.4 %copy-done.1 = bf16[1,1,192,4096]{3,2,1,0:T(8,128)(2,1)S(1)} copy-done((bf16[1,1,192,4096]{3,2,1,0:T(8,128)(2,1)S(1)}, bf16[1,1,192,4096]{3,2,1,0:T(8,128)(2,1)}, u32[]{:S(2)}) %copy-start.1) | copy-done | bytes 1572888
  60.5 2.1 %shard_map.92 = (f32[392,256]{1,0:T(8,128)S(1)}, bf16[3,192,512]{2,1,0:T(8,128)(2,1)S(1)}, bf16[3,192,512]{2,1,0:T(8,128)(2,1)S(1)}) custom-call(bf16[256,2560]{1,0:T(8,128)(2,1)S(1)} %bitcast.22, bf16[1,4096]{1,0:T(2,128)(2,1)S(1)} %copy-done.14, bf16[192,4096]{1,0:T(8,128)(2,1)S(1)} %bitcast.24, bf16[192,4096]{1,0:T(8,128)(2,1)S(1)} %bitcast.25), custom_call_target="tpu_custom_call" | custom-call | tf_op jit(solution)/shard_map/pallas_call | solution.py:25
  62.6 0.8 copy-done.5
  63.4 4.8 %all-to-all-done.7 = bf16[16,16,1536]{2,1,0:T(8,128)(2,1)S(1)} async-done(((bf16[16,16,1536]{2,1,0:T(8,128)(2,1)}), bf16[16,16,1536]{2,1,0:T(8,128)(2,1)S(1)}, u32[]{:S(2)}, u32[]{:S(2)}) %all-to-all-start.7) | async-done | bytes 786464 | tf_op jit(solution)/shard_map/all_to_all | solution.py:249
  68.2 1.0 copy-done.6
  69.2 1.7 %shard_map.93 = (bf16[192,256]{1,0:T(8,128)(2,1)S(1)}, bf16[4,192,256]{2,1,0:T(8,128)(2,1)}) custom-call(bf16[256,1536]{1,0:T(8,128)(2,1)S(1)} %bitcast.23, f32[392,256]{1,0:T(8,128)S(1)} %copy-done.6, bf16[1,4096]{1,0:T(2,128)(2,1)S(1)} %copy-done.14, bf16[3,192,512]{2,1,0:T(8,128)(2,1)S(1)} %get-tuple-element.275.gate_rest, ...), custom_call_target="tpu_custom_call" | custom-call | tf_op jit(solution)/shard_map/pallas_call | solution.py:25
  71.0 2.1 %collective-permute-start.20 = (bf16[192,256]{1,0:T(8,128)(2,1)S(1)}, bf16[192,256]{1,0:T(8,128)(2,1)S(1)}, u32[]{:S(2)}, u32[]{:S(2)}) collective-permute-start(bf16[192,256]{1,0:T(8,128)(2,1)S(1)} %get-tuple-element.278), channel_id=1, source_target_pairs={{0,4},{1,5},{2,6},{3,7},{4,0},{5,1},{6,2},{7,3},{8,12},{9,13},{10,... | collective-permute-start | bytes 294920 | tf_op jit(solution)/shard_map/ppermute | solution.py:244
  73.7 15.9 %conditional.10 = (bf16[4,192,256]{2,1,0:T(8,128)(2,1)S(1)}) conditional(s32[]{:T(128)} %bitcast.10, () %tuple.74, bf16[4,192,256]{2,1,0:T(8,128)(2,1)} %get-tuple-element.277), branch_computations={%region_20.0_spmd, %region_21.0_spmd} | conditional | bytes 786440 | solution.py:355
  73.7 15.9 %all_to_all.49 = bf16[4,192,256]{2,1,0:T(8,128)(2,1)S(1)} all-to-all(bf16[4,192,256]{2,1,0:T(8,128)(2,1)} %param.21), channel_id=1, replica_groups={{0,1,2,3},{4,5,6,7},{8,9,10,11},{12,13,14,15},{16,17,18,19},{20,21,22,2..., dimensions={0} | all-to-all | bytes 786432 | tf_op jit(solution)/shard_map/cond/branch_1_fun/all_to_all | solution.py:231
  89.6 10.4 %all_to_all.50.second_ref = bf16[4,192,256]{2,1,0:T(8,128)(2,1)S(1)} all-to-all(bf16[4,192,256]{2,1,0:T(8,128)(2,1)S(1)} %broadcast_in_dim.26), channel_id=1, replica_groups={{0,1,2,3},{4,5,6,7},{8,9,10,11},{12,13,14,15},{16,17,18,19},{20,21,22,2..., dimensions={0} | all-to-all | bytes 786432 | tf_op jit(solution)/shard_map/all_to_all | solution.py:231
  100.0 0.7 shard_map.94
  100.7 14.1 %all_to_all.51 = bf16[16,16,512]{2,1,0:T(8,128)(2,1)S(1)} all-to-all(bf16[16,16,512]{2,1,0:T(8,128)(2,1)S(1)} %bitcast.27), channel_id=1, replica_groups=mesh['section'=4,'dp'=16,'tensor'=8] {'dp'}, dimensions={0} | all-to-all | bytes 524288 | tf_op jit(solution)/shard_map/all_to_all | solution.py:249
  115.0 14.8 %collective-permute-start.21 = (bf16[128,512]{1,0:T(8,128)(2,1)S(1)}, bf16[128,512]{1,0:T(8,128)(2,1)S(1)}, u32[]{:S(2)}, u32[]{:S(2)}) collective-permute-start(bf16[128,512]{1,0:T(8,128)(2,1)S(1)} %shard_map.95), channel_id=1, source_target_pairs={{0,128},{128,256},{256,384},{384,0},{1,129},{129,257},{257,385},{3... | collective-permute-start | bytes 393224 | tf_op jit(solution)/shard_map/ppermute | solution.py:368
  129.8 3.5 %collective-permute-done.21 = bf16[128,512]{1,0:T(8,128)(2,1)S(1)} collective-permute-done((bf16[128,512]{1,0:T(8,128)(2,1)S(1)}, bf16[128,512]{1,0:T(8,128)(2,1)S(1)}, u32[]{:S(2)}, u32[]{:S(2)}) %collective-permute-start.21) | collective-permute-done | bytes 131104 | tf_op jit(solution)/shard_map/ppermute | solution.py:368
  (31 shorter events, 2.3 us)
Async XLA Ops:
  0.7 0.9 copy-start.3
  1.6 0.7 copy-start.7
  2.2 0.7 copy-start.8
  4.4 22.0 %copy-start.10 = (bf16[16,4096]{1,0:T(8,128)(2,1)S(1)}, bf16[16,4096]{1,0:T(8,128)(2,1)}, u32[]{:S(2)}) copy-start(bf16[16,4096]{1,0:T(8,128)(2,1)} %get-tuple-element.180.router_ref) | copy-start | bytes 393220 | tf_op jit(solution)/shard_map/cond
  4.4 22.0 %copy-start.15 = (bf16[1,4096]{1,0:T(2,128)(2,1)S(1)}, bf16[1,4096]{1,0:T(2,128)(2,1)}, u32[]{:S(2)}) copy-start(bf16[1,4096]{1,0:T(2,128)(2,1)} %get-tuple-element.179.gain_ref) | copy-start | bytes 24580 | tf_op jit(solution)/shard_map/cond
  4.5 22.0 %collective-permute-start.1 = (bf16[64,512]{1,0:T(8,128)(2,1)S(1)}, bf16[64,512]{1,0:T(8,128)(2,1)S(1)}, u32[]{:S(2)}, u32[]{:S(2)}) collective-permute-start(bf16[64,512]{1,0:T(8,128)(2,1)S(1)} %slice.29), channel_id=1, source_target_pairs={{0,4},{1,5},{2,6},{3,7},{4,0},{5,1},{6,2},{7,3},{8,12},{9,13},{10,... | collective-permute-start | bytes 196616 | tf_op jit(solution)/shard_map/cond/branch_1_fun/ppermute | solution.py:244
  27.9 7.4 %copy-start.9 = (bf16[1,16,4096]{2,1,0:T(8,128)(2,1)S(1)}, bf16[1,16,4096]{2,1,0:T(8,128)(2,1)}, u32[]{:S(2)}) copy-start(bf16[1,16,4096]{2,1,0:T(8,128)(2,1)} %param.36) | copy-start | bytes 393220
  27.9 7.4 %copy-start.14 = (bf16[1,4096]{1,0:T(2,128)(2,1)S(1)}, bf16[1,4096]{1,0:T(2,128)(2,1)}, u32[]{:S(2)}) copy-start(bf16[1,4096]{1,0:T(2,128)(2,1)} %gain_ref.3) | copy-start | bytes 24580
  27.9 24.1 %all-to-all-start.6 = ((bf16[16,16,2560]{2,1,0:T(8,128)(2,1)}), bf16[16,16,2560]{2,1,0:T(8,128)(2,1)S(1)}, u32[]{:S(2)}, u32[]{:S(2)}) async-start(bf16[16,16,2560]{2,1,0:T(8,128)(2,1)} %bitcast.11), calls=%async_computation.6 | async-start | bytes 2621440 | tf_op jit(solution)/shard_map/all_to_all | solution.py:249
  35.3 9.3 %collective-permute-start.10 = (bf16[64,512]{1,0:T(8,128)(2,1)S(1)}, bf16[64,512]{1,0:T(8,128)(2,1)S(1)}, u32[]{:S(2)}, u32[]{:S(2)}) collective-permute-start(bf16[64,512]{1,0:T(8,128)(2,1)S(1)} %slice.41), channel_id=1, source_target_pairs={{0,3},{1,2},{2,1},{3,0},{4,7},{5,6},{6,5},{7,4},{8,11},{9,10},{10,... | collective-permute-start | bytes 196616 | tf_op jit(solution)/shard_map/cond/branch_1_fun/ppermute | solution.py:244
  40.4 6.4 %collective-permute-start.9 = (bf16[64,512]{1,0:T(8,128)(2,1)S(1)}, bf16[64,512]{1,0:T(8,128)(2,1)S(1)}, u32[]{:S(2)}, u32[]{:S(2)}) collective-permute-start(bf16[64,512]{1,0:T(8,128)(2,1)S(1)} %slice.41), channel_id=1, source_target_pairs={{0,2},{1,3},{2,0},{3,1},{4,6},{5,7},{6,4},{7,5},{8,10},{9,11},{10,... | collective-permute-start | bytes 196616 | tf_op jit(solution)/shard_map/cond/branch_1_fun/ppermute | solution.py:244
  42.3 5.3 %collective-permute-start.8 = (bf16[64,512]{1,0:T(8,128)(2,1)S(1)}, bf16[64,512]{1,0:T(8,128)(2,1)S(1)}, u32[]{:S(2)}, u32[]{:S(2)}) collective-permute-start(bf16[64,512]{1,0:T(8,128)(2,1)S(1)} %slice.41), channel_id=1, source_target_pairs={{0,1},{1,0},{2,3},{3,2},{4,5},{5,4},{6,7},{7,6},{8,9},{9,8},{10,11... | collective-permute-start | bytes 196616 | tf_op jit(solution)/shard_map/cond/branch_1_fun/ppermute | solution.py:244
  52.0 16.2 %all-to-all-start.7 = ((bf16[16,16,1536]{2,1,0:T(8,128)(2,1)}), bf16[16,16,1536]{2,1,0:T(8,128)(2,1)S(1)}, u32[]{:S(2)}, u32[]{:S(2)}) async-start(bf16[16,16,1536]{2,1,0:T(8,128)(2,1)} %bitcast.13), calls=%async_computation.7 | async-start | bytes 1572864 | tf_op jit(solution)/shard_map/all_to_all | solution.py:249
  57.7 1.4 %copy-start = (bf16[1,1,192,4096]{3,2,1,0:T(8,128)(2,1)S(1)}, bf16[1,1,192,4096]{3,2,1,0:T(8,128)(2,1)}, u32[]{:S(2)}) copy-start(bf16[1,1,192,4096]{3,2,1,0:T(8,128)(2,1)} %param.37) | copy-start | bytes 4718596
  59.1 1.4 %copy-start.1 = (bf16[1,1,192,4096]{3,2,1,0:T(8,128)(2,1)S(1)}, bf16[1,1,192,4096]{3,2,1,0:T(8,128)(2,1)}, u32[]{:S(2)}) copy-start(bf16[1,1,192,4096]{3,2,1,0:T(8,128)(2,1)} %param.38) | copy-start | bytes 4718596
  62.6 0.8 copy-start.5
  68.2 1.0 copy-start.6
  71.0 29.0 %copy-start.2 = (bf16[1,1,1536,512]{3,2,1,0:T(8,128)(2,1)S(1)}, bf16[1,1,1536,512]{3,2,1,0:T(8,128)(2,1)}, u32[]{:S(2)}) copy-start(bf16[1,1,1536,512]{3,2,1,0:T(8,128)(2,1)} %param.39) | copy-start | bytes 4718596
  71.0 18.6 %collective-permute-start.20 = (bf16[192,256]{1,0:T(8,128)(2,1)S(1)}, bf16[192,256]{1,0:T(8,128)(2,1)S(1)}, u32[]{:S(2)}, u32[]{:S(2)}) collective-permute-start(bf16[192,256]{1,0:T(8,128)(2,1)S(1)} %get-tuple-element.278), channel_id=1, source_target_pairs={{0,4},{1,5},{2,6},{3,7},{4,0},{5,1},{6,2},{7,3},{8,12},{9,13},{10,... | collective-permute-start | bytes 294920 | tf_op jit(solution)/shard_map/ppermute | solution.py:244
  100.0 14.8 %copy-start.4 = (bf16[1,128,512]{2,1,0:T(8,128)(2,1)S(1)}, bf16[1,128,512]{2,1,0:T(8,128)(2,1)}, u32[]{:S(2)}) copy-start(bf16[1,128,512]{2,1,0:T(8,128)(2,1)} %param.31) | copy-start | bytes 393220
  115.0 18.3 %collective-permute-start.21 = (bf16[128,512]{1,0:T(8,128)(2,1)S(1)}, bf16[128,512]{1,0:T(8,128)(2,1)S(1)}, u32[]{:S(2)}, u32[]{:S(2)}) collective-permute-start(bf16[128,512]{1,0:T(8,128)(2,1)S(1)} %shard_map.95), channel_id=1, source_target_pairs={{0,128},{128,256},{256,384},{384,0},{1,129},{129,257},{257,385},{3... | collective-permute-start | bytes 393224 | tf_op jit(solution)/shard_map/ppermute | solution.py:368

commit v6 on v5

--- a/solution.py
+++ b/solution.py
@@ -323,7 +323,6 @@
 
         return run
 
-    always = which[0] < len(SIZES)
     first, far, squares, logits = lax.switch(
         which[0], [first_part(size) for size in SIZES], which, rows, again, held, gain, router
     )
@@ -352,7 +351,7 @@
         limit=16,
     )
     hidden_other = along(hidden, 4)
-    hidden_first = lax.cond(always, fours, jnp.zeros_like, copies)
+    hidden_first = fours(copies)
     hidden_second = to_fours(hidden_other)
     reply = call(
         contract_body,

time: 135 us -> 138 us (1.022)
  blocking collectives: 51.8 us -> 42.1 us
  starting transfers between devices: 48.9 us -> 56.9 us
  waiting for transfers between devices: 14.6 us -> 19.6 us
    all_to_all x3 -> x2, blocking collectives: 37.7 us -> 27.5 us  [fours(): return lax.all_to_all(copies, 'tensor', 0, 0, axis_index_groups=FOURS)]
    ppermute x5, waiting for transfers between devices: 2.99 us -> 9.35 us  [along(): return lax.ppermute(shard, 'tensor', [(i, i ^ by) for i in range(8)])]
    all_to_all x0 -> x1, starting transfers between devices: none -> 4.81 us  [fours(): return lax.all_to_all(copies, 'tensor', 0, 0, axis_index_groups=FOURS)]
    ppermute x1, starting transfers between devices: 14.8 us -> 17.2 us  [on_device(): lax.ppermute(layer_out, 'section', [(i, (i + 1) % count) for i in range(c...]
    unnamed x23 -> x25, local copies, waits for them, and re-layouts: 7.49 us -> 8.24 us
  transfers between devices with their start and end apart: 8 -> 9, of which waited for: 5 -> 6; matrix products, arithmetic and copies ran while one was open for 0% -> 0% of each run, Pallas kernels for 2% -> 2%
where the time goes in v6:
time: 138 us; the launch traced here: 137 us
  starting transfers between devices  56.9 us (41%)
  blocking collectives  42.1 us (31%)
  waiting for transfers between devices  19.6 us (14%)
  local copies, waits for them, and re-layouts  8.32 us (6%)
  Pallas kernels  7.53 us (5%)
  between operations  1.47 us (1%)
    all_to_all x2, blocking collectives, fours(): return lax.all_to_all(copies, 'tensor', 0, 0, axis_index_groups=FOURS)  27.5 us
    ppermute x5, starting transfers between devices, along(): return lax.ppermute(shard, 'tensor', [(i, i ^ by) for i in range(8)])  22.5 us
    ppermute x1, starting transfers between devices, on_device(): lax.ppermute(layer_out, 'section', [(i, (i + 1) % count) for i in range(c...  17.2 us
    all_to_all x1, blocking collectives, over_dp(): lax.all_to_all(rows.reshape(EXPERTS, n // EXPERTS, width), 'dp', 0, 0)  14.6 us
    all_to_all x2, starting transfers between devices, over_dp(): lax.all_to_all(rows.reshape(EXPERTS, n // EXPERTS, width), 'dp', 0, 0)  12.4 us
    ppermute x5, waiting for transfers between devices, along(): return lax.ppermute(shard, 'tensor', [(i, i ^ by) for i in range(8)])  9.35 us
    unnamed x25, local copies, waits for them, and re-layouts  8.24 us
    pallas_call x7, Pallas kernels, call(): pl.pallas_call(body, scratch_shapes=list(scratch), out_shape=shape, in_sp...  7.53 us
  transfers between devices with their start and end apart: 9, of which 6 were waited for; matrix products, arithmetic and copies ran while one was open for 0% of the time, Pallas kernels for 2%

profile of v6, /device:TPU:1, one launch (start us, length us, event | category | flops | bytes accessed | tf_op | source)
XLA Modules:
  0.0 136.7 jit_solution(6362928827512620510)
XLA Ops:
  0.7 0.9 copy-done.3
  2.9 0.8 shard_map.91
  4.4 24.0 %conditional.7 = ((bf16[256,2560]{1,0:T(8,128)(2,1)}, bf16[128,512]{1,0:T(8,128)(2,1)S(1)}, f32[128,128]{1,0:T(8,128)S(1)}, f32[128,16]{1,0:T(8,128)S(1)})) conditional(s32[]{:T(128)} %bitcast.8, (s32[1]{0:T(128)}, bf16[128,512]{1,0:T(8,128)(2,1)S(1)}, bf16[128,512]{1,0:T(8,128)(2,1)S(1)}, ...), branch_computations={%region_0.0_spmd, %region_3.0_spmd, %region_6.0_spmd, %region_9.0_... | conditional | flops 2 | bytes 2785406 | solution.py:326
  4.5 9.8 %collective-permute-start.1 = (bf16[64,512]{1,0:T(8,128)(2,1)S(1)}, bf16[64,512]{1,0:T(8,128)(2,1)S(1)}, u32[]{:S(2)}, u32[]{:S(2)}) collective-permute-start(bf16[64,512]{1,0:T(8,128)(2,1)S(1)} %slice.29), channel_id=1, source_target_pairs={{0,4},{1,5},{2,6},{3,7},{4,0},{5,1},{6,2},{7,3},{8,12},{9,13},{10,... | collective-permute-start | bytes 196616 | tf_op jit(solution)/shard_map/cond/branch_1_fun/ppermute | solution.py:244
  14.9 12.0 %conditional.1 = (bf16[4,64,512]{2,1,0:T(8,128)(2,1)S(1)}) conditional(s32[]{:T(128)} %bitcast.1, () %tuple.51, bf16[128,512]{1,0:T(8,128)(2,1)S(1)} %get-tuple-element.172), branch_computations={%region_4.0_spmd, %region_5.0_spmd} | conditional | bytes 983048 | solution.py:240
  15.0 12.0 %all_to_all.46 = bf16[4,64,512]{2,1,0:T(8,128)(2,1)S(1)} all-to-all(bf16[4,64,512]{2,1,0:T(8,128)(2,1)S(1)} %broadcast_in_dim.16), channel_id=1, replica_groups={{0,1,2,3},{4,5,6,7},{8,9,10,11},{12,13,14,15},{16,17,18,19},{20,21,22,2..., dimensions={0} | all-to-all | bytes 524288 | tf_op jit(solution)/shard_map/cond/branch_1_fun/cond/branch_1_fun/all_to_all | solution.py:231
  26.9 1.4 %branch_1_fun.2 = (bf16[256,2560]{1,0:T(8,128)(2,1)}, bf16[128,512]{1,0:T(8,128)(2,1)S(1)}, f32[128,128]{1,0:T(8,128)S(1)}, f32[128,16]{1,0:T(8,128)S(1)}) custom-call(bf16[4,64,512]{2,1,0:T(8,128)(2,1)S(1)} %get-tuple-element.311.own_ref, bf16[64,512]{1,0:T(8,128)(2,1)S(1)} %collective-permute-done.1.far_ref, ...), custom_call_target="tpu_custom_call" | custom-call | tf_op jit(solution)/shard_map/cond/branch_1_fun/pallas_call | solution.py:25
  28.4 6.6 %all-to-all-start.5 = ((bf16[16,16,2560]{2,1,0:T(8,128)(2,1)}), bf16[16,16,2560]{2,1,0:T(8,128)(2,1)S(1)}, u32[]{:S(2)}, u32[]{:S(2)}) async-start(bf16[16,16,2560]{2,1,0:T(8,128)(2,1)} %bitcast.10), calls=%async_computation.5 | async-start | bytes 2621440 | tf_op jit(solution)/shard_map/all_to_all | solution.py:249
  35.1 14.0 %conditional.8 = ((bf16[256,1536]{1,0:T(8,128)(2,1)}, bf16[128,256]{1,0:T(8,128)(2,1)S(1)}, bf16[128,256]{1,0:T(8,128)(2,1)S(1)})) conditional(s32[]{:T(128)} %bitcast.8, (bf16[128,512]{1,0:T(8,128)(2,1)S(1)}, bf16[128,256]{1,0:T(8,128)(2,1)S(1)}, bf16[1,4096]{1,0:T(2,128)(2,1)S(1)}, bf16[16,4096]{1,0:T(8,128)(2,1)S(1)}, ...), branch_computations={%region_15.0_spmd, %region_16.0_spmd, %region_17.0_spmd, %region_1... | conditional | bytes 1572992 | solution.py:330
  35.1 5.5 %collective-permute-start.10 = (bf16[64,512]{1,0:T(8,128)(2,1)S(1)}, bf16[64,512]{1,0:T(8,128)(2,1)S(1)}, u32[]{:S(2)}, u32[]{:S(2)}) collective-permute-start(bf16[64,512]{1,0:T(8,128)(2,1)S(1)} %slice.41), channel_id=1, source_target_pairs={{0,3},{1,2},{2,1},{3,0},{4,7},{5,6},{6,5},{7,4},{8,11},{9,10},{10,... | collective-permute-start | bytes 196616 | tf_op jit(solution)/shard_map/cond/branch_1_fun/ppermute | solution.py:244
  40.6 1.9 %collective-permute-start.9 = (bf16[64,512]{1,0:T(8,128)(2,1)S(1)}, bf16[64,512]{1,0:T(8,128)(2,1)S(1)}, u32[]{:S(2)}, u32[]{:S(2)}) collective-permute-start(bf16[64,512]{1,0:T(8,128)(2,1)S(1)} %slice.41), channel_id=1, source_target_pairs={{0,2},{1,3},{2,0},{3,1},{4,6},{5,7},{6,4},{7,5},{8,10},{9,11},{10,... | collective-permute-start | bytes 196616 | tf_op jit(solution)/shard_map/cond/branch_1_fun/ppermute | solution.py:244
  42.5 2.2 %collective-permute-start.8 = (bf16[64,512]{1,0:T(8,128)(2,1)S(1)}, bf16[64,512]{1,0:T(8,128)(2,1)S(1)}, u32[]{:S(2)}, u32[]{:S(2)}) collective-permute-start(bf16[64,512]{1,0:T(8,128)(2,1)S(1)} %slice.41), channel_id=1, source_target_pairs={{0,1},{1,0},{2,3},{3,2},{4,5},{5,4},{6,7},{7,6},{8,9},{9,8},{10,11... | collective-permute-start | bytes 196616 | tf_op jit(solution)/shard_map/cond/branch_1_fun/ppermute | solution.py:244
  44.8 2.3 %collective-permute-done.9.b_ref = bf16[64,512]{1,0:T(8,128)(2,1)S(1)} collective-permute-done((bf16[64,512]{1,0:T(8,128)(2,1)S(1)}, bf16[64,512]{1,0:T(8,128)(2,1)S(1)}, u32[]{:S(2)}, u32[]{:S(2)}) %collective-permute-start.9) | collective-permute-done | bytes 65568 | tf_op jit(solution)/shard_map/cond/branch_1_fun/ppermute | solution.py:244
  47.0 0.8 collective-permute-done.8.a_ref
  47.9 1.2 branch_1_fun.3
  49.1 2.5 %all-to-all-done.5 = bf16[16,16,2560]{2,1,0:T(8,128)(2,1)S(1)} async-done(((bf16[16,16,2560]{2,1,0:T(8,128)(2,1)}), bf16[16,16,2560]{2,1,0:T(8,128)(2,1)S(1)}, u32[]{:S(2)}, u32[]{:S(2)}) %all-to-all-start.5) | async-done | bytes 1310752 | tf_op jit(solution)/shard_map/all_to_all | solution.py:249
  51.5 5.7 %all-to-all-start.6 = ((bf16[16,16,1536]{2,1,0:T(8,128)(2,1)}), bf16[16,16,1536]{2,1,0:T(8,128)(2,1)S(1)}, u32[]{:S(2)}, u32[]{:S(2)}) async-start(bf16[16,16,1536]{2,1,0:T(8,128)(2,1)} %bitcast.12), calls=%async_computation.6 | async-start | bytes 1572864 | tf_op jit(solution)/shard_map/all_to_all | solution.py:249
  57.3 1.4 %copy-done = bf16[1,1,192,4096]{3,2,1,0:T(8,128)(2,1)S(1)} copy-done((bf16[1,1,192,4096]{3,2,1,0:T(8,128)(2,1)S(1)}, bf16[1,1,192,4096]{3,2,1,0:T(8,128)(2,1)}, u32[]{:S(2)}) %copy-start) | copy-done | bytes 1572888
  58.7 1.4 %copy-done.1 = bf16[1,1,192,4096]{3,2,1,0:T(8,128)(2,1)S(1)} copy-done((bf16[1,1,192,4096]{3,2,1,0:T(8,128)(2,1)S(1)}, bf16[1,1,192,4096]{3,2,1,0:T(8,128)(2,1)}, u32[]{:S(2)}) %copy-start.1) | copy-done | bytes 1572888
  60.1 2.1 %shard_map.92 = (f32[392,256]{1,0:T(8,128)S(1)}, bf16[3,192,512]{2,1,0:T(8,128)(2,1)S(1)}, bf16[3,192,512]{2,1,0:T(8,128)(2,1)S(1)}) custom-call(bf16[256,2560]{1,0:T(8,128)(2,1)S(1)} %bitcast.21, bf16[1,4096]{1,0:T(2,128)(2,1)S(1)} %copy-done.15, bf16[192,4096]{1,0:T(8,128)(2,1)S(1)} %bitcast.23, bf16[192,4096]{1,0:T(8,128)(2,1)S(1)} %bitcast.24), custom_call_target="tpu_custom_call" | custom-call | tf_op jit(solution)/shard_map/pallas_call | solution.py:25
  62.2 0.8 copy-done.5
  63.0 5.0 %all-to-all-done.6 = bf16[16,16,1536]{2,1,0:T(8,128)(2,1)S(1)} async-done(((bf16[16,16,1536]{2,1,0:T(8,128)(2,1)}), bf16[16,16,1536]{2,1,0:T(8,128)(2,1)S(1)}, u32[]{:S(2)}, u32[]{:S(2)}) %all-to-all-start.6) | async-done | bytes 786464 | tf_op jit(solution)/shard_map/all_to_all | solution.py:249
  68.0 1.0 copy-done.6
  69.0 1.0 shard_map.93
  70.0 0.8 copy-done.7
  70.7 4.8 %all-to-all-start.7 = ((bf16[4,192,256]{2,1,0:T(8,128)(2,1)}), bf16[4,192,256]{2,1,0:T(8,128)(2,1)S(1)}, u32[]{:S(2)}, u32[]{:S(2)}) async-start(bf16[4,192,256]{2,1,0:T(8,128)(2,1)} %copy-done.7), calls=%async_computation.7 | async-start | bytes 786432 | tf_op jit(solution)/shard_map/all_to_all | solution.py:231
  75.6 3.1 %collective-permute-start.20 = (bf16[192,256]{1,0:T(8,128)(2,1)S(1)}, bf16[192,256]{1,0:T(8,128)(2,1)S(1)}, u32[]{:S(2)}, u32[]{:S(2)}) collective-permute-start(bf16[192,256]{1,0:T(8,128)(2,1)S(1)} %get-tuple-element.274), channel_id=1, source_target_pairs={{0,4},{1,5},{2,6},{3,7},{4,0},{5,1},{6,2},{7,3},{8,12},{9,13},{10,... | collective-permute-start | bytes 294920 | tf_op jit(solution)/shard_map/ppermute | solution.py:244
  78.7 6.2 %collective-permute-done.20 = bf16[192,256]{1,0:T(8,128)(2,1)S(1)} collective-permute-done((bf16[192,256]{1,0:T(8,128)(2,1)S(1)}, bf16[192,256]{1,0:T(8,128)(2,1)S(1)}, u32[]{:S(2)}, u32[]{:S(2)}) %collective-permute-start.20) | collective-permute-done | bytes 98336 | tf_op jit(solution)/shard_map/ppermute | solution.py:244
  85.0 15.5 %all_to_all.50.second_ref = bf16[4,192,256]{2,1,0:T(8,128)(2,1)S(1)} all-to-all(bf16[4,192,256]{2,1,0:T(8,128)(2,1)S(1)} %broadcast_in_dim.26), channel_id=1, replica_groups={{0,1,2,3},{4,5,6,7},{8,9,10,11},{12,13,14,15},{16,17,18,19},{20,21,22,2..., dimensions={0} | all-to-all | bytes 786432 | tf_op jit(solution)/shard_map/all_to_all | solution.py:231
  101.2 14.6 %all_to_all.51 = bf16[16,16,512]{2,1,0:T(8,128)(2,1)S(1)} all-to-all(bf16[16,16,512]{2,1,0:T(8,128)(2,1)S(1)} %bitcast.26), channel_id=1, replica_groups=mesh['section'=4,'dp'=16,'tensor'=8] {'dp'}, dimensions={0} | all-to-all | bytes 524288 | tf_op jit(solution)/shard_map/all_to_all | solution.py:249
  116.1 17.2 %collective-permute-start.21 = (bf16[128,512]{1,0:T(8,128)(2,1)S(1)}, bf16[128,512]{1,0:T(8,128)(2,1)S(1)}, u32[]{:S(2)}, u32[]{:S(2)}) collective-permute-start(bf16[128,512]{1,0:T(8,128)(2,1)S(1)} %shard_map.95), channel_id=1, source_target_pairs={{0,128},{128,256},{256,384},{384,0},{1,129},{129,257},{257,385},{3... | collective-permute-start | bytes 393224 | tf_op jit(solution)/shard_map/ppermute | solution.py:367
  133.3 2.8 %collective-permute-done.21 = bf16[128,512]{1,0:T(8,128)(2,1)S(1)} collective-permute-done((bf16[128,512]{1,0:T(8,128)(2,1)S(1)}, bf16[128,512]{1,0:T(8,128)(2,1)S(1)}, u32[]{:S(2)}, u32[]{:S(2)}) %collective-permute-start.21) | collective-permute-done | bytes 131104 | tf_op jit(solution)/shard_map/ppermute | solution.py:367
  (33 shorter events, 3.1 us)
Async XLA Ops:
  0.7 0.9 copy-start.3
  1.6 0.7 copy-start.8
  2.2 0.7 copy-start.9
  4.4 22.5 %copy-start.11 = (bf16[16,4096]{1,0:T(8,128)(2,1)S(1)}, bf16[16,4096]{1,0:T(8,128)(2,1)}, u32[]{:S(2)}) copy-start(bf16[16,4096]{1,0:T(8,128)(2,1)} %get-tuple-element.176.router_ref) | copy-start | bytes 393220 | tf_op jit(solution)/shard_map/cond
  4.4 22.5 %copy-start.16 = (bf16[1,4096]{1,0:T(2,128)(2,1)S(1)}, bf16[1,4096]{1,0:T(2,128)(2,1)}, u32[]{:S(2)}) copy-start(bf16[1,4096]{1,0:T(2,128)(2,1)} %get-tuple-element.175.gain_ref) | copy-start | bytes 24580 | tf_op jit(solution)/shard_map/cond
  4.5 22.5 %collective-permute-start.1 = (bf16[64,512]{1,0:T(8,128)(2,1)S(1)}, bf16[64,512]{1,0:T(8,128)(2,1)S(1)}, u32[]{:S(2)}, u32[]{:S(2)}) collective-permute-start(bf16[64,512]{1,0:T(8,128)(2,1)S(1)} %slice.29), channel_id=1, source_target_pairs={{0,4},{1,5},{2,6},{3,7},{4,0},{5,1},{6,2},{7,3},{8,12},{9,13},{10,... | collective-permute-start | bytes 196616 | tf_op jit(solution)/shard_map/cond/branch_1_fun/ppermute | solution.py:244
  28.4 6.7 %copy-start.10 = (bf16[1,16,4096]{2,1,0:T(8,128)(2,1)S(1)}, bf16[1,16,4096]{2,1,0:T(8,128)(2,1)}, u32[]{:S(2)}) copy-start(bf16[1,16,4096]{2,1,0:T(8,128)(2,1)} %param.34) | copy-start | bytes 393220
  28.4 6.7 %copy-start.15 = (bf16[1,4096]{1,0:T(2,128)(2,1)S(1)}, bf16[1,4096]{1,0:T(2,128)(2,1)}, u32[]{:S(2)}) copy-start(bf16[1,4096]{1,0:T(2,128)(2,1)} %gain_ref.3) | copy-start | bytes 24580
  28.4 23.1 %all-to-all-start.5 = ((bf16[16,16,2560]{2,1,0:T(8,128)(2,1)}), bf16[16,16,2560]{2,1,0:T(8,128)(2,1)S(1)}, u32[]{:S(2)}, u32[]{:S(2)}) async-start(bf16[16,16,2560]{2,1,0:T(8,128)(2,1)} %bitcast.10), calls=%async_computation.5 | async-start | bytes 2621440 | tf_op jit(solution)/shard_map/all_to_all | solution.py:249
  35.1 9.6 %collective-permute-start.10 = (bf16[64,512]{1,0:T(8,128)(2,1)S(1)}, bf16[64,512]{1,0:T(8,128)(2,1)S(1)}, u32[]{:S(2)}, u32[]{:S(2)}) collective-permute-start(bf16[64,512]{1,0:T(8,128)(2,1)S(1)} %slice.41), channel_id=1, source_target_pairs={{0,3},{1,2},{2,1},{3,0},{4,7},{5,6},{6,5},{7,4},{8,11},{9,10},{10,... | collective-permute-start | bytes 196616 | tf_op jit(solution)/shard_map/cond/branch_1_fun/ppermute | solution.py:244
  40.6 6.4 %collective-permute-start.9 = (bf16[64,512]{1,0:T(8,128)(2,1)S(1)}, bf16[64,512]{1,0:T(8,128)(2,1)S(1)}, u32[]{:S(2)}, u32[]{:S(2)}) collective-permute-start(bf16[64,512]{1,0:T(8,128)(2,1)S(1)} %slice.41), channel_id=1, source_target_pairs={{0,2},{1,3},{2,0},{3,1},{4,6},{5,7},{6,4},{7,5},{8,10},{9,11},{10,... | collective-permute-start | bytes 196616 | tf_op jit(solution)/shard_map/cond/branch_1_fun/ppermute | solution.py:244
  42.5 5.3 %collective-permute-start.8 = (bf16[64,512]{1,0:T(8,128)(2,1)S(1)}, bf16[64,512]{1,0:T(8,128)(2,1)S(1)}, u32[]{:S(2)}, u32[]{:S(2)}) collective-permute-start(bf16[64,512]{1,0:T(8,128)(2,1)S(1)} %slice.41), channel_id=1, source_target_pairs={{0,1},{1,0},{2,3},{3,2},{4,5},{5,4},{6,7},{7,6},{8,9},{9,8},{10,11... | collective-permute-start | bytes 196616 | tf_op jit(solution)/shard_map/cond/branch_1_fun/ppermute | solution.py:244
  51.5 16.5 %all-to-all-start.6 = ((bf16[16,16,1536]{2,1,0:T(8,128)(2,1)}), bf16[16,16,1536]{2,1,0:T(8,128)(2,1)S(1)}, u32[]{:S(2)}, u32[]{:S(2)}) async-start(bf16[16,16,1536]{2,1,0:T(8,128)(2,1)} %bitcast.12), calls=%async_computation.6 | async-start | bytes 1572864 | tf_op jit(solution)/shard_map/all_to_all | solution.py:249
  57.3 1.4 %copy-start = (bf16[1,1,192,4096]{3,2,1,0:T(8,128)(2,1)S(1)}, bf16[1,1,192,4096]{3,2,1,0:T(8,128)(2,1)}, u32[]{:S(2)}) copy-start(bf16[1,1,192,4096]{3,2,1,0:T(8,128)(2,1)} %param.35) | copy-start | bytes 4718596
  58.7 1.4 %copy-start.1 = (bf16[1,1,192,4096]{3,2,1,0:T(8,128)(2,1)S(1)}, bf16[1,1,192,4096]{3,2,1,0:T(8,128)(2,1)}, u32[]{:S(2)}) copy-start(bf16[1,1,192,4096]{3,2,1,0:T(8,128)(2,1)} %param.36) | copy-start | bytes 4718596
  62.2 0.8 copy-start.5
  68.0 1.0 copy-start.6
  70.0 0.8 copy-start.7
  70.7 29.8 %copy-start.2 = (bf16[1,1,1536,512]{3,2,1,0:T(8,128)(2,1)S(1)}, bf16[1,1,1536,512]{3,2,1,0:T(8,128)(2,1)}, u32[]{:S(2)}) copy-start(bf16[1,1,1536,512]{3,2,1,0:T(8,128)(2,1)} %param.37) | copy-start | bytes 4718596
  70.7 14.2 %all-to-all-start.7 = ((bf16[4,192,256]{2,1,0:T(8,128)(2,1)}), bf16[4,192,256]{2,1,0:T(8,128)(2,1)S(1)}, u32[]{:S(2)}, u32[]{:S(2)}) async-start(bf16[4,192,256]{2,1,0:T(8,128)(2,1)} %copy-done.7), calls=%async_computation.7 | async-start | bytes 786432 | tf_op jit(solution)/shard_map/all_to_all | solution.py:231
  75.6 9.4 %collective-permute-start.20 = (bf16[192,256]{1,0:T(8,128)(2,1)S(1)}, bf16[192,256]{1,0:T(8,128)(2,1)S(1)}, u32[]{:S(2)}, u32[]{:S(2)}) collective-permute-start(bf16[192,256]{1,0:T(8,128)(2,1)S(1)} %get-tuple-element.274), channel_id=1, source_target_pairs={{0,4},{1,5},{2,6},{3,7},{4,0},{5,1},{6,2},{7,3},{8,12},{9,13},{10,... | collective-permute-start | bytes 294920 | tf_op jit(solution)/shard_map/ppermute | solution.py:244
  100.5 15.4 %copy-start.4 = (bf16[1,128,512]{2,1,0:T(8,128)(2,1)S(1)}, bf16[1,128,512]{2,1,0:T(8,128)(2,1)}, u32[]{:S(2)}) copy-start(bf16[1,128,512]{2,1,0:T(8,128)(2,1)} %param.29) | copy-start | bytes 393220
  116.1 20.0 %collective-permute-start.21 = (bf16[128,512]{1,0:T(8,128)(2,1)S(1)}, bf16[128,512]{1,0:T(8,128)(2,1)S(1)}, u32[]{:S(2)}, u32[]{:S(2)}) collective-permute-start(bf16[128,512]{1,0:T(8,128)(2,1)S(1)} %shard_map.95), channel_id=1, source_target_pairs={{0,128},{128,256},{256,384},{384,0},{1,129},{129,257},{257,385},{3... | collective-permute-start | bytes 393224 | tf_op jit(solution)/shard_map/ppermute | solution.py:367

commit v7 on v6

--- a/solution.py
+++ b/solution.py
@@ -37,7 +37,7 @@
     return (lax.broadcasted_iota(jnp.int32, (n, n), 0) == lax.broadcasted_iota(jnp.int32, (n, n), 1)).astype(BF)
 
 
-def route_body(ids_ref, length_ref, quota_ref, tokens_ref, rows_ref, again_ref, match_ref, held_ref, chosen_ref, which_ref):
+def route_body(ids_ref, length_ref, quota_ref, compact_ref, match_ref, held_ref, chosen_ref, which_ref):
     n = ids_ref.shape[1]
     expert = lax.broadcasted_iota(jnp.int32, (EXPERTS, n), 0)
     chosen = jnp.zeros((EXPERTS, n), F32)
@@ -56,14 +56,18 @@
     used = jnp.max(kept, axis=0, keepdims=True)
     place = dot(jnp.broadcast_to(used, (8, n)).astype(BF), before, 1, 0)[0:1, :]
     compact = ((place == down.astype(F32)).astype(F32) * used).astype(BF)
-    rows = dot(compact, tokens_ref[...], 1, 0).astype(BF)
-    rows_ref[...] = rows
-    again_ref[...] = rows
+    compact_ref[...] = compact
     match_ref[...] = match
     held_ref[...] = dot(compact, match, 1, 0).astype(BF)
     chosen_ref[...] = dot(compact, chosen.astype(BF), 1, 1)
     count = jnp.sum(used).astype(jnp.int32)
     which_ref[0] = sum((count > size).astype(jnp.int32) for size in SIZES[:-1])
+
+
+def compact_body(compact_ref, tokens_ref, rows_ref, again_ref):
+    rows = dot(compact_ref[...], tokens_ref[...], 1, 0).astype(BF)
+    rows_ref[...] = rows
+    again_ref[...] = rows
 
 
 def blocks_of(rank, width):
@@ -272,21 +276,22 @@
     hid = w_gate.shape[0]
 
     table = jax.ShapeDtypeStruct((n, slots), BF)
-    rows, again, match, held, chosen, which = call(
+    compact, match, held, chosen, which = call(
         route_body,
         (
-            jax.ShapeDtypeStruct((n, width), BF),
-            jax.ShapeDtypeStruct((n, width), BF),
+            jax.ShapeDtypeStruct((n, n), BF),
             table,
             table,
             jax.ShapeDtypeStruct((n, EXPERTS), F32),
             jax.ShapeDtypeStruct((1,), jnp.int32),
         ),
-        [VM] * 4,
-        (ids, candidate_active_extent, seat_quota_per_specialist, tokens),
-        out_specs=(VM,) * 5 + (SM,),
+        [VM] * 3,
+        (ids, candidate_active_extent, seat_quota_per_specialist),
+        out_specs=(VM,) * 4 + (SM,),
         limit=16,
     )
+    packed = jax.ShapeDtypeStruct((n, width), BF)
+    rows, again = call(compact_body, (packed, packed), [VM] * 2, (compact, tokens), limit=16)
 
     def first_part(size):
         def run(which, rows, again, held, gain, router):

time: 138 us -> 135 us (0.978)
  blocking collectives: 42.1 us -> 37.9 us
  starting transfers between devices: 56.9 us -> 55.3 us
    all_to_all x1, blocking collectives: 14.6 us -> 11.4 us  [over_dp(): lax.all_to_all(rows.reshape(EXPERTS, n // EXPERTS, width), 'dp', 0, 0)]
    pallas_call x7 -> x8, Pallas kernels: 7.53 us -> 8.6 us  [call(): pl.pallas_call(body, scratch_shapes=list(scratch), out_shape=shape, in_sp...]
where the time goes in v7:
time: 135 us; the launch traced here: 133 us
  starting transfers between devices  55.3 us (41%)
  blocking collectives  37.9 us (28%)
  waiting for transfers between devices  20.9 us (15%)
  Pallas kernels  8.6 us (6%)
  local copies, waits for them, and re-layouts  8.29 us (6%)
  between operations  1.48 us (1%)
    all_to_all x2, blocking collectives, fours(): return lax.all_to_all(copies, 'tensor', 0, 0, axis_index_groups=FOURS)  26.5 us
    ppermute x5, starting transfers between devices, along(): return lax.ppermute(shard, 'tensor', [(i, i ^ by) for i in range(8)])  22.3 us
    ppermute x1, starting transfers between devices, on_device(): lax.ppermute(layer_out, 'section', [(i, (i + 1) % count) for i in range(c...  16.1 us
    all_to_all x2, starting transfers between devices, over_dp(): lax.all_to_all(rows.reshape(EXPERTS, n // EXPERTS, width), 'dp', 0, 0)  12.8 us
    all_to_all x1, blocking collectives, over_dp(): lax.all_to_all(rows.reshape(EXPERTS, n // EXPERTS, width), 'dp', 0, 0)  11.4 us
    pallas_call x8, Pallas kernels, call(): pl.pallas_call(body, scratch_shapes=list(scratch), out_shape=shape, in_sp...  8.6 us
    ppermute x5, waiting for transfers between devices, along(): return lax.ppermute(shard, 'tensor', [(i, i ^ by) for i in range(8)])  8.59 us
    all_to_all x2, waiting for transfers between devices, over_dp(): lax.all_to_all(rows.reshape(EXPERTS, n // EXPERTS, width), 'dp', 0, 0)  8.34 us
  transfers between devices with their start and end apart: 9, of which 6 were waited for; matrix products, arithmetic and copies ran while one was open for 0% of the time, Pallas kernels for 2%

profile of v7, /device:TPU:1, one launch (start us, length us, event | category | flops | bytes accessed | tf_op | source)
XLA Modules:
  0.0 133.3 jit_solution(3073551152642576706)
XLA Ops:
  2.0 0.8 shard_map.91
  2.9 0.9 copy-done.3
  4.6 23.9 %conditional.7 = ((bf16[256,2560]{1,0:T(8,128)(2,1)}, bf16[128,512]{1,0:T(8,128)(2,1)S(1)}, f32[128,128]{1,0:T(8,128)S(1)}, f32[128,16]{1,0:T(8,128)S(1)})) conditional(s32[]{:T(128)} %bitcast.7, (s32[1]{0:T(128)}, bf16[128,512]{1,0:T(8,128)(2,1)S(1)}, bf16[128,512]{1,0:T(8,128)(2,1)S(1)}, ...), branch_computations={%region_0.0_spmd, %region_3.0_spmd, %region_6.0_spmd, %region_9.0_... | conditional | flops 2 | bytes 2785406 | solution.py:331
  4.6 9.7 %collective-permute-start = (bf16[48,512]{1,0:T(8,128)(2,1)S(1)}, bf16[48,512]{1,0:T(8,128)(2,1)S(1)}, u32[]{:S(2)}, u32[]{:S(2)}) collective-permute-start(bf16[48,512]{1,0:T(8,128)(2,1)S(1)} %slice.24), channel_id=1, source_target_pairs={{0,4},{1,5},{2,6},{3,7},{4,0},{5,1},{6,2},{7,3},{8,12},{9,13},{10,... | collective-permute-start | bytes 147464 | tf_op jit(solution)/shard_map/cond/branch_0_fun/ppermute | solution.py:248
  14.9 11.2 %conditional = (bf16[4,48,512]{2,1,0:T(8,128)(2,1)S(1)}) conditional(s32[]{:T(128)} %bitcast, () %tuple.50, bf16[128,512]{1,0:T(8,128)(2,1)S(1)} %get-tuple-element.166), branch_computations={%region_1.0_spmd, %region_2.0_spmd} | conditional | bytes 737288 | solution.py:244
  15.0 11.1 %all_to_all.45 = bf16[4,48,512]{2,1,0:T(8,128)(2,1)S(1)} all-to-all(bf16[4,48,512]{2,1,0:T(8,128)(2,1)S(1)} %broadcast_in_dim.11), channel_id=1, replica_groups={{0,1,2,3},{4,5,6,7},{8,9,10,11},{12,13,14,15},{16,17,18,19},{20,21,22,2..., dimensions={0} | all-to-all | bytes 393216 | tf_op jit(solution)/shard_map/cond/branch_0_fun/cond/branch_1_fun/all_to_all | solution.py:235
  26.1 2.3 %branch_0_fun.2 = (bf16[256,2560]{1,0:T(8,128)(2,1)}, bf16[128,512]{1,0:T(8,128)(2,1)S(1)}, f32[128,128]{1,0:T(8,128)S(1)}, f32[128,16]{1,0:T(8,128)S(1)}) custom-call(bf16[4,48,512]{2,1,0:T(8,128)(2,1)S(1)} %get-tuple-element.312.own_ref, bf16[48,512]{1,0:T(8,128)(2,1)S(1)} %collective-permute-done.far_ref, ...), custom_call_target="tpu_custom_call" | custom-call | tf_op jit(solution)/shard_map/cond/branch_0_fun/pallas_call | solution.py:25
  28.5 7.0 %all-to-all-start.5 = ((bf16[16,16,2560]{2,1,0:T(8,128)(2,1)}), bf16[16,16,2560]{2,1,0:T(8,128)(2,1)S(1)}, u32[]{:S(2)}, u32[]{:S(2)}) async-start(bf16[16,16,2560]{2,1,0:T(8,128)(2,1)} %bitcast.10), calls=%async_computation.5 | async-start | bytes 2621440 | tf_op jit(solution)/shard_map/all_to_all | solution.py:253
  35.5 13.2 %conditional.8 = ((bf16[256,1536]{1,0:T(8,128)(2,1)}, bf16[128,256]{1,0:T(8,128)(2,1)S(1)}, bf16[128,256]{1,0:T(8,128)(2,1)S(1)})) conditional(s32[]{:T(128)} %bitcast.7, (bf16[128,512]{1,0:T(8,128)(2,1)S(1)}, bf16[128,256]{1,0:T(8,128)(2,1)S(1)}, bf16[1,4096]{1,0:T(2,128)(2,1)S(1)}, bf16[16,4096]{1,0:T(8,128)(2,1)S(1)}, ...), branch_computations={%region_15.0_spmd, %region_16.0_spmd, %region_17.0_spmd, %region_1... | conditional | bytes 1572992 | solution.py:335
  35.5 4.9 %collective-permute-start.7 = (bf16[48,512]{1,0:T(8,128)(2,1)S(1)}, bf16[48,512]{1,0:T(8,128)(2,1)S(1)}, u32[]{:S(2)}, u32[]{:S(2)}) collective-permute-start(bf16[48,512]{1,0:T(8,128)(2,1)S(1)} %slice.40), channel_id=1, source_target_pairs={{0,3},{1,2},{2,1},{3,0},{4,7},{5,6},{6,5},{7,4},{8,11},{9,10},{10,... | collective-permute-start | bytes 147464 | tf_op jit(solution)/shard_map/cond/branch_0_fun/ppermute | solution.py:248
  40.4 1.9 %collective-permute-start.6 = (bf16[48,512]{1,0:T(8,128)(2,1)S(1)}, bf16[48,512]{1,0:T(8,128)(2,1)S(1)}, u32[]{:S(2)}, u32[]{:S(2)}) collective-permute-start(bf16[48,512]{1,0:T(8,128)(2,1)S(1)} %slice.40), channel_id=1, source_target_pairs={{0,2},{1,3},{2,0},{3,1},{4,6},{5,7},{6,4},{7,5},{8,10},{9,11},{10,... | collective-permute-start | bytes 147464 | tf_op jit(solution)/shard_map/cond/branch_0_fun/ppermute | solution.py:248
  42.3 2.5 %collective-permute-start.5 = (bf16[48,512]{1,0:T(8,128)(2,1)S(1)}, bf16[48,512]{1,0:T(8,128)(2,1)S(1)}, u32[]{:S(2)}, u32[]{:S(2)}) collective-permute-start(bf16[48,512]{1,0:T(8,128)(2,1)S(1)} %slice.40), channel_id=1, source_target_pairs={{0,1},{1,0},{2,3},{3,2},{4,5},{5,4},{6,7},{7,6},{8,9},{9,8},{10,11... | collective-permute-start | bytes 147464 | tf_op jit(solution)/shard_map/cond/branch_0_fun/ppermute | solution.py:248
  44.8 2.1 %collective-permute-done.6.b_ref = bf16[48,512]{1,0:T(8,128)(2,1)S(1)} collective-permute-done((bf16[48,512]{1,0:T(8,128)(2,1)S(1)}, bf16[48,512]{1,0:T(8,128)(2,1)S(1)}, u32[]{:S(2)}, u32[]{:S(2)}) %collective-permute-start.6) | collective-permute-done | bytes 49184 | tf_op jit(solution)/shard_map/cond/branch_0_fun/ppermute | solution.py:248
  47.5 1.2 branch_0_fun.3
  48.7 3.3 %all-to-all-done.5 = bf16[16,16,2560]{2,1,0:T(8,128)(2,1)S(1)} async-done(((bf16[16,16,2560]{2,1,0:T(8,128)(2,1)}), bf16[16,16,2560]{2,1,0:T(8,128)(2,1)S(1)}, u32[]{:S(2)}, u32[]{:S(2)}) %all-to-all-start.5) | async-done | bytes 1310752 | tf_op jit(solution)/shard_map/all_to_all | solution.py:253
  52.0 5.8 %all-to-all-start.6 = ((bf16[16,16,1536]{2,1,0:T(8,128)(2,1)}), bf16[16,16,1536]{2,1,0:T(8,128)(2,1)S(1)}, u32[]{:S(2)}, u32[]{:S(2)}) async-start(bf16[16,16,1536]{2,1,0:T(8,128)(2,1)} %bitcast.12), calls=%async_computation.6 | async-start | bytes 1572864 | tf_op jit(solution)/shard_map/all_to_all | solution.py:253
  57.8 1.4 %copy-done = bf16[1,1,192,4096]{3,2,1,0:T(8,128)(2,1)S(1)} copy-done((bf16[1,1,192,4096]{3,2,1,0:T(8,128)(2,1)S(1)}, bf16[1,1,192,4096]{3,2,1,0:T(8,128)(2,1)}, u32[]{:S(2)}) %copy-start) | copy-done | bytes 1572888
  59.2 1.4 %copy-done.1 = bf16[1,1,192,4096]{3,2,1,0:T(8,128)(2,1)S(1)} copy-done((bf16[1,1,192,4096]{3,2,1,0:T(8,128)(2,1)S(1)}, bf16[1,1,192,4096]{3,2,1,0:T(8,128)(2,1)}, u32[]{:S(2)}) %copy-start.1) | copy-done | bytes 1572888
  60.6 2.1 %shard_map.93 = (f32[392,256]{1,0:T(8,128)S(1)}, bf16[3,192,512]{2,1,0:T(8,128)(2,1)S(1)}, bf16[3,192,512]{2,1,0:T(8,128)(2,1)S(1)}) custom-call(bf16[256,2560]{1,0:T(8,128)(2,1)S(1)} %bitcast.21, bf16[1,4096]{1,0:T(2,128)(2,1)S(1)} %copy-done.15, bf16[192,4096]{1,0:T(8,128)(2,1)S(1)} %bitcast.23, bf16[192,4096]{1,0:T(8,128)(2,1)S(1)} %bitcast.24), custom_call_target="tpu_custom_call" | custom-call | tf_op jit(solution)/shard_map/pallas_call | solution.py:25
  62.7 0.8 copy-done.5
  63.5 5.1 %all-to-all-done.6 = bf16[16,16,1536]{2,1,0:T(8,128)(2,1)S(1)} async-done(((bf16[16,16,1536]{2,1,0:T(8,128)(2,1)}), bf16[16,16,1536]{2,1,0:T(8,128)(2,1)S(1)}, u32[]{:S(2)}, u32[]{:S(2)}) %all-to-all-start.6) | async-done | bytes 786464 | tf_op jit(solution)/shard_map/all_to_all | solution.py:253
  68.6 1.0 copy-done.6
  69.6 1.0 shard_map.94
  70.6 0.8 copy-done.7
  71.3 4.0 %all-to-all-start.7 = ((bf16[4,192,256]{2,1,0:T(8,128)(2,1)}), bf16[4,192,256]{2,1,0:T(8,128)(2,1)S(1)}, u32[]{:S(2)}, u32[]{:S(2)}) async-start(bf16[4,192,256]{2,1,0:T(8,128)(2,1)} %copy-done.7), calls=%async_computation.7 | async-start | bytes 786432 | tf_op jit(solution)/shard_map/all_to_all | solution.py:235
  75.4 3.4 %collective-permute-start.20 = (bf16[192,256]{1,0:T(8,128)(2,1)S(1)}, bf16[192,256]{1,0:T(8,128)(2,1)S(1)}, u32[]{:S(2)}, u32[]{:S(2)}) collective-permute-start(bf16[192,256]{1,0:T(8,128)(2,1)S(1)} %get-tuple-element.276), channel_id=1, source_target_pairs={{0,4},{1,5},{2,6},{3,7},{4,0},{5,1},{6,2},{7,3},{8,12},{9,13},{10,... | collective-permute-start | bytes 294920 | tf_op jit(solution)/shard_map/ppermute | solution.py:248
  78.8 5.9 %collective-permute-done.20 = bf16[192,256]{1,0:T(8,128)(2,1)S(1)} collective-permute-done((bf16[192,256]{1,0:T(8,128)(2,1)S(1)}, bf16[192,256]{1,0:T(8,128)(2,1)S(1)}, u32[]{:S(2)}, u32[]{:S(2)}) %collective-permute-start.20) | collective-permute-done | bytes 98336 | tf_op jit(solution)/shard_map/ppermute | solution.py:248
  84.8 15.4 %all_to_all.50.second_ref = bf16[4,192,256]{2,1,0:T(8,128)(2,1)S(1)} all-to-all(bf16[4,192,256]{2,1,0:T(8,128)(2,1)S(1)} %broadcast_in_dim.26), channel_id=1, replica_groups={{0,1,2,3},{4,5,6,7},{8,9,10,11},{12,13,14,15},{16,17,18,19},{20,21,22,2..., dimensions={0} | all-to-all | bytes 786432 | tf_op jit(solution)/shard_map/all_to_all | solution.py:235
  100.2 0.7 shard_map.95
  100.9 11.4 %all_to_all.51 = bf16[16,16,512]{2,1,0:T(8,128)(2,1)S(1)} all-to-all(bf16[16,16,512]{2,1,0:T(8,128)(2,1)S(1)} %bitcast.26), channel_id=1, replica_groups=mesh['section'=4,'dp'=16,'tensor'=8] {'dp'}, dimensions={0} | all-to-all | bytes 524288 | tf_op jit(solution)/shard_map/all_to_all | solution.py:253
  112.5 16.1 %collective-permute-start.21 = (bf16[128,512]{1,0:T(8,128)(2,1)S(1)}, bf16[128,512]{1,0:T(8,128)(2,1)S(1)}, u32[]{:S(2)}, u32[]{:S(2)}) collective-permute-start(bf16[128,512]{1,0:T(8,128)(2,1)S(1)} %shard_map.96), channel_id=1, source_target_pairs={{0,128},{128,256},{256,384},{384,0},{1,129},{129,257},{257,385},{3... | collective-permute-start | bytes 393224 | tf_op jit(solution)/shard_map/ppermute | solution.py:372
  128.6 4.0 %collective-permute-done.21 = bf16[128,512]{1,0:T(8,128)(2,1)S(1)} collective-permute-done((bf16[128,512]{1,0:T(8,128)(2,1)S(1)}, bf16[128,512]{1,0:T(8,128)(2,1)S(1)}, u32[]{:S(2)}, u32[]{:S(2)}) %collective-permute-start.21) | collective-permute-done | bytes 131104 | tf_op jit(solution)/shard_map/ppermute | solution.py:372
  (30 shorter events, 3.0 us)
Async XLA Ops:
  0.7 0.7 copy-start.8
  1.3 0.7 copy-start.9
  2.8 0.9 copy-start.3
  4.6 21.5 %collective-permute-start = (bf16[48,512]{1,0:T(8,128)(2,1)S(1)}, bf16[48,512]{1,0:T(8,128)(2,1)S(1)}, u32[]{:S(2)}, u32[]{:S(2)}) collective-permute-start(bf16[48,512]{1,0:T(8,128)(2,1)S(1)} %slice.24), channel_id=1, source_target_pairs={{0,4},{1,5},{2,6},{3,7},{4,0},{5,1},{6,2},{7,3},{8,12},{9,13},{10,... | collective-permute-start | bytes 147464 | tf_op jit(solution)/shard_map/cond/branch_0_fun/ppermute | solution.py:248
  28.4 7.1 %copy-start.10 = (bf16[1,16,4096]{2,1,0:T(8,128)(2,1)S(1)}, bf16[1,16,4096]{2,1,0:T(8,128)(2,1)}, u32[]{:S(2)}) copy-start(bf16[1,16,4096]{2,1,0:T(8,128)(2,1)} %param.34) | copy-start | bytes 393220
  28.5 7.1 %copy-start.15 = (bf16[1,4096]{1,0:T(2,128)(2,1)S(1)}, bf16[1,4096]{1,0:T(2,128)(2,1)}, u32[]{:S(2)}) copy-start(bf16[1,4096]{1,0:T(2,128)(2,1)} %gain_ref.3) | copy-start | bytes 24580
  28.5 23.5 %all-to-all-start.5 = ((bf16[16,16,2560]{2,1,0:T(8,128)(2,1)}), bf16[16,16,2560]{2,1,0:T(8,128)(2,1)S(1)}, u32[]{:S(2)}, u32[]{:S(2)}) async-start(bf16[16,16,2560]{2,1,0:T(8,128)(2,1)} %bitcast.10), calls=%async_computation.5 | async-start | bytes 2621440 | tf_op jit(solution)/shard_map/all_to_all | solution.py:253
  35.5 9.3 %collective-permute-start.7 = (bf16[48,512]{1,0:T(8,128)(2,1)S(1)}, bf16[48,512]{1,0:T(8,128)(2,1)S(1)}, u32[]{:S(2)}, u32[]{:S(2)}) collective-permute-start(bf16[48,512]{1,0:T(8,128)(2,1)S(1)} %slice.40), channel_id=1, source_target_pairs={{0,3},{1,2},{2,1},{3,0},{4,7},{5,6},{6,5},{7,4},{8,11},{9,10},{10,... | collective-permute-start | bytes 147464 | tf_op jit(solution)/shard_map/cond/branch_0_fun/ppermute | solution.py:248
  40.4 6.6 %collective-permute-start.6 = (bf16[48,512]{1,0:T(8,128)(2,1)S(1)}, bf16[48,512]{1,0:T(8,128)(2,1)S(1)}, u32[]{:S(2)}, u32[]{:S(2)}) collective-permute-start(bf16[48,512]{1,0:T(8,128)(2,1)S(1)} %slice.40), channel_id=1, source_target_pairs={{0,2},{1,3},{2,0},{3,1},{4,6},{5,7},{6,4},{7,5},{8,10},{9,11},{10,... | collective-permute-start | bytes 147464 | tf_op jit(solution)/shard_map/cond/branch_0_fun/ppermute | solution.py:248
  42.3 5.2 %collective-permute-start.5 = (bf16[48,512]{1,0:T(8,128)(2,1)S(1)}, bf16[48,512]{1,0:T(8,128)(2,1)S(1)}, u32[]{:S(2)}, u32[]{:S(2)}) collective-permute-start(bf16[48,512]{1,0:T(8,128)(2,1)S(1)} %slice.40), channel_id=1, source_target_pairs={{0,1},{1,0},{2,3},{3,2},{4,5},{5,4},{6,7},{7,6},{8,9},{9,8},{10,11... | collective-permute-start | bytes 147464 | tf_op jit(solution)/shard_map/cond/branch_0_fun/ppermute | solution.py:248
  52.0 16.6 %all-to-all-start.6 = ((bf16[16,16,1536]{2,1,0:T(8,128)(2,1)}), bf16[16,16,1536]{2,1,0:T(8,128)(2,1)S(1)}, u32[]{:S(2)}, u32[]{:S(2)}) async-start(bf16[16,16,1536]{2,1,0:T(8,128)(2,1)} %bitcast.12), calls=%async_computation.6 | async-start | bytes 1572864 | tf_op jit(solution)/shard_map/all_to_all | solution.py:253
  57.8 1.4 %copy-start = (bf16[1,1,192,4096]{3,2,1,0:T(8,128)(2,1)S(1)}, bf16[1,1,192,4096]{3,2,1,0:T(8,128)(2,1)}, u32[]{:S(2)}) copy-start(bf16[1,1,192,4096]{3,2,1,0:T(8,128)(2,1)} %param.35) | copy-start | bytes 4718596
  59.2 1.4 %copy-start.1 = (bf16[1,1,192,4096]{3,2,1,0:T(8,128)(2,1)S(1)}, bf16[1,1,192,4096]{3,2,1,0:T(8,128)(2,1)}, u32[]{:S(2)}) copy-start(bf16[1,1,192,4096]{3,2,1,0:T(8,128)(2,1)} %param.36) | copy-start | bytes 4718596
  62.7 0.8 copy-start.5
  68.6 1.0 copy-start.6
  70.6 0.8 copy-start.7
  71.3 28.9 %copy-start.2 = (bf16[1,1,1536,512]{3,2,1,0:T(8,128)(2,1)S(1)}, bf16[1,1,1536,512]{3,2,1,0:T(8,128)(2,1)}, u32[]{:S(2)}) copy-start(bf16[1,1,1536,512]{3,2,1,0:T(8,128)(2,1)} %param.37) | copy-start | bytes 4718596
  71.3 13.4 %all-to-all-start.7 = ((bf16[4,192,256]{2,1,0:T(8,128)(2,1)}), bf16[4,192,256]{2,1,0:T(8,128)(2,1)S(1)}, u32[]{:S(2)}, u32[]{:S(2)}) async-start(bf16[4,192,256]{2,1,0:T(8,128)(2,1)} %copy-done.7), calls=%async_computation.7 | async-start | bytes 786432 | tf_op jit(solution)/shard_map/all_to_all | solution.py:235
  75.4 9.4 %collective-permute-start.20 = (bf16[192,256]{1,0:T(8,128)(2,1)S(1)}, bf16[192,256]{1,0:T(8,128)(2,1)S(1)}, u32[]{:S(2)}, u32[]{:S(2)}) collective-permute-start(bf16[192,256]{1,0:T(8,128)(2,1)S(1)} %get-tuple-element.276), channel_id=1, source_target_pairs={{0,4},{1,5},{2,6},{3,7},{4,0},{5,1},{6,2},{7,3},{8,12},{9,13},{10,... | collective-permute-start | bytes 294920 | tf_op jit(solution)/shard_map/ppermute | solution.py:248
  100.2 12.1 %copy-start.4 = (bf16[1,128,512]{2,1,0:T(8,128)(2,1)S(1)}, bf16[1,128,512]{2,1,0:T(8,128)(2,1)}, u32[]{:S(2)}) copy-start(bf16[1,128,512]{2,1,0:T(8,128)(2,1)} %param.29) | copy-start | bytes 393220
  112.5 20.1 %collective-permute-start.21 = (bf16[128,512]{1,0:T(8,128)(2,1)S(1)}, bf16[128,512]{1,0:T(8,128)(2,1)S(1)}, u32[]{:S(2)}, u32[]{:S(2)}) collective-permute-start(bf16[128,512]{1,0:T(8,128)(2,1)S(1)} %shard_map.96), channel_id=1, source_target_pairs={{0,128},{128,256},{256,384},{384,0},{1,129},{129,257},{257,385},{3... | collective-permute-start | bytes 393224 | tf_op jit(solution)/shard_map/ppermute | solution.py:372
